TPU v7x, 512 devices: a whole 4x8x8 slice. The times are simulated.
512 devices in a mesh: brow: 16 (over y, z_lo), bcol: 32 (over x, z_hi, core).
Axes of the slice: x: 4, y: 8, z: 8 (z_hi: 4, z_lo: 2; z = z_hi * 2 + z_lo), core: 2. Of those that a mesh axis runs over, the one named last changes fastest.
Arguments:
- scores: float32 [32, 1024, 128], P('bcol', 'brow'), may hold values from 0.01 to 32
- degree: int32 [32, 1024], P('bcol', 'brow'), may hold values from 50 to 200
- seed_mask: int32 [32, 1024], P('bcol', 'brow'), may hold values 0 or 1
- tiles: bfloat16 [16, 32, 64, 128, 128], P('brow', 'bcol'), may hold values from 0 to 2, as said below
- tile_list: int32 [16, 32, 2, 64], P('brow', 'bcol'), may hold values from 0 to 15, as said below
- tile_count: int32 [16, 32], P('brow', 'bcol'), may hold values from 1 to 64, as said below
Outputs:
- propagated: float32 [32, 1024, 128], P('bcol', 'brow')
Inputs may be any that keep to these rules, and one draw needn't show every extreme that they name: Slots 0 to tile_count - 1 of a device are live, the others empty; some device holds 64 live tiles. `tile_list`: entry 0 is below 16, entry 1 below 8; the live slots of a device name distinct tile blocks (a, b) with b >= a; every block (a, a) is named by a live slot. `tiles`: entries are nonnegative; a tile with a == b is symmetric and has a nonzero entry in every row; empty slots hold finite values.
All inputs are finite; a program needn't handle non-finite values. No bound on the sum of `seed_mask` on one device may be relied on, other than what follows from the above.
Results may differ from a plain program's by a relative error of at most 0.0007.
Values may be sent and summed in bfloat16 or wider, within the bound.
No kernel may reach another device: no remote copies, remote signals or barrier semaphores. Data moves between devices by JAX's collectives and lax.ppermute only.
A program may use at most 64 MiB of HBM per device.

v0:
```python
import math

import jax
import jax.numpy as jnp
from jax import lax
from jax.sharding import PartitionSpec as P

SWEEPS = 2


def spread(value, axis, source):
    kept = jnp.where(lax.axis_index(axis) == source, value, 0).astype(value.dtype)
    return lax.psum(kept, axis)


def row_weights(field):
    total = jnp.sum(field, axis=-1, keepdims=True)
    share = field / total
    entropy = -jnp.sum(share * jnp.log(share), axis=-1, keepdims=True)
    return (2.0 - entropy / math.log(field.shape[-1])) * field


def column_scatter(col_flat):
    return lax.psum_scatter(col_flat, "brow", scatter_dimension=0, tiled=True)


def on_device(scores, degree, seed_mask, tiles, tile_list, tile_count):
    n_brow = lax.axis_size("brow")
    n_bcol = lax.axis_size("bcol")
    ratio = n_bcol // n_brow
    rows_dev = scores.shape[1]
    classes = scores.shape[2]
    capacity = tiles.shape[2]
    tile_size = tiles.shape[-1]
    col_tiles = n_brow * rows_dev // tile_size
    row_tiles = ratio * col_tiles
    my_row = lax.axis_index("brow")
    my_col = lax.axis_index("bcol")
    stored = tiles[0, 0].astype(jnp.float32)
    local_row = tile_list[0, 0, 0]
    local_col = tile_list[0, 0, 1]
    live = jnp.arange(capacity, dtype=jnp.int32) < tile_count[0, 0]
    same = my_row + n_brow * local_row == my_col + n_bcol * local_col
    row_onehot = (
        (local_row[:, None] == jnp.arange(row_tiles, dtype=jnp.int32)[None, :]) & live[:, None]
    ).astype(jnp.float32)
    col_onehot = (
        (local_col[:, None] == jnp.arange(col_tiles, dtype=jnp.int32)[None, :])
        & (live & jnp.logical_not(same))[:, None]
    ).astype(jnp.float32)
    initial = scores[0]
    seeded = seed_mask[0][:, None] > 0
    scale = degree[0].astype(jnp.float32)[:, None]
    field = initial
    for sweep in range(SWEEPS):
        message = row_weights(field)
        col_range = lax.all_gather(message, "brow", axis=0, tiled=True)
        col_blocks = col_range.reshape(col_tiles, tile_size, classes)
        pieces = []
        for half in range(ratio):
            got = spread(col_range, "bcol", my_row + n_brow * half)
            pieces.append(got.reshape(col_tiles, tile_size, classes))
        row_blocks = jnp.stack(pieces, axis=1).reshape(row_tiles, tile_size, classes)
        col_pick = col_blocks[local_col]
        row_pick = row_blocks[local_row]
        forward = jnp.einsum("sij,sjk->sik", stored, col_pick, precision=lax.Precision.HIGHEST)
        mirror = jnp.einsum("sji,sjk->sik", stored, row_pick, precision=lax.Precision.HIGHEST)
        row_part = jnp.einsum("sl,sik->lik", row_onehot, forward, precision=lax.Precision.HIGHEST)
        col_part = jnp.einsum("sl,sik->lik", col_onehot, mirror, precision=lax.Precision.HIGHEST)
        row_part = (
            row_part.reshape(col_tiles, ratio, tile_size, classes)
            .transpose(1, 0, 2, 3)
            .reshape(ratio, n_brow * rows_dev, classes)
        )
        col_flat = col_part.reshape(n_brow * rows_dev, classes)
        moved = lax.all_to_all(row_part, "brow", split_axis=1, concat_axis=1, tiled=True)
        col_total = column_scatter(col_flat)
        arranged = moved.reshape(ratio * n_brow, rows_dev, classes)
        row_total = lax.psum_scatter(arranged, "bcol", scatter_dimension=0, tiled=True)[0]
        total = row_total + col_total
        field = jnp.where(seeded, initial, total / scale)
    return field[None]


def solution(mesh):
    placed = (
        P("bcol", "brow", None),
        P("bcol", "brow"),
        P("bcol", "brow"),
        P("brow", "bcol", None, None, None),
        P("brow", "bcol", None, None),
        P("brow", "bcol"),
    )
    return jax.shard_map(
        on_device, mesh=mesh, in_specs=placed, out_specs=P("bcol", "brow", None), check_vma=False
    )
```

profile of v0, /device:TPU:56, one launch (start us, length us, event | category | flops | bytes accessed | tf_op | source)
XLA Modules:
  0.0 1068.4 jit_solution(9725051248601173599)
XLA Ops:
  9.4 35.0 %all_gather.6 = f32[1024,128]{1,0:T(8,128)S(1)} all-gather(f32[64,128]{1,0:T(8,128)S(1)} %bitcast_multiply_fusion), channel_id=1, replica_groups=mesh['brow'=16,'bcol'=32] {'brow'}, dimensions={0}, use_global_device_ids=true | all-gather | bytes 557056 | tf_op jit(solution)/shard_map/all_gather | solution.py:57
  46.2 2.8 gather_fusion
  49.0 7.6 convolution_bitcast_fusion.3
  57.3 5.4 copy.30
  62.7 3.7 fusion.15
  66.7 1.8 copy.32
  68.5 7.0 all-to-all-start
  75.8 268.1 %all-reduce.7.cloned.1.call-done = (f32[8,1,128,128]{3,2,1,0:T(8,128)}, f32[8,1,128,128]{3,2,1,0:T(8,128)}) async-done(((f32[8,1,128,128]{3,2,1,0:T(8,128)}, f32[8,1,128,128]{3,2,1,0:T(8,128)}), (f32[8,1,128,128]{3,2,1,0:T(8,128)}, f32[8,1,128,128]{3,2,1,0:T(8,128)})) %all-reduce.7.cloned.1.call-update) | async-done | bytes 1048592 | tf_op jit(solution)/shard_map/psum | solution.py:13
  343.9 1.3 pad_maximum_fusion
  345.2 2.8 gather_fusion.1
  348.0 7.6 convolution_bitcast_fusion.2
  355.5 5.4 copy.35
  360.9 3.7 fusion.25
  365.6 2.3 copy.33
  368.0 67.3 %reduce-scatter.7.cloned.1.call-done = f32[64,128]{1,0:T(8,128)} async-done(((f32[1024,128]{1,0:T(8,128)}), f32[64,128]{1,0:T(8,128)}) %reduce-scatter.7.cloned.1.call-update) | async-done | bytes 32784 | tf_op jit(solution)/shard_map/reduce_scatter | solution.py:24
  435.3 102.9 %reduce-scatter.5.cloned.1.call-done = f32[1,64,128]{2,1,0:T(8,128)} async-done(((f32[32,64,128]{2,1,0:T(8,128)}), f32[1,64,128]{2,1,0:T(8,128)}) %reduce-scatter.5.cloned.1.call-update) | async-done | bytes 32784 | tf_op jit(solution)/shard_map/reduce_scatter | solution.py:79
  539.4 32.2 %all_gather.7 = f32[1024,128]{1,0:T(8,128)S(1)} all-gather(f32[64,128]{1,0:T(8,128)S(1)} %broadcast_multiply_fusion), channel_id=1, replica_groups=mesh['brow'=16,'bcol'=32] {'brow'}, dimensions={0}, use_global_device_ids=true | all-gather | bytes 557056 | tf_op jit(solution)/shard_map/all_gather | solution.py:57
  572.8 2.8 gather_fusion.2
  575.6 7.6 convolution_bitcast_fusion.1
  583.2 5.4 copy.38
  588.6 3.7 fusion.13
  592.6 1.8 copy.40
  594.4 9.1 all-to-all-start.1
  603.8 261.6 %all-reduce.5.cloned.1.call-done = (f32[8,1,128,128]{3,2,1,0:T(8,128)}, f32[8,1,128,128]{3,2,1,0:T(8,128)}) async-done(((f32[8,1,128,128]{3,2,1,0:T(8,128)}, f32[8,1,128,128]{3,2,1,0:T(8,128)}), (f32[8,1,128,128]{3,2,1,0:T(8,128)}, f32[8,1,128,128]{3,2,1,0:T(8,128)})) %all-reduce.5.cloned.1.call-update) | async-done | bytes 1048592 | tf_op jit(solution)/shard_map/psum | solution.py:13
  866.7 2.8 gather_fusion.3
  869.5 7.6 convolution_bitcast_fusion
  877.0 5.4 copy.45
  882.4 3.7 fusion.23
  887.1 2.3 copy.41
  889.4 67.5 %reduce-scatter.11.cloned.1.call-done = f32[64,128]{1,0:T(8,128)} async-done(((f32[1024,128]{1,0:T(8,128)}), f32[64,128]{1,0:T(8,128)}) %reduce-scatter.11.cloned.1.call-update) | async-done | bytes 32784 | tf_op jit(solution)/shard_map/reduce_scatter | solution.py:24
  956.8 103.2 %reduce-scatter.9.cloned.1.call-done = f32[1,64,128]{2,1,0:T(8,128)} async-done(((f32[32,64,128]{2,1,0:T(8,128)}), f32[1,64,128]{2,1,0:T(8,128)}) %reduce-scatter.9.cloned.1.call-update) | async-done | bytes 32784 | tf_op jit(solution)/shard_map/reduce_scatter | solution.py:79
  1060.1 1.5 fusion.8
  (46 shorter events, 11.5 us)
Async XLA Ops:
  6.5 42.5 %copy-start = (bf16[1,1,64,128,128]{4,3,2,1,0:T(8,128)(2,1)S(1)}, bf16[1,1,64,128,128]{4,3,2,1,0:T(8,128)(2,1)}, u32[]{:S(2)}) copy-start(bf16[1,1,64,128,128]{4,3,2,1,0:T(8,128)(2,1)} %param.9) | copy-start | bytes 6291460
  6.5 337.4 %all-reduce.7.cloned.1.call-start = ((), (), s32[]{:S(2)}) async-start(), calls=%async_computation.11 | async-start | bytes 2097152 | tf_op jit(solution)/shard_map/psum | solution.py:13
  57.3 5.4 copy-start.2
  68.5 297.1 %all-to-all-start = ((f32[2,1024,128]{2,0,1:T(2,128)}), f32[2,1024,128]{2,0,1:T(2,128)}, u32[]{:S(2)}, u32[]{:S(2)}) async-start(f32[2,1024,128]{2,0,1:T(2,128)} %copy.32), calls=%async_computation | async-start | bytes 2097152 | tf_op jit(solution)/shard_map/all_to_all | solution.py:76
  75.6 359.7 %reduce-scatter.7.cloned.1.call-start = ((), (), s32[]{:S(2)}) async-start(), calls=%async_computation.7 | async-start | bytes 557056 | tf_op jit(solution)/shard_map/reduce_scatter | solution.py:24
  360.9 7.0 copy-start.3
  360.9 7.0 copy-start.4
  360.9 177.2 %copy-start.1 = (f32[1,64,128]{2,1,0:T(8,128)S(1)}, f32[1,64,128]{2,1,0:T(8,128)}, u32[]{:S(2)}) copy-start(f32[1,64,128]{2,1,0:T(8,128)} %param.6) | copy-start | bytes 98308
  365.6 172.6 %reduce-scatter.5.cloned.1.call-start = ((), (), s32[]{:S(2)}) async-start(), calls=%async_computation.6 | async-start | bytes 1081344 | tf_op jit(solution)/shard_map/reduce_scatter | solution.py:79
  367.9 497.5 %all-reduce.5.cloned.1.call-start = ((), (), s32[]{:S(2)}) async-start(), calls=%async_computation.10 | async-start | bytes 2097152 | tf_op jit(solution)/shard_map/psum | solution.py:13
  594.4 292.7 %all-to-all-start.1 = ((f32[2,1024,128]{2,0,1:T(2,128)}), f32[2,1024,128]{2,0,1:T(2,128)}, u32[]{:S(2)}, u32[]{:S(2)}) async-start(f32[2,1024,128]{2,0,1:T(2,128)} %copy.40), calls=%async_computation.3 | async-start | bytes 2097152 | tf_op jit(solution)/shard_map/all_to_all | solution.py:76
  603.5 353.3 %reduce-scatter.11.cloned.1.call-start = ((), (), s32[]{:S(2)}) async-start(), calls=%async_computation.9 | async-start | bytes 557056 | tf_op jit(solution)/shard_map/reduce_scatter | solution.py:24
  887.0 173.1 %reduce-scatter.9.cloned.1.call-start = ((), (), s32[]{:S(2)}) async-start(), calls=%async_computation.8 | async-start | bytes 1081344 | tf_op jit(solution)/shard_map/reduce_scatter | solution.py:79
Sparse Core Ops, SparseCore 0:
  45.6 298.2 all-reduce.6
  365.7 69.5 reduce-scatter.6
  439.7 98.4 reduce-scatter.4
  572.9 292.4 all-reduce.4
  887.1 69.6 reduce-scatter.10
  961.7 98.3 reduce-scatter.8
where the time goes:
time: 1070 us
  waiting for transfers between devices  871 us (81%)
  blocking collectives  67.2 us (6%)
  matrix products  45 us (4%)
  local copies, waits for them, and re-layouts  43.4 us (4%)
  starting transfers between devices  16.8 us (2%)
  between operations  14.3 us (1%)
  other arithmetic  11 us (1%)
    psum x2, waiting for transfers between devices, spread(): return lax.psum(kept, axis)  530 us
    reduce_scatter x2, waiting for transfers between devices, on_device(): lax.psum_scatter(arranged, 'bcol', scatter_dimension=0, tiled=True)[0]  206 us
    reduce_scatter x2, waiting for transfers between devices, column_scatter(): return lax.psum_scatter(col_flat, 'brow', scatter_dimension=0, tiled=True)  135 us
    all_gather x2, blocking collectives, on_device(): col_range = lax.all_gather(message, 'brow', axis=0, tiled=True)  67.2 us
  transfers between devices with their start and end apart: 8, of which 6 were waited for; matrix products, arithmetic and copies ran while one was open for 9% of the time, Pallas kernels for 0%

commit v1 on v0

v1 whole, which is shorter than its diff:
```python
import math

import jax
import jax.numpy as jnp
from jax import lax
from jax.experimental import pallas as pl
from jax.experimental.pallas import tpu as pltpu
from jax.sharding import PartitionSpec as P

SWEEPS = 2
HEAD = 16
STEPS = 3840.0
SCALE_STEPS = 64.0
TINY = 1e-37
VMEM = 48 * 1024 * 1024


def encode(x):
    biggest = jnp.max(jnp.max(x, axis=0, keepdims=True), axis=1, keepdims=True)
    scale = jnp.floor(jnp.log(jnp.maximum(biggest, TINY)) * SCALE_STEPS) + 2.0
    below = jnp.log(jnp.maximum(x, TINY)) - scale * (1.0 / SCALE_STEPS)
    code = jnp.clip(below * STEPS + 65535.5, 0.0, 65535.0)
    code = jnp.where(x > 0.0, code, 0.0).astype(jnp.int32) - 32768
    head = jnp.broadcast_to(scale, (HEAD, x.shape[1])).astype(jnp.int32)
    return code.astype(jnp.int16), head.astype(jnp.int16)


def decode(piece):
    rows = piece.shape[0] - HEAD
    code = piece[:rows].astype(jnp.int32).astype(jnp.float32)
    head = piece[rows:].astype(jnp.int32).astype(jnp.float32)[:1]
    base = head * (1.0 / SCALE_STEPS) - 32767.0 / STEPS
    return jnp.where(code > -32768.0, jnp.exp(code * (1.0 / STEPS) + base), 0.0)


def weighted(field):
    total = jnp.maximum(jnp.sum(field, axis=-1, keepdims=True), TINY)
    share = field / total
    entropy = -jnp.sum(share * jnp.log(jnp.maximum(share, TINY)), axis=-1, keepdims=True)
    return (2.0 - entropy / math.log(field.shape[-1])) * field


def put_message(field, copies_ref, one_ref):
    rows = field.shape[0]
    code, head = encode(weighted(field))
    one_ref[:rows] = code
    one_ref[rows:] = head
    for i in range(copies_ref.shape[0]):
        copies_ref[i, :rows] = code
        copies_ref[i, rows:] = head


def split(value):
    high = value.astype(jnp.bfloat16)
    return high, (value - high.astype(jnp.float32)).astype(jnp.bfloat16)


def first_kernel(scores_ref, copies_ref, one_ref):
    put_message(scores_ref[...], copies_ref, one_ref)


def copies_kernel(after_ref, one_ref, copies_ref):
    for i in range(copies_ref.shape[0]):
        copies_ref[i] = one_ref[...]


def forward_kernel(meta_ref, got_ref, tiles_ref, keep_ref, send_ref, msg, acc):
    pieces = got_ref.shape[0]
    rows = got_ref.shape[1] - HEAD
    size = tiles_ref.shape[-1]
    classes = got_ref.shape[2]
    for i in range(pieces):
        high, low = split(decode(got_ref[i]))
        msg[i * rows : (i + 1) * rows, :classes] = high
        msg[i * rows : (i + 1) * rows, classes:] = low
    acc[...] = jnp.zeros_like(acc)

    def body(s, carry):
        col = meta_ref[0, s]
        row = meta_ref[1, s]
        part = jnp.dot(
            tiles_ref[s], msg[pl.ds(pl.multiple_of(col * size, size), size), :],
            preferred_element_type=jnp.float32,
        )
        where = pl.ds(pl.multiple_of(row * size, size), size)
        acc[where, :] += part[:, :classes] + part[:, classes:]
        return carry

    lax.fori_loop(0, tiles_ref.shape[0], body, 0, unroll=8)
    core = meta_ref[4, 0]
    kept = keep_ref.shape[0]
    for j in range(kept):
        p = 2 * (j % (kept // 2)) + j // (kept // 2)
        keep_ref[j] = acc[pl.ds(pl.multiple_of(p * size + core * rows, rows), rows), :]
        send_ref[j] = acc[pl.ds(pl.multiple_of(p * size + (1 - core) * rows, rows), rows), :]


def join_kernel(after_ref, keep_ref, got_ref, out_ref):
    rows = keep_ref.shape[1]
    for j in range(keep_ref.shape[0]):
        code, head = encode(keep_ref[j] + got_ref[j])
        out_ref[j, :rows] = code
        out_ref[j, rows:] = head


def mirror_kernel(meta_ref, own_ref, other_ref, tiles_ref, out_ref, msg, acc):
    pieces = own_ref.shape[0]
    rows = own_ref.shape[1] - HEAD
    size = tiles_ref.shape[-1]
    classes = own_ref.shape[2]
    core = meta_ref[4, 0]
    for j in range(pieces):
        p = 2 * (j % (pieces // 2)) + j // (pieces // 2)
        for ref, half in ((own_ref, core), (other_ref, 1 - core)):
            high, low = split(decode(ref[j]))
            where = pl.ds(pl.multiple_of(p * size + half * rows, rows), rows)
            msg[where, :classes] = high
            msg[where, classes:] = low
    acc[...] = jnp.zeros_like(acc)

    def body(s, carry):
        row = meta_ref[2, s]
        col = meta_ref[3, s]
        part = lax.dot_general(
            tiles_ref[s], msg[pl.ds(pl.multiple_of(row * size, size), size), :],
            (((0,), (0,)), ((), ())), preferred_element_type=jnp.float32,
        )
        where = pl.ds(pl.multiple_of(col * size, size), size)
        acc[where, :] += part[:, :classes] + part[:, classes:]
        return carry

    lax.fori_loop(0, tiles_ref.shape[0], body, 0, unroll=8)
    for i in range(out_ref.shape[0]):
        code, head = encode(acc[i * rows : (i + 1) * rows, :])
        out_ref[i, :rows] = code
        out_ref[i, rows:] = head


def total_of(ref):
    total = decode(ref[0])
    for i in range(1, ref.shape[0]):
        total = total + decode(ref[i])
    return total


def sum_kernel(got_ref, out_ref):
    out_ref[...] = total_of(got_ref)


def next_field(got_ref, row_ref, scores_ref, scale_ref, seed_ref):
    total = total_of(got_ref) + row_ref[...]
    return jnp.where(seed_ref[...] > 0.0, scores_ref[...], total / scale_ref[...])


def middle_kernel(got_ref, row_ref, scores_ref, scale_ref, seed_ref, copies_ref, one_ref):
    field = next_field(got_ref, row_ref, scores_ref, scale_ref, seed_ref)
    put_message(field, copies_ref, one_ref)


def last_kernel(got_ref, row_ref, scores_ref, scale_ref, seed_ref, out_ref):
    out_ref[...] = next_field(got_ref, row_ref, scores_ref, scale_ref, seed_ref)


WHOLE = pl.BlockSpec(memory_space=pltpu.VMEM)
SCALARS = pl.BlockSpec(memory_space=pltpu.SMEM)
ANYWHERE = pl.BlockSpec(memory_space=pl.ANY)


def call(kernel, name, outs, args, specs=None, scratch=()):
    single = not isinstance(outs, (tuple, list))
    return pl.pallas_call(
        kernel,
        out_shape=outs,
        in_specs=specs or [WHOLE] * len(args),
        out_specs=WHOLE if single else tuple(WHOLE for _ in outs),
        scratch_shapes=list(scratch),
        compiler_params=pltpu.CompilerParams(vmem_limit_bytes=VMEM),
        name=name,
    )(*args)


def on_device(scores, degree, seed_mask, tiles, tile_list, tile_count):
    n_brow = lax.axis_size("brow")
    n_bcol = lax.axis_size("bcol")
    ratio = n_bcol // n_brow
    rows = scores.shape[1]
    classes = scores.shape[2]
    capacity = tiles.shape[2]
    size = tiles.shape[-1]
    col_tiles = n_brow * rows // size
    row_tiles = ratio * col_tiles
    my_row = lax.axis_index("brow")
    my_col = lax.axis_index("bcol")
    stored = tiles[0, 0]
    local_row = jnp.clip(tile_list[0, 0, 0], 0, row_tiles - 1)
    local_col = jnp.clip(tile_list[0, 0, 1], 0, col_tiles - 1)
    live = jnp.arange(capacity, dtype=jnp.int32) < tile_count[0, 0]
    same = my_row + n_brow * local_row == my_col + n_bcol * local_col
    meta = jnp.stack([
        local_col,
        jnp.where(live, local_row, row_tiles),
        local_row,
        jnp.where(live & jnp.logical_not(same), local_col, col_tiles),
        jnp.full((capacity,), my_col % 2, jnp.int32),
    ])
    initial = scores[0]
    seeds = jnp.broadcast_to(seed_mask[0].astype(jnp.float32)[:, None], (rows, classes))
    scale = jnp.broadcast_to(degree[0].astype(jnp.float32)[:, None], (rows, classes))

    half = n_bcol // 2
    groups = [[2 * j + k for j in range(half)] for k in range(2)]
    exchange = [(i, i ^ 1) for i in range(n_bcol)]
    transpose = [
        (a * n_bcol + n_brow * h + b, b * n_bcol + n_brow * h + a)
        for a in range(n_brow) for h in range(ratio) for b in range(n_brow)
    ]

    def swap(value):
        return lax.ppermute(value, ("brow", "bcol"), transpose)

    def over_brow(value):
        return lax.all_to_all(value, "brow", split_axis=0, concat_axis=0, tiled=True)

    def over_bcol(value):
        return lax.all_to_all(
            value, "bcol", split_axis=0, concat_axis=0, tiled=True, axis_index_groups=groups
        )

    piece = jax.ShapeDtypeStruct((rows + HEAD, classes), jnp.int16)
    brow_pieces = jax.ShapeDtypeStruct((n_brow,) + piece.shape, jnp.int16)
    bcol_pieces = jax.ShapeDtypeStruct((half,) + piece.shape, jnp.int16)
    sums = jax.ShapeDtypeStruct((half, rows, classes), jnp.float32)
    share = jax.ShapeDtypeStruct((rows, classes), jnp.float32)

    copies, one = call(first_kernel, "first", (brow_pieces, piece), (initial,))
    for sweep in range(SWEEPS):
        col_got = over_brow(copies)
        copies = call(
            copies_kernel, "copies", bcol_pieces, (col_got, swap(one)), [ANYWHERE, WHOLE]
        )
        row_own = over_bcol(copies)
        keep, send = call(
            forward_kernel, "forward", (sums, sums), (meta, col_got, stored),
            [SCALARS, WHOLE, WHOLE],
            [pltpu.VMEM((col_tiles * size, 2 * classes), jnp.bfloat16),
             pltpu.VMEM(((row_tiles + 1) * size, classes), jnp.float32)],
        )
        got = lax.ppermute(send, "bcol", exchange)
        joined = call(
            join_kernel, "join", bcol_pieces, (row_own, keep, got), [ANYWHERE, WHOLE, WHOLE]
        )
        row_got = over_bcol(joined)
        row_other = lax.ppermute(row_own, "bcol", exchange)
        col_parts = call(
            mirror_kernel, "mirror", brow_pieces, (meta, row_own, row_other, stored),
            [SCALARS, WHOLE, WHOLE, WHOLE],
            [pltpu.VMEM((row_tiles * size, 2 * classes), jnp.bfloat16),
             pltpu.VMEM(((col_tiles + 1) * size, classes), jnp.float32)],
        )
        col_sums = over_brow(col_parts)
        row_sum = swap(call(sum_kernel, "sum", share, (row_got,)))
        args = (col_sums, row_sum, initial, scale, seeds)
        if sweep < SWEEPS - 1:
            copies, one = call(middle_kernel, "middle", (brow_pieces, piece), args)
        else:
            field = call(last_kernel, "last", share, args)
    return field[None]


def solution(mesh):
    placed = (
        P("bcol", "brow", None),
        P("bcol", "brow"),
        P("bcol", "brow"),
        P("brow", "bcol", None, None, None),
        P("brow", "bcol", None, None),
        P("brow", "bcol"),
    )
    return jax.shard_map(
        on_device, mesh=mesh, in_specs=placed, out_specs=P("bcol", "brow", None), check_vma=False
    )
```

time: 1070 us -> 181 us (0.17)
  the two profiles are of different devices: /device:TPU:56 before, /device:TPU:11 now
where the time goes in v1:
time: 181 us; the launch traced here: 180 us
  starting transfers between devices  118 us (65%)
  waiting for transfers between devices  29.6 us (16%)
  Pallas kernels  23.6 us (13%)
  local copies, waits for them, and re-layouts  6.19 us (3%)
    ppermute x4, starting transfers between devices, swap(): return lax.ppermute(value, ('brow', 'bcol'), transpose)  48 us
    all_to_all x4, starting transfers between devices, over_bcol(): lax.all_to_all(value, 'bcol', split_axis=0, concat_axis=0, tiled=True, ax...  28.1 us
    all_to_all x4, starting transfers between devices, over_brow(): lax.all_to_all(value, 'brow', split_axis=0, concat_axis=0, tiled=True)  27.2 us
    pallas_call x13, Pallas kernels, call(): pl.pallas_call(kernel, out_shape=outs, in_specs=specs or [WHOLE] * len(ar...  23.6 us
    ppermute x4, waiting for transfers between devices, swap(): return lax.ppermute(value, ('brow', 'bcol'), transpose)  19.1 us
    ppermute x2, starting transfers between devices, on_device(): got = lax.ppermute(send, 'bcol', exchange)  9.26 us
    unnamed x20, local copies, waits for them, and re-layouts  6.02 us
    ppermute x2, starting transfers between devices, on_device(): row_other = lax.ppermute(row_own, 'bcol', exchange)  5.67 us
  transfers between devices with their start and end apart: 16, of which 10 were waited for; matrix products, arithmetic and copies ran while one was open for 1% of the time, Pallas kernels for 9%

profile of v1, /device:TPU:11, one launch (start us, length us, event | category | flops | bytes accessed | tf_op | source)
XLA Modules:
  0.0 180.1 jit_solution(2667512343381211941)
XLA Ops:
  1.8 8.8 %all-to-all-start = ((s16[16,80,128]{2,1,0:T(8,128)(2,1)}), s16[16,80,128]{2,1,0:T(8,128)(2,1)S(1)}, u32[]{:S(2)}, u32[]{:S(2)}) async-start(s16[16,80,128]{2,1,0:T(8,128)(2,1)} %get-tuple-element.13), calls=%async_computation | async-start | bytes 655360 | tf_op jit(solution)/shard_map/all_to_all | solution.py:222
  10.6 11.7 %collective-permute-start = (s16[80,128]{1,0:T(8,128)(2,1)S(1)}, s16[80,128]{1,0:T(8,128)(2,1)S(1)}, u32[]{:S(2)}, u32[]{:S(2)}) collective-permute-start(s16[80,128]{1,0:T(8,128)(2,1)S(1)} %get-tuple-element.14), channel_id=1, source_target_pairs={{0,0},{1,32},{2,64},{3,96},{4,128},{5,160},{6,192},{7,224},{8,256}... | collective-permute-start | bytes 61448 | tf_op jit(solution)/shard_map/ppermute | solution.py:219
  23.7 4.8 %collective-permute-done.one_ref = s16[80,128]{1,0:T(8,128)(2,1)S(1)} collective-permute-done((s16[80,128]{1,0:T(8,128)(2,1)S(1)}, s16[80,128]{1,0:T(8,128)(2,1)S(1)}, u32[]{:S(2)}, u32[]{:S(2)}) %collective-permute-start) | collective-permute-done | bytes 20512 | tf_op jit(solution)/shard_map/ppermute | solution.py:219
  29.3 5.7 %all-to-all-start.1 = ((s16[16,80,128]{2,1,0:T(8,128)(2,1)}), s16[16,80,128]{2,1,0:T(8,128)(2,1)S(1)}, u32[]{:S(2)}, u32[]{:S(2)}) async-start(s16[16,80,128]{2,1,0:T(8,128)(2,1)} %copies.2), calls=%async_computation.1 | async-start | bytes 655360 | tf_op jit(solution)/shard_map/all_to_all | solution.py:225
  35.8 1.6 copy-done
  37.4 3.4 %forward.2 = (f32[16,64,128]{2,1,0:T(8,128)S(1)}, f32[16,64,128]{2,1,0:T(8,128)S(1)}) custom-call(s32[5,64]{1,0:T(8,128)S(1)} %stack.2.meta_ref, s16[16,80,128]{2,1,0:T(8,128)(2,1)S(1)} %all-to-all-done.after_ref.got_ref, bf16[64,128,128]{2,1,0:T(8,128)(2,1)S(1)} %bitcast.19), custom_call_target="tpu_custom_call" | custom-call | tf_op jit(solution)/shard_map/forward/pallas_call | solution.py:171
  40.8 5.2 %collective-permute-start.2 = (f32[16,64,128]{2,1,0:T(8,128)S(1)}, f32[16,64,128]{2,1,0:T(8,128)S(1)}, u32[]{:S(2)}, u32[]{:S(2)}) collective-permute-start(f32[16,64,128]{2,1,0:T(8,128)S(1)} %get-tuple-element.16), channel_id=1, source_target_pairs={{0,1},{1,0},{2,3},{3,2},{4,5},{5,4},{6,7},{7,6},{8,9},{9,8},{10,11... | collective-permute-start | bytes 1572872 | tf_op jit(solution)/shard_map/ppermute | solution.py:248
  46.0 1.5 collective-permute-done.2.got_ref
  50.4 9.2 %all-to-all-start.3 = ((s16[16,80,128]{2,1,0:T(8,128)(2,1)}), s16[16,80,128]{2,1,0:T(8,128)(2,1)S(1)}, u32[]{:S(2)}, u32[]{:S(2)}) async-start(s16[16,80,128]{2,1,0:T(8,128)(2,1)} %join.2), calls=%async_computation.3 | async-start | bytes 655360 | tf_op jit(solution)/shard_map/all_to_all | solution.py:225
  59.6 2.8 %collective-permute-start.1 = (s16[16,80,128]{2,1,0:T(8,128)(2,1)S(1)}, s16[16,80,128]{2,1,0:T(8,128)(2,1)S(1)}, u32[]{:S(2)}, u32[]{:S(2)}) collective-permute-start(s16[16,80,128]{2,1,0:T(8,128)(2,1)S(1)} %all-to-all-done.1.own_ref.after_ref), channel_id=1, source_target_pairs={{0,1},{1,0},{2,3},{3,2},{4,5},{5,4},{6,7},{7,6},{8,9},{9,8},{10,11... | collective-permute-start | bytes 983048 | tf_op jit(solution)/shard_map/ppermute | solution.py:253
  62.5 1.2 collective-permute-done.1.other_ref
  63.7 4.8 %mirror.2 = s16[16,80,128]{2,1,0:T(8,128)(2,1)} custom-call(s32[5,64]{1,0:T(8,128)S(1)} %stack.2.meta_ref, s16[16,80,128]{2,1,0:T(8,128)(2,1)S(1)} %all-to-all-done.1.own_ref.after_ref, s16[16,80,128]{2,1,0:T(8,128)(2,1)S(1)} %collective-permute-done.1.other_ref, bf16[64,128,128]{2,1,0:T(8,128)(2,1)S(1)} %bitcast.20), custom_call_target="tpu_custom_call" | custom-call | tf_op jit(solution)/shard_map/mirror/pallas_call | solution.py:171
  68.6 2.6 %all-to-all-done.3.got_ref = s16[16,80,128]{2,1,0:T(8,128)(2,1)S(1)} async-done(((s16[16,80,128]{2,1,0:T(8,128)(2,1)}), s16[16,80,128]{2,1,0:T(8,128)(2,1)S(1)}, u32[]{:S(2)}, u32[]{:S(2)}) %all-to-all-start.3) | async-done | bytes 327712 | tf_op jit(solution)/shard_map/all_to_all | solution.py:225
  71.1 6.8 %all-to-all-start.2 = ((s16[16,80,128]{2,1,0:T(8,128)(2,1)}), s16[16,80,128]{2,1,0:T(8,128)(2,1)S(1)}, u32[]{:S(2)}, u32[]{:S(2)}) async-start(s16[16,80,128]{2,1,0:T(8,128)(2,1)} %mirror.2), calls=%async_computation.2 | async-start | bytes 655360 | tf_op jit(solution)/shard_map/all_to_all | solution.py:222
  78.2 12.1 %collective-permute-start.3 = (f32[64,128]{1,0:T(8,128)S(1)}, f32[64,128]{1,0:T(8,128)S(1)}, u32[]{:S(2)}, u32[]{:S(2)}) collective-permute-start(f32[64,128]{1,0:T(8,128)S(1)} %sum.2), channel_id=1, source_target_pairs={{0,0},{1,32},{2,64},{3,96},{4,128},{5,160},{6,192},{7,224},{8,256}... | collective-permute-start | bytes 98312 | tf_op jit(solution)/shard_map/ppermute | solution.py:219
  90.3 5.0 %collective-permute-done.3.row_ref = f32[64,128]{1,0:T(8,128)S(1)} collective-permute-done((f32[64,128]{1,0:T(8,128)S(1)}, f32[64,128]{1,0:T(8,128)S(1)}, u32[]{:S(2)}, u32[]{:S(2)}) %collective-permute-start.3) | collective-permute-done | bytes 32800 | tf_op jit(solution)/shard_map/ppermute | solution.py:219
  95.4 1.2 middle.1
  96.7 3.4 %all-to-all-start.4 = ((s16[16,80,128]{2,1,0:T(8,128)(2,1)}), s16[16,80,128]{2,1,0:T(8,128)(2,1)S(1)}, u32[]{:S(2)}, u32[]{:S(2)}) async-start(s16[16,80,128]{2,1,0:T(8,128)(2,1)} %get-tuple-element.17), calls=%async_computation.4 | async-start | bytes 655360 | tf_op jit(solution)/shard_map/all_to_all | solution.py:222
  100.1 12.2 %collective-permute-start.4 = (s16[80,128]{1,0:T(8,128)(2,1)S(1)}, s16[80,128]{1,0:T(8,128)(2,1)S(1)}, u32[]{:S(2)}, u32[]{:S(2)}) collective-permute-start(s16[80,128]{1,0:T(8,128)(2,1)S(1)} %get-tuple-element.18), channel_id=1, source_target_pairs={{0,0},{1,32},{2,64},{3,96},{4,128},{5,160},{6,192},{7,224},{8,256}... | collective-permute-start | bytes 61448 | tf_op jit(solution)/shard_map/ppermute | solution.py:219
  112.3 3.5 %collective-permute-done.4.one_ref = s16[80,128]{1,0:T(8,128)(2,1)S(1)} collective-permute-done((s16[80,128]{1,0:T(8,128)(2,1)S(1)}, s16[80,128]{1,0:T(8,128)(2,1)S(1)}, u32[]{:S(2)}, u32[]{:S(2)}) %collective-permute-start.4) | collective-permute-done | bytes 20512 | tf_op jit(solution)/shard_map/ppermute | solution.py:219
  116.6 4.2 %all-to-all-start.5 = ((s16[16,80,128]{2,1,0:T(8,128)(2,1)}), s16[16,80,128]{2,1,0:T(8,128)(2,1)S(1)}, u32[]{:S(2)}, u32[]{:S(2)}) async-start(s16[16,80,128]{2,1,0:T(8,128)(2,1)} %copies.3), calls=%async_computation.5 | async-start | bytes 655360 | tf_op jit(solution)/shard_map/all_to_all | solution.py:225
  120.8 3.3 %forward.3 = (f32[16,64,128]{2,1,0:T(8,128)S(1)}, f32[16,64,128]{2,1,0:T(8,128)S(1)}) custom-call(s32[5,64]{1,0:T(8,128)S(1)} %stack.2.meta_ref, s16[16,80,128]{2,1,0:T(8,128)(2,1)S(1)} %all-to-all-done.4.after_ref.got_ref, bf16[64,128,128]{2,1,0:T(8,128)(2,1)S(1)} %bitcast.21), custom_call_target="tpu_custom_call" | custom-call | tf_op jit(solution)/shard_map/forward/pallas_call | solution.py:171
  124.1 4.1 %collective-permute-start.6 = (f32[16,64,128]{2,1,0:T(8,128)S(1)}, f32[16,64,128]{2,1,0:T(8,128)S(1)}, u32[]{:S(2)}, u32[]{:S(2)}) collective-permute-start(f32[16,64,128]{2,1,0:T(8,128)S(1)} %get-tuple-element.20), channel_id=1, source_target_pairs={{0,1},{1,0},{2,3},{3,2},{4,5},{5,4},{6,7},{7,6},{8,9},{9,8},{10,11... | collective-permute-start | bytes 1572872 | tf_op jit(solution)/shard_map/ppermute | solution.py:248
  128.2 1.5 collective-permute-done.6.got_ref
  132.7 9.1 %all-to-all-start.7 = ((s16[16,80,128]{2,1,0:T(8,128)(2,1)}), s16[16,80,128]{2,1,0:T(8,128)(2,1)S(1)}, u32[]{:S(2)}, u32[]{:S(2)}) async-start(s16[16,80,128]{2,1,0:T(8,128)(2,1)} %join.3), calls=%async_computation.7 | async-start | bytes 655360 | tf_op jit(solution)/shard_map/all_to_all | solution.py:225
  141.7 2.8 %collective-permute-start.5 = (s16[16,80,128]{2,1,0:T(8,128)(2,1)S(1)}, s16[16,80,128]{2,1,0:T(8,128)(2,1)S(1)}, u32[]{:S(2)}, u32[]{:S(2)}) collective-permute-start(s16[16,80,128]{2,1,0:T(8,128)(2,1)S(1)} %all-to-all-done.5.own_ref.after_ref), channel_id=1, source_target_pairs={{0,1},{1,0},{2,3},{3,2},{4,5},{5,4},{6,7},{7,6},{8,9},{9,8},{10,11... | collective-permute-start | bytes 983048 | tf_op jit(solution)/shard_map/ppermute | solution.py:253
  144.6 1.2 collective-permute-done.5.other_ref
  145.8 4.8 %mirror.3 = s16[16,80,128]{2,1,0:T(8,128)(2,1)} custom-call(s32[5,64]{1,0:T(8,128)S(1)} %stack.2.meta_ref, s16[16,80,128]{2,1,0:T(8,128)(2,1)S(1)} %all-to-all-done.5.own_ref.after_ref, s16[16,80,128]{2,1,0:T(8,128)(2,1)S(1)} %collective-permute-done.5.other_ref, bf16[64,128,128]{2,1,0:T(8,128)(2,1)S(1)} %bitcast.22), custom_call_target="tpu_custom_call" | custom-call | tf_op jit(solution)/shard_map/mirror/pallas_call | solution.py:171
  150.6 2.4 %all-to-all-done.7.got_ref = s16[16,80,128]{2,1,0:T(8,128)(2,1)S(1)} async-done(((s16[16,80,128]{2,1,0:T(8,128)(2,1)}), s16[16,80,128]{2,1,0:T(8,128)(2,1)S(1)}, u32[]{:S(2)}, u32[]{:S(2)}) %all-to-all-start.7) | async-done | bytes 327712 | tf_op jit(solution)/shard_map/all_to_all | solution.py:225
  153.0 8.1 %all-to-all-start.6 = ((s16[16,80,128]{2,1,0:T(8,128)(2,1)}), s16[16,80,128]{2,1,0:T(8,128)(2,1)S(1)}, u32[]{:S(2)}, u32[]{:S(2)}) async-start(s16[16,80,128]{2,1,0:T(8,128)(2,1)} %mirror.3), calls=%async_computation.6 | async-start | bytes 655360 | tf_op jit(solution)/shard_map/all_to_all | solution.py:222
  161.4 12.0 %collective-permute-start.7 = (f32[64,128]{1,0:T(8,128)S(1)}, f32[64,128]{1,0:T(8,128)S(1)}, u32[]{:S(2)}, u32[]{:S(2)}) collective-permute-start(f32[64,128]{1,0:T(8,128)S(1)} %sum.3), channel_id=1, source_target_pairs={{0,0},{1,32},{2,64},{3,96},{4,128},{5,160},{6,192},{7,224},{8,256}... | collective-permute-start | bytes 98312 | tf_op jit(solution)/shard_map/ppermute | solution.py:219
  173.4 5.9 %collective-permute-done.7.row_ref = f32[64,128]{1,0:T(8,128)S(1)} collective-permute-done((f32[64,128]{1,0:T(8,128)S(1)}, f32[64,128]{1,0:T(8,128)S(1)}, u32[]{:S(2)}, u32[]{:S(2)}) %collective-permute-start.7) | collective-permute-done | bytes 32800 | tf_op jit(solution)/shard_map/ppermute | solution.py:219
  (41 shorter events, 12.1 us)
Async XLA Ops:
  0.0 0.8 copy-start.6
  1.8 26.7 %all-to-all-start = ((s16[16,80,128]{2,1,0:T(8,128)(2,1)}), s16[16,80,128]{2,1,0:T(8,128)(2,1)S(1)}, u32[]{:S(2)}, u32[]{:S(2)}) async-start(s16[16,80,128]{2,1,0:T(8,128)(2,1)} %get-tuple-element.13), calls=%async_computation | async-start | bytes 655360 | tf_op jit(solution)/shard_map/all_to_all | solution.py:222
  10.6 17.9 %collective-permute-start = (s16[80,128]{1,0:T(8,128)(2,1)S(1)}, s16[80,128]{1,0:T(8,128)(2,1)S(1)}, u32[]{:S(2)}, u32[]{:S(2)}) collective-permute-start(s16[80,128]{1,0:T(8,128)(2,1)S(1)} %get-tuple-element.14), channel_id=1, source_target_pairs={{0,0},{1,32},{2,64},{3,96},{4,128},{5,160},{6,192},{7,224},{8,256}... | collective-permute-start | bytes 61448 | tf_op jit(solution)/shard_map/ppermute | solution.py:219
  29.3 19.0 %all-to-all-start.1 = ((s16[16,80,128]{2,1,0:T(8,128)(2,1)}), s16[16,80,128]{2,1,0:T(8,128)(2,1)S(1)}, u32[]{:S(2)}, u32[]{:S(2)}) async-start(s16[16,80,128]{2,1,0:T(8,128)(2,1)} %copies.2), calls=%async_computation.1 | async-start | bytes 655360 | tf_op jit(solution)/shard_map/all_to_all | solution.py:225
  35.8 1.6 copy-start
  37.4 26.3 %copy-start.1 = (bf16[1,1,64,128,128]{4,3,2,1,0:T(8,128)(2,1)S(1)}, bf16[1,1,64,128,128]{4,3,2,1,0:T(8,128)(2,1)}, u32[]{:S(2)}) copy-start(bf16[1,1,64,128,128]{4,3,2,1,0:T(8,128)(2,1)} %param.9) | copy-start | bytes 6291460
  40.8 6.7 %collective-permute-start.2 = (f32[16,64,128]{2,1,0:T(8,128)S(1)}, f32[16,64,128]{2,1,0:T(8,128)S(1)}, u32[]{:S(2)}, u32[]{:S(2)}) collective-permute-start(f32[16,64,128]{2,1,0:T(8,128)S(1)} %get-tuple-element.16), channel_id=1, source_target_pairs={{0,1},{1,0},{2,3},{3,2},{4,5},{5,4},{6,7},{7,6},{8,9},{9,8},{10,11... | collective-permute-start | bytes 1572872 | tf_op jit(solution)/shard_map/ppermute | solution.py:248
  47.5 0.8 copy-start.2
  48.3 1.0 copy-start.3
  50.4 27.5 %copy-start.8 = (s32[1,64]{1,0:T(1,128)S(1)}, s32[1,64]{1,0:T(1,128)}, u32[]{:S(2)}) copy-start(s32[1,64]{1,0:T(1,128)} %param.7) | copy-start | bytes 772
  50.4 20.7 %all-to-all-start.3 = ((s16[16,80,128]{2,1,0:T(8,128)(2,1)}), s16[16,80,128]{2,1,0:T(8,128)(2,1)S(1)}, u32[]{:S(2)}, u32[]{:S(2)}) async-start(s16[16,80,128]{2,1,0:T(8,128)(2,1)} %join.2), calls=%async_computation.3 | async-start | bytes 655360 | tf_op jit(solution)/shard_map/all_to_all | solution.py:225
  59.6 30.6 %copy-start.9 = (s32[1,64]{1,0:T(1,128)S(1)}, s32[1,64]{1,0:T(1,128)}, u32[]{:S(2)}) copy-start(s32[1,64]{1,0:T(1,128)} %param.8) | copy-start | bytes 772
  59.6 35.8 %copy-start.7 = (f32[1,64,128]{2,1,0:T(8,128)S(1)}, f32[1,64,128]{2,1,0:T(8,128)}, u32[]{:S(2)}) copy-start(f32[1,64,128]{2,1,0:T(8,128)} %param.6) | copy-start | bytes 98308
  59.6 4.1 %collective-permute-start.1 = (s16[16,80,128]{2,1,0:T(8,128)(2,1)S(1)}, s16[16,80,128]{2,1,0:T(8,128)(2,1)S(1)}, u32[]{:S(2)}, u32[]{:S(2)}) collective-permute-start(s16[16,80,128]{2,1,0:T(8,128)(2,1)S(1)} %all-to-all-done.1.own_ref.after_ref), channel_id=1, source_target_pairs={{0,1},{1,0},{2,3},{3,2},{4,5},{5,4},{6,7},{7,6},{8,9},{9,8},{10,11... | collective-permute-start | bytes 983048 | tf_op jit(solution)/shard_map/ppermute | solution.py:253
  71.1 24.1 %all-to-all-start.2 = ((s16[16,80,128]{2,1,0:T(8,128)(2,1)}), s16[16,80,128]{2,1,0:T(8,128)(2,1)S(1)}, u32[]{:S(2)}, u32[]{:S(2)}) async-start(s16[16,80,128]{2,1,0:T(8,128)(2,1)} %mirror.2), calls=%async_computation.2 | async-start | bytes 655360 | tf_op jit(solution)/shard_map/all_to_all | solution.py:222
  78.2 17.1 %collective-permute-start.3 = (f32[64,128]{1,0:T(8,128)S(1)}, f32[64,128]{1,0:T(8,128)S(1)}, u32[]{:S(2)}, u32[]{:S(2)}) collective-permute-start(f32[64,128]{1,0:T(8,128)S(1)} %sum.2), channel_id=1, source_target_pairs={{0,0},{1,32},{2,64},{3,96},{4,128},{5,160},{6,192},{7,224},{8,256}... | collective-permute-start | bytes 98312 | tf_op jit(solution)/shard_map/ppermute | solution.py:219
  96.7 19.2 %all-to-all-start.4 = ((s16[16,80,128]{2,1,0:T(8,128)(2,1)}), s16[16,80,128]{2,1,0:T(8,128)(2,1)S(1)}, u32[]{:S(2)}, u32[]{:S(2)}) async-start(s16[16,80,128]{2,1,0:T(8,128)(2,1)} %get-tuple-element.17), calls=%async_computation.4 | async-start | bytes 655360 | tf_op jit(solution)/shard_map/all_to_all | solution.py:222
  100.1 15.7 %collective-permute-start.4 = (s16[80,128]{1,0:T(8,128)(2,1)S(1)}, s16[80,128]{1,0:T(8,128)(2,1)S(1)}, u32[]{:S(2)}, u32[]{:S(2)}) collective-permute-start(s16[80,128]{1,0:T(8,128)(2,1)S(1)} %get-tuple-element.18), channel_id=1, source_target_pairs={{0,0},{1,32},{2,64},{3,96},{4,128},{5,160},{6,192},{7,224},{8,256}... | collective-permute-start | bytes 61448 | tf_op jit(solution)/shard_map/ppermute | solution.py:219
  116.6 13.9 %all-to-all-start.5 = ((s16[16,80,128]{2,1,0:T(8,128)(2,1)}), s16[16,80,128]{2,1,0:T(8,128)(2,1)S(1)}, u32[]{:S(2)}, u32[]{:S(2)}) async-start(s16[16,80,128]{2,1,0:T(8,128)(2,1)} %copies.3), calls=%async_computation.5 | async-start | bytes 655360 | tf_op jit(solution)/shard_map/all_to_all | solution.py:225
  124.1 5.6 %collective-permute-start.6 = (f32[16,64,128]{2,1,0:T(8,128)S(1)}, f32[16,64,128]{2,1,0:T(8,128)S(1)}, u32[]{:S(2)}, u32[]{:S(2)}) collective-permute-start(f32[16,64,128]{2,1,0:T(8,128)S(1)} %get-tuple-element.20), channel_id=1, source_target_pairs={{0,1},{1,0},{2,3},{3,2},{4,5},{5,4},{6,7},{7,6},{8,9},{9,8},{10,11... | collective-permute-start | bytes 1572872 | tf_op jit(solution)/shard_map/ppermute | solution.py:248
  129.7 0.8 copy-start.4
  130.5 1.0 copy-start.5
  132.7 20.4 %all-to-all-start.7 = ((s16[16,80,128]{2,1,0:T(8,128)(2,1)}), s16[16,80,128]{2,1,0:T(8,128)(2,1)S(1)}, u32[]{:S(2)}, u32[]{:S(2)}) async-start(s16[16,80,128]{2,1,0:T(8,128)(2,1)} %join.3), calls=%async_computation.7 | async-start | bytes 655360 | tf_op jit(solution)/shard_map/all_to_all | solution.py:225
  141.7 4.1 %collective-permute-start.5 = (s16[16,80,128]{2,1,0:T(8,128)(2,1)S(1)}, s16[16,80,128]{2,1,0:T(8,128)(2,1)S(1)}, u32[]{:S(2)}, u32[]{:S(2)}) collective-permute-start(s16[16,80,128]{2,1,0:T(8,128)(2,1)S(1)} %all-to-all-done.5.own_ref.after_ref), channel_id=1, source_target_pairs={{0,1},{1,0},{2,3},{3,2},{4,5},{5,4},{6,7},{7,6},{8,9},{9,8},{10,11... | collective-permute-start | bytes 983048 | tf_op jit(solution)/shard_map/ppermute | solution.py:253
  153.0 26.2 %all-to-all-start.6 = ((s16[16,80,128]{2,1,0:T(8,128)(2,1)}), s16[16,80,128]{2,1,0:T(8,128)(2,1)S(1)}, u32[]{:S(2)}, u32[]{:S(2)}) async-start(s16[16,80,128]{2,1,0:T(8,128)(2,1)} %mirror.3), calls=%async_computation.6 | async-start | bytes 655360 | tf_op jit(solution)/shard_map/all_to_all | solution.py:222
  161.4 17.9 %collective-permute-start.7 = (f32[64,128]{1,0:T(8,128)S(1)}, f32[64,128]{1,0:T(8,128)S(1)}, u32[]{:S(2)}, u32[]{:S(2)}) collective-permute-start(f32[64,128]{1,0:T(8,128)S(1)} %sum.3), channel_id=1, source_target_pairs={{0,0},{1,32},{2,64},{3,96},{4,128},{5,160},{6,192},{7,224},{8,256}... | collective-permute-start | bytes 98312 | tf_op jit(solution)/shard_map/ppermute | solution.py:219

commit v2 on v1

--- a/solution.py
+++ b/solution.py
@@ -12,7 +12,7 @@
 STEPS = 3840.0
 SCALE_STEPS = 64.0
 TINY = 1e-37
-VMEM = 48 * 1024 * 1024
+VMEM = 24 * 1024 * 1024
 
 
 def encode(x):
@@ -64,11 +64,26 @@
         copies_ref[i] = one_ref[...]
 
 
-def forward_kernel(meta_ref, got_ref, tiles_ref, keep_ref, send_ref, msg, acc):
-    pieces = got_ref.shape[0]
-    rows = got_ref.shape[1] - HEAD
+def place(list_ref, count_ref, slot, row_tiles, col_tiles):
+    n_brow, n_bcol = lax.axis_size("brow"), lax.axis_size("bcol")
+    row = jnp.clip(list_ref[0, slot], 0, row_tiles - 1)
+    col = jnp.clip(list_ref[1, slot], 0, col_tiles - 1)
+    live = slot < count_ref[0, 0]
+    same = lax.axis_index("brow") + n_brow * row == lax.axis_index("bcol") + n_bcol * col
+    return row, col, live, same
+
+
+def held_at(held_ref, column, rows):
+    return pl.multiple_of(held_ref[lax.axis_index("brow"), column] * rows, rows)
+
+
+def forward_kernel(
+    list_ref, count_ref, held_ref, got_ref, tiles_ref, keep_ref, send_ref, msg, acc
+):
+    pieces, rows, classes = got_ref.shape[0], got_ref.shape[1] - HEAD, got_ref.shape[2]
     size = tiles_ref.shape[-1]
-    classes = got_ref.shape[2]
+    col_tiles = msg.shape[0] // size
+    row_tiles = acc.shape[0] // size - 1
     for i in range(pieces):
         high, low = split(decode(got_ref[i]))
         msg[i * rows : (i + 1) * rows, :classes] = high
@@ -76,26 +91,24 @@
     acc[...] = jnp.zeros_like(acc)
 
     def body(s, carry):
-        col = meta_ref[0, s]
-        row = meta_ref[1, s]
+        row, col, live, _ = place(list_ref, count_ref, s, row_tiles, col_tiles)
         part = jnp.dot(
             tiles_ref[s], msg[pl.ds(pl.multiple_of(col * size, size), size), :],
             preferred_element_type=jnp.float32,
         )
+        row = jnp.where(live, row, row_tiles)
         where = pl.ds(pl.multiple_of(row * size, size), size)
         acc[where, :] += part[:, :classes] + part[:, classes:]
         return carry
 
     lax.fori_loop(0, tiles_ref.shape[0], body, 0, unroll=8)
-    core = meta_ref[4, 0]
-    kept = keep_ref.shape[0]
-    for j in range(kept):
-        p = 2 * (j % (kept // 2)) + j // (kept // 2)
-        keep_ref[j] = acc[pl.ds(pl.multiple_of(p * size + core * rows, rows), rows), :]
-        send_ref[j] = acc[pl.ds(pl.multiple_of(p * size + (1 - core) * rows, rows), rows), :]
-
-
-def join_kernel(after_ref, keep_ref, got_ref, out_ref):
+    core = lax.rem(lax.axis_index("bcol"), 2)
+    for j in range(keep_ref.shape[0]):
+        keep_ref[j] = acc[pl.ds(held_at(held_ref, 2 * j + core, rows), rows), :]
+        send_ref[j] = acc[pl.ds(held_at(held_ref, 2 * j + 1 - core, rows), rows), :]
+
+
+def join_kernel(keep_ref, got_ref, out_ref):
     rows = keep_ref.shape[1]
     for j in range(keep_ref.shape[0]):
         code, head = encode(keep_ref[j] + got_ref[j])
@@ -103,28 +116,29 @@
         out_ref[j, rows:] = head
 
 
-def mirror_kernel(meta_ref, own_ref, other_ref, tiles_ref, out_ref, msg, acc):
-    pieces = own_ref.shape[0]
-    rows = own_ref.shape[1] - HEAD
+def mirror_kernel(
+    list_ref, count_ref, held_ref, own_ref, other_ref, tiles_ref, out_ref, msg, acc
+):
+    pieces, rows, classes = own_ref.shape[0], own_ref.shape[1] - HEAD, own_ref.shape[2]
     size = tiles_ref.shape[-1]
-    classes = own_ref.shape[2]
-    core = meta_ref[4, 0]
+    row_tiles = msg.shape[0] // size
+    col_tiles = acc.shape[0] // size - 1
+    core = lax.rem(lax.axis_index("bcol"), 2)
     for j in range(pieces):
-        p = 2 * (j % (pieces // 2)) + j // (pieces // 2)
-        for ref, half in ((own_ref, core), (other_ref, 1 - core)):
+        for ref, column in ((own_ref, 2 * j + core), (other_ref, 2 * j + 1 - core)):
             high, low = split(decode(ref[j]))
-            where = pl.ds(pl.multiple_of(p * size + half * rows, rows), rows)
+            where = pl.ds(held_at(held_ref, column, rows), rows)
             msg[where, :classes] = high
             msg[where, classes:] = low
     acc[...] = jnp.zeros_like(acc)
 
     def body(s, carry):
-        row = meta_ref[2, s]
-        col = meta_ref[3, s]
+        row, col, live, same = place(list_ref, count_ref, s, row_tiles, col_tiles)
         part = lax.dot_general(
             tiles_ref[s], msg[pl.ds(pl.multiple_of(row * size, size), size), :],
             (((0,), (0,)), ((), ())), preferred_element_type=jnp.float32,
         )
+        col = jnp.where(live & jnp.logical_not(same), col, col_tiles)
         where = pl.ds(pl.multiple_of(col * size, size), size)
         acc[where, :] += part[:, :classes] + part[:, classes:]
         return carry
@@ -159,6 +173,60 @@
 
 def last_kernel(got_ref, row_ref, scores_ref, scale_ref, seed_ref, out_ref):
     out_ref[...] = next_field(got_ref, row_ref, scores_ref, scale_ref, seed_ref)
+
+
+def hops(a, b):
+    def chip(device):
+        r, c = device
+        return c // 8, r // 2, c // 2 % 4 * 2 + r % 2
+
+    steps = (abs(i - j) for i, j in zip(chip(a), chip(b)))
+    return sum(min(step, length - step) for step, length in zip(steps, (4, 8, 8)))
+
+
+def cheapest(cost):
+    n = len(cost)
+    u, v, match, way = [0] * (n + 1), [0] * (n + 1), [0] * (n + 1), [0] * (n + 1)
+    for i in range(1, n + 1):
+        match[0], j0 = i, 0
+        least, used = [math.inf] * (n + 1), [False] * (n + 1)
+        while match[j0]:
+            used[j0] = True
+            i0, delta, j1 = match[j0], math.inf, 0
+            for j in range(1, n + 1):
+                if not used[j]:
+                    now = cost[i0 - 1][j - 1] - u[i0] - v[j]
+                    if now < least[j]:
+                        least[j], way[j] = now, j0
+                    if least[j] < delta:
+                        delta, j1 = least[j], j
+            for j in range(n + 1):
+                if used[j]:
+                    u[match[j]] += delta
+                    v[j] -= delta
+                else:
+                    least[j] -= delta
+            j0 = j1
+        while j0:
+            match[j0] = match[way[j0]]
+            j0 = way[j0]
+    columns = [0] * n
+    for j in range(1, n + 1):
+        columns[match[j] - 1] = j - 1
+    return columns
+
+
+def holders(n_brow, n_bcol):
+    pairs, pieces = [], []
+    for r in range(n_brow):
+        owners = [(b, c) for c in range(r, n_bcol, n_brow) for b in range(n_brow)]
+        cost = [[hops(owner, (r, k)) ** 6 for k in range(n_bcol)] for owner in owners]
+        held = [0] * n_bcol
+        for (b, c), k in zip(owners, cheapest(cost)):
+            pairs.append((b * n_bcol + c, r * n_bcol + k))
+            held[k] = 2 * (b // 2 * (n_bcol // n_brow) + c // n_brow) + b % 2
+        pieces.append(held)
+    return pairs, pieces
 
 
 WHOLE = pl.BlockSpec(memory_space=pltpu.VMEM)
@@ -189,20 +257,10 @@
     size = tiles.shape[-1]
     col_tiles = n_brow * rows // size
     row_tiles = ratio * col_tiles
-    my_row = lax.axis_index("brow")
-    my_col = lax.axis_index("bcol")
     stored = tiles[0, 0]
-    local_row = jnp.clip(tile_list[0, 0, 0], 0, row_tiles - 1)
-    local_col = jnp.clip(tile_list[0, 0, 1], 0, col_tiles - 1)
-    live = jnp.arange(capacity, dtype=jnp.int32) < tile_count[0, 0]
-    same = my_row + n_brow * local_row == my_col + n_bcol * local_col
-    meta = jnp.stack([
-        local_col,
-        jnp.where(live, local_row, row_tiles),
-        local_row,
-        jnp.where(live & jnp.logical_not(same), local_col, col_tiles),
-        jnp.full((capacity,), my_col % 2, jnp.int32),
-    ])
+    slots = tile_list[0, 0]
+    pairs, pieces = holders(n_brow, n_bcol)
+    held = jnp.asarray(pieces, jnp.int32)
     initial = scores[0]
     seeds = jnp.broadcast_to(seed_mask[0].astype(jnp.float32)[:, None], (rows, classes))
     scale = jnp.broadcast_to(degree[0].astype(jnp.float32)[:, None], (rows, classes))
@@ -210,13 +268,10 @@
     half = n_bcol // 2
     groups = [[2 * j + k for j in range(half)] for k in range(2)]
     exchange = [(i, i ^ 1) for i in range(n_bcol)]
-    transpose = [
-        (a * n_bcol + n_brow * h + b, b * n_bcol + n_brow * h + a)
-        for a in range(n_brow) for h in range(ratio) for b in range(n_brow)
-    ]
-
-    def swap(value):
-        return lax.ppermute(value, ("brow", "bcol"), transpose)
+    back = [(holder, owner) for owner, holder in pairs]
+
+    def swap(value, way):
+        return lax.ppermute(value, ("brow", "bcol"), way)
 
     def over_brow(value):
         return lax.all_to_all(value, "brow", split_axis=0, concat_axis=0, tiled=True)
@@ -236,29 +291,28 @@
     for sweep in range(SWEEPS):
         col_got = over_brow(copies)
         copies = call(
-            copies_kernel, "copies", bcol_pieces, (col_got, swap(one)), [ANYWHERE, WHOLE]
+            copies_kernel, "copies", bcol_pieces, (col_got, swap(one, pairs)), [ANYWHERE, WHOLE]
         )
         row_own = over_bcol(copies)
         keep, send = call(
-            forward_kernel, "forward", (sums, sums), (meta, col_got, stored),
-            [SCALARS, WHOLE, WHOLE],
+            forward_kernel, "forward", (sums, sums), (slots, tile_count, held, col_got, stored),
+            [SCALARS, SCALARS, SCALARS, WHOLE, WHOLE],
             [pltpu.VMEM((col_tiles * size, 2 * classes), jnp.bfloat16),
              pltpu.VMEM(((row_tiles + 1) * size, classes), jnp.float32)],
         )
         got = lax.ppermute(send, "bcol", exchange)
-        joined = call(
-            join_kernel, "join", bcol_pieces, (row_own, keep, got), [ANYWHERE, WHOLE, WHOLE]
-        )
+        joined = call(join_kernel, "join", bcol_pieces, (keep, got))
         row_got = over_bcol(joined)
         row_other = lax.ppermute(row_own, "bcol", exchange)
         col_parts = call(
-            mirror_kernel, "mirror", brow_pieces, (meta, row_own, row_other, stored),
-            [SCALARS, WHOLE, WHOLE, WHOLE],
+            mirror_kernel, "mirror", brow_pieces,
+            (slots, tile_count, held, row_own, row_other, stored),
+            [SCALARS, SCALARS, SCALARS, WHOLE, WHOLE, WHOLE],
             [pltpu.VMEM((row_tiles * size, 2 * classes), jnp.bfloat16),
              pltpu.VMEM(((col_tiles + 1) * size, classes), jnp.float32)],
         )
         col_sums = over_brow(col_parts)
-        row_sum = swap(call(sum_kernel, "sum", share, (row_got,)))
+        row_sum = swap(call(sum_kernel, "sum", share, (row_got,)), back)
         args = (col_sums, row_sum, initial, scale, seeds)
         if sweep < SWEEPS - 1:
             copies, one = call(middle_kernel, "middle", (brow_pieces, piece), args)

time: 181 us -> 170 us (0.939)
  the two profiles are of different devices: /device:TPU:11 before, /device:TPU:56 now
where the time goes in v2:
time: 170 us; the launch traced here: 169 us
  starting transfers between devices  81.3 us (48%)
  waiting for transfers between devices  58.6 us (34%)
  Pallas kernels  24 us (14%)
  local copies, waits for them, and re-layouts  3.89 us (2%)
    ppermute x4, waiting for transfers between devices, swap(): return lax.ppermute(value, ('brow', 'bcol'), way)  33.9 us
    all_to_all x4, starting transfers between devices, over_brow(): lax.all_to_all(value, 'brow', split_axis=0, concat_axis=0, tiled=True)  31.2 us
    pallas_call x13, Pallas kernels, call(): pl.pallas_call(kernel, out_shape=outs, in_specs=specs or [WHOLE] * len(ar...  24 us
    ppermute x4, starting transfers between devices, swap(): return lax.ppermute(value, ('brow', 'bcol'), way)  22.2 us
    all_to_all x4, starting transfers between devices, over_bcol(): lax.all_to_all(value, 'bcol', split_axis=0, concat_axis=0, tiled=True, ax...  20.2 us
    all_to_all x4, waiting for transfers between devices, over_bcol(): lax.all_to_all(value, 'bcol', split_axis=0, concat_axis=0, tiled=True, ax...  17.8 us
    ppermute x2, starting transfers between devices, on_device(): got = lax.ppermute(send, 'bcol', exchange)  3.84 us
    ppermute x2, starting transfers between devices, on_device(): row_other = lax.ppermute(row_own, 'bcol', exchange)  3.84 us
  transfers between devices with their start and end apart: 16, of which 12 were waited for; matrix products, arithmetic and copies ran while one was open for 0% of the time, Pallas kernels for 11%

profile of v2, /device:TPU:56, one launch (start us, length us, event | category | flops | bytes accessed | tf_op | source)
XLA Modules:
  0.0 168.6 jit_solution(14396154957900954871)
XLA Ops:
  1.8 8.7 %all-to-all-start = ((s16[16,80,128]{2,1,0:T(8,128)(2,1)}), s16[16,80,128]{2,1,0:T(8,128)(2,1)S(1)}, u32[]{:S(2)}, u32[]{:S(2)}) async-start(s16[16,80,128]{2,1,0:T(8,128)(2,1)} %get-tuple-element.13), calls=%async_computation | async-start | bytes 655360 | tf_op jit(solution)/shard_map/all_to_all | solution.py:277
  10.5 11.8 %collective-permute-start = (s16[80,128]{1,0:T(8,128)(2,1)S(1)}, s16[80,128]{1,0:T(8,128)(2,1)S(1)}, u32[]{:S(2)}, u32[]{:S(2)}) collective-permute-start(s16[80,128]{1,0:T(8,128)(2,1)S(1)} %get-tuple-element.14), channel_id=1, source_target_pairs={{0,28},{32,12},{64,31},{96,4},{128,7},{160,26},{192,25},{224,3},{2... | collective-permute-start | bytes 61448 | tf_op jit(solution)/shard_map/ppermute | solution.py:274
  22.3 8.1 %collective-permute-done.one_ref = s16[80,128]{1,0:T(8,128)(2,1)S(1)} collective-permute-done((s16[80,128]{1,0:T(8,128)(2,1)S(1)}, s16[80,128]{1,0:T(8,128)(2,1)S(1)}, u32[]{:S(2)}, u32[]{:S(2)}) %collective-permute-start) | collective-permute-done | bytes 20512 | tf_op jit(solution)/shard_map/ppermute | solution.py:274
  31.2 3.5 %all-to-all-start.1 = ((s16[16,80,128]{2,1,0:T(8,128)(2,1)}), s16[16,80,128]{2,1,0:T(8,128)(2,1)S(1)}, u32[]{:S(2)}, u32[]{:S(2)}) async-start(s16[16,80,128]{2,1,0:T(8,128)(2,1)} %copies.2), calls=%async_computation.1 | async-start | bytes 655360 | tf_op jit(solution)/shard_map/all_to_all | solution.py:280
  38.3 3.5 %forward.2 = (f32[16,64,128]{2,1,0:T(8,128)S(1)}, f32[16,64,128]{2,1,0:T(8,128)S(1)}) custom-call(s32[2,64]{1,0:T(2,128)S(1)} %bitcast.15, s32[1,1]{1,0:T(1,128)S(6)} %copy.8.count_ref, s32[16,32]{1,0:T(8,128)S(1)} %copy-done.4, s16[16,80,128]{2,1,0:T(8,128)(2,1)S(1)} %all-to-all-done.after_ref.got_ref, bf16[64,128,128]{2,1,0:T(8,128)(2,1)S(1)} %bitcast.8), custom_call_target="tpu_custom_call" | custom-call | tf_op jit(solution)/shard_map/forward/pallas_call | solution.py:239
  41.9 1.9 %collective-permute-start.2 = (f32[16,64,128]{2,1,0:T(8,128)S(1)}, f32[16,64,128]{2,1,0:T(8,128)S(1)}, u32[]{:S(2)}, u32[]{:S(2)}) collective-permute-start(f32[16,64,128]{2,1,0:T(8,128)S(1)} %get-tuple-element.16), channel_id=1, source_target_pairs={{0,1},{1,0},{2,3},{3,2},{4,5},{5,4},{6,7},{7,6},{8,9},{9,8},{10,11... | collective-permute-start | bytes 1572872 | tf_op jit(solution)/shard_map/ppermute | solution.py:303
  43.8 1.9 %collective-permute-done.2.got_ref = f32[16,64,128]{2,1,0:T(8,128)S(1)} collective-permute-done((f32[16,64,128]{2,1,0:T(8,128)S(1)}, f32[16,64,128]{2,1,0:T(8,128)S(1)}, u32[]{:S(2)}, u32[]{:S(2)}) %collective-permute-start.2) | collective-permute-done | bytes 524320 | tf_op jit(solution)/shard_map/ppermute | solution.py:303
  46.8 2.2 %all-to-all-done.1.own_ref = s16[16,80,128]{2,1,0:T(8,128)(2,1)S(1)} async-done(((s16[16,80,128]{2,1,0:T(8,128)(2,1)}), s16[16,80,128]{2,1,0:T(8,128)(2,1)S(1)}, u32[]{:S(2)}, u32[]{:S(2)}) %all-to-all-start.1) | async-done | bytes 327712 | tf_op jit(solution)/shard_map/all_to_all | solution.py:280
  48.9 7.5 %all-to-all-start.3 = ((s16[16,80,128]{2,1,0:T(8,128)(2,1)}), s16[16,80,128]{2,1,0:T(8,128)(2,1)S(1)}, u32[]{:S(2)}, u32[]{:S(2)}) async-start(s16[16,80,128]{2,1,0:T(8,128)(2,1)} %join.2), calls=%async_computation.3 | async-start | bytes 655360 | tf_op jit(solution)/shard_map/all_to_all | solution.py:280
  56.5 1.9 %collective-permute-start.1 = (s16[16,80,128]{2,1,0:T(8,128)(2,1)S(1)}, s16[16,80,128]{2,1,0:T(8,128)(2,1)S(1)}, u32[]{:S(2)}, u32[]{:S(2)}) collective-permute-start(s16[16,80,128]{2,1,0:T(8,128)(2,1)S(1)} %all-to-all-done.1.own_ref), channel_id=1, source_target_pairs={{0,1},{1,0},{2,3},{3,2},{4,5},{5,4},{6,7},{7,6},{8,9},{9,8},{10,11... | collective-permute-start | bytes 983048 | tf_op jit(solution)/shard_map/ppermute | solution.py:306
  58.4 1.6 collective-permute-done.1.other_ref
  60.0 4.9 %mirror.2 = s16[16,80,128]{2,1,0:T(8,128)(2,1)} custom-call(s32[2,64]{1,0:T(2,128)S(1)} %bitcast.16, s32[1,1]{1,0:T(1,128)S(6)} %copy.8.count_ref, s32[16,32]{1,0:T(8,128)S(1)} %copy-done.5, s16[16,80,128]{2,1,0:T(8,128)(2,1)S(1)} %all-to-all-done.1.own_ref, s16[16,80,128]{2,1,0:T(8,128)(2,1)S(1)} %collective-permute-done.1.other_ref, ...), custom_call_target="tpu_custom_call" | custom-call | tf_op jit(solution)/shard_map/mirror/pallas_call | solution.py:239
  65.0 5.8 %all-to-all-done.3.got_ref = s16[16,80,128]{2,1,0:T(8,128)(2,1)S(1)} async-done(((s16[16,80,128]{2,1,0:T(8,128)(2,1)}), s16[16,80,128]{2,1,0:T(8,128)(2,1)S(1)}, u32[]{:S(2)}, u32[]{:S(2)}) %all-to-all-start.3) | async-done | bytes 327712 | tf_op jit(solution)/shard_map/all_to_all | solution.py:280
  70.8 7.9 %all-to-all-start.2 = ((s16[16,80,128]{2,1,0:T(8,128)(2,1)}), s16[16,80,128]{2,1,0:T(8,128)(2,1)S(1)}, u32[]{:S(2)}, u32[]{:S(2)}) async-start(s16[16,80,128]{2,1,0:T(8,128)(2,1)} %mirror.2), calls=%async_computation.2 | async-start | bytes 655360 | tf_op jit(solution)/shard_map/all_to_all | solution.py:277
  78.9 4.5 %collective-permute-start.3 = (f32[64,128]{1,0:T(8,128)S(1)}, f32[64,128]{1,0:T(8,128)S(1)}, u32[]{:S(2)}, u32[]{:S(2)}) collective-permute-start(f32[64,128]{1,0:T(8,128)S(1)} %sum.2), channel_id=1, source_target_pairs={{28,0},{12,32},{31,64},{4,96},{7,128},{26,160},{25,192},{3,224},{0... | collective-permute-start | bytes 98312 | tf_op jit(solution)/shard_map/ppermute | solution.py:274
  83.3 7.7 %collective-permute-done.3.row_ref = f32[64,128]{1,0:T(8,128)S(1)} collective-permute-done((f32[64,128]{1,0:T(8,128)S(1)}, f32[64,128]{1,0:T(8,128)S(1)}, u32[]{:S(2)}, u32[]{:S(2)}) %collective-permute-start.3) | collective-permute-done | bytes 32800 | tf_op jit(solution)/shard_map/ppermute | solution.py:274
  92.4 6.6 %all-to-all-start.4 = ((s16[16,80,128]{2,1,0:T(8,128)(2,1)}), s16[16,80,128]{2,1,0:T(8,128)(2,1)S(1)}, u32[]{:S(2)}, u32[]{:S(2)}) async-start(s16[16,80,128]{2,1,0:T(8,128)(2,1)} %get-tuple-element.17), calls=%async_computation.4 | async-start | bytes 655360 | tf_op jit(solution)/shard_map/all_to_all | solution.py:277
  99.0 1.9 %collective-permute-start.4 = (s16[80,128]{1,0:T(8,128)(2,1)S(1)}, s16[80,128]{1,0:T(8,128)(2,1)S(1)}, u32[]{:S(2)}, u32[]{:S(2)}) collective-permute-start(s16[80,128]{1,0:T(8,128)(2,1)S(1)} %get-tuple-element.18), channel_id=1, source_target_pairs={{0,28},{32,12},{64,31},{96,4},{128,7},{160,26},{192,25},{224,3},{2... | collective-permute-start | bytes 61448 | tf_op jit(solution)/shard_map/ppermute | solution.py:274
  100.9 10.1 %collective-permute-done.4.one_ref = s16[80,128]{1,0:T(8,128)(2,1)S(1)} collective-permute-done((s16[80,128]{1,0:T(8,128)(2,1)S(1)}, s16[80,128]{1,0:T(8,128)(2,1)S(1)}, u32[]{:S(2)}, u32[]{:S(2)}) %collective-permute-start.4) | collective-permute-done | bytes 20512 | tf_op jit(solution)/shard_map/ppermute | solution.py:274
  111.7 3.5 %all-to-all-start.5 = ((s16[16,80,128]{2,1,0:T(8,128)(2,1)}), s16[16,80,128]{2,1,0:T(8,128)(2,1)S(1)}, u32[]{:S(2)}, u32[]{:S(2)}) async-start(s16[16,80,128]{2,1,0:T(8,128)(2,1)} %copies.3), calls=%async_computation.5 | async-start | bytes 655360 | tf_op jit(solution)/shard_map/all_to_all | solution.py:280
  115.3 3.5 %forward.3 = (f32[16,64,128]{2,1,0:T(8,128)S(1)}, f32[16,64,128]{2,1,0:T(8,128)S(1)}) custom-call(s32[2,64]{1,0:T(2,128)S(1)} %bitcast.17, s32[1,1]{1,0:T(1,128)S(6)} %copy.8.count_ref, s32[16,32]{1,0:T(8,128)S(1)} %copy-done.5, s16[16,80,128]{2,1,0:T(8,128)(2,1)S(1)} %all-to-all-done.4.after_ref.got_ref, bf16[64,128,128]{2,1,0:T(8,128)(2,1)S(1)} %bitcast.10), custom_call_target="tpu_custom_call" | custom-call | tf_op jit(solution)/shard_map/forward/pallas_call | solution.py:239
  118.8 1.9 %collective-permute-start.6 = (f32[16,64,128]{2,1,0:T(8,128)S(1)}, f32[16,64,128]{2,1,0:T(8,128)S(1)}, u32[]{:S(2)}, u32[]{:S(2)}) collective-permute-start(f32[16,64,128]{2,1,0:T(8,128)S(1)} %get-tuple-element.20), channel_id=1, source_target_pairs={{0,1},{1,0},{2,3},{3,2},{4,5},{5,4},{6,7},{7,6},{8,9},{9,8},{10,11... | collective-permute-start | bytes 1572872 | tf_op jit(solution)/shard_map/ppermute | solution.py:303
  120.7 1.9 %collective-permute-done.6.got_ref = f32[16,64,128]{2,1,0:T(8,128)S(1)} collective-permute-done((f32[16,64,128]{2,1,0:T(8,128)S(1)}, f32[16,64,128]{2,1,0:T(8,128)S(1)}, u32[]{:S(2)}, u32[]{:S(2)}) %collective-permute-start.6) | collective-permute-done | bytes 524320 | tf_op jit(solution)/shard_map/ppermute | solution.py:303
  123.7 4.0 %all-to-all-done.5.own_ref = s16[16,80,128]{2,1,0:T(8,128)(2,1)S(1)} async-done(((s16[16,80,128]{2,1,0:T(8,128)(2,1)}), s16[16,80,128]{2,1,0:T(8,128)(2,1)S(1)}, u32[]{:S(2)}, u32[]{:S(2)}) %all-to-all-start.5) | async-done | bytes 327712 | tf_op jit(solution)/shard_map/all_to_all | solution.py:280
  127.6 5.6 %all-to-all-start.7 = ((s16[16,80,128]{2,1,0:T(8,128)(2,1)}), s16[16,80,128]{2,1,0:T(8,128)(2,1)S(1)}, u32[]{:S(2)}, u32[]{:S(2)}) async-start(s16[16,80,128]{2,1,0:T(8,128)(2,1)} %join.3), calls=%async_computation.7 | async-start | bytes 655360 | tf_op jit(solution)/shard_map/all_to_all | solution.py:280
  133.2 1.9 %collective-permute-start.5 = (s16[16,80,128]{2,1,0:T(8,128)(2,1)S(1)}, s16[16,80,128]{2,1,0:T(8,128)(2,1)S(1)}, u32[]{:S(2)}, u32[]{:S(2)}) collective-permute-start(s16[16,80,128]{2,1,0:T(8,128)(2,1)S(1)} %all-to-all-done.5.own_ref), channel_id=1, source_target_pairs={{0,1},{1,0},{2,3},{3,2},{4,5},{5,4},{6,7},{7,6},{8,9},{9,8},{10,11... | collective-permute-start | bytes 983048 | tf_op jit(solution)/shard_map/ppermute | solution.py:306
  135.2 1.6 collective-permute-done.5.other_ref
  136.7 4.9 %mirror.3 = s16[16,80,128]{2,1,0:T(8,128)(2,1)} custom-call(s32[2,64]{1,0:T(2,128)S(1)} %bitcast.18, s32[1,1]{1,0:T(1,128)S(6)} %copy.8.count_ref, s32[16,32]{1,0:T(8,128)S(1)} %copy-done.5, s16[16,80,128]{2,1,0:T(8,128)(2,1)S(1)} %all-to-all-done.5.own_ref, s16[16,80,128]{2,1,0:T(8,128)(2,1)S(1)} %collective-permute-done.5.other_ref, ...), custom_call_target="tpu_custom_call" | custom-call | tf_op jit(solution)/shard_map/mirror/pallas_call | solution.py:239
  141.7 5.8 %all-to-all-done.7.got_ref = s16[16,80,128]{2,1,0:T(8,128)(2,1)S(1)} async-done(((s16[16,80,128]{2,1,0:T(8,128)(2,1)}), s16[16,80,128]{2,1,0:T(8,128)(2,1)S(1)}, u32[]{:S(2)}, u32[]{:S(2)}) %all-to-all-start.7) | async-done | bytes 327712 | tf_op jit(solution)/shard_map/all_to_all | solution.py:280
  147.5 8.0 %all-to-all-start.6 = ((s16[16,80,128]{2,1,0:T(8,128)(2,1)}), s16[16,80,128]{2,1,0:T(8,128)(2,1)S(1)}, u32[]{:S(2)}, u32[]{:S(2)}) async-start(s16[16,80,128]{2,1,0:T(8,128)(2,1)} %mirror.3), calls=%async_computation.6 | async-start | bytes 655360 | tf_op jit(solution)/shard_map/all_to_all | solution.py:277
  155.7 4.0 %collective-permute-start.7 = (f32[64,128]{1,0:T(8,128)S(1)}, f32[64,128]{1,0:T(8,128)S(1)}, u32[]{:S(2)}, u32[]{:S(2)}) collective-permute-start(f32[64,128]{1,0:T(8,128)S(1)} %sum.3), channel_id=1, source_target_pairs={{28,0},{12,32},{31,64},{4,96},{7,128},{26,160},{25,192},{3,224},{0... | collective-permute-start | bytes 98312 | tf_op jit(solution)/shard_map/ppermute | solution.py:274
  159.7 8.1 %collective-permute-done.7.row_ref = f32[64,128]{1,0:T(8,128)S(1)} collective-permute-done((f32[64,128]{1,0:T(8,128)S(1)}, f32[64,128]{1,0:T(8,128)S(1)}, u32[]{:S(2)}, u32[]{:S(2)}) %collective-permute-start.7) | collective-permute-done | bytes 32800 | tf_op jit(solution)/shard_map/ppermute | solution.py:274
  (37 shorter events, 11.0 us)
Async XLA Ops:
  0.0 0.8 copy-start.2
  1.8 28.6 %all-to-all-start = ((s16[16,80,128]{2,1,0:T(8,128)(2,1)}), s16[16,80,128]{2,1,0:T(8,128)(2,1)S(1)}, u32[]{:S(2)}, u32[]{:S(2)}) async-start(s16[16,80,128]{2,1,0:T(8,128)(2,1)} %get-tuple-element.13), calls=%async_computation | async-start | bytes 655360 | tf_op jit(solution)/shard_map/all_to_all | solution.py:277
  10.5 19.9 %collective-permute-start = (s16[80,128]{1,0:T(8,128)(2,1)S(1)}, s16[80,128]{1,0:T(8,128)(2,1)S(1)}, u32[]{:S(2)}, u32[]{:S(2)}) collective-permute-start(s16[80,128]{1,0:T(8,128)(2,1)S(1)} %get-tuple-element.14), channel_id=1, source_target_pairs={{0,28},{32,12},{64,31},{96,4},{128,7},{160,26},{192,25},{224,3},{2... | collective-permute-start | bytes 61448 | tf_op jit(solution)/shard_map/ppermute | solution.py:274
  31.2 17.8 %all-to-all-start.1 = ((s16[16,80,128]{2,1,0:T(8,128)(2,1)}), s16[16,80,128]{2,1,0:T(8,128)(2,1)S(1)}, u32[]{:S(2)}, u32[]{:S(2)}) async-start(s16[16,80,128]{2,1,0:T(8,128)(2,1)} %copies.2), calls=%async_computation.1 | async-start | bytes 655360 | tf_op jit(solution)/shard_map/all_to_all | solution.py:280
  35.4 1.6 copy-start
  37.0 0.7 copy-start.4
  37.7 0.7 copy-start.6
  38.3 21.7 %copy-start.1 = (bf16[1,1,64,128,128]{4,3,2,1,0:T(8,128)(2,1)S(1)}, bf16[1,1,64,128,128]{4,3,2,1,0:T(8,128)(2,1)}, u32[]{:S(2)}) copy-start(bf16[1,1,64,128,128]{4,3,2,1,0:T(8,128)(2,1)} %param.10) | copy-start | bytes 6291460
  38.3 21.7 %copy-start.5 = (s32[16,32]{1,0:T(8,128)S(1)}, s32[16,32]{1,0:T(8,128)}, u32[]{:S(2)}) copy-start(s32[16,32]{1,0:T(8,128)} %constant.2.clone.held_ref) | copy-start | bytes 6148
  38.3 21.7 %copy-start.7 = (s32[1,1,2,64]{3,2,1,0:T(2,128)S(1)}, s32[1,1,2,64]{3,2,1,0:T(2,128)}, u32[]{:S(2)}) copy-start(s32[1,1,2,64]{3,2,1,0:T(2,128)} %param.11) | copy-start | bytes 1540
  41.9 3.8 %collective-permute-start.2 = (f32[16,64,128]{2,1,0:T(8,128)S(1)}, f32[16,64,128]{2,1,0:T(8,128)S(1)}, u32[]{:S(2)}, u32[]{:S(2)}) collective-permute-start(f32[16,64,128]{2,1,0:T(8,128)S(1)} %get-tuple-element.16), channel_id=1, source_target_pairs={{0,1},{1,0},{2,3},{3,2},{4,5},{5,4},{6,7},{7,6},{8,9},{9,8},{10,11... | collective-permute-start | bytes 1572872 | tf_op jit(solution)/shard_map/ppermute | solution.py:303
  46.7 31.9 %copy-start.8 = (s32[1,64]{1,0:T(1,128)S(1)}, s32[1,64]{1,0:T(1,128)}, u32[]{:S(2)}) copy-start(s32[1,64]{1,0:T(1,128)} %param.8) | copy-start | bytes 772
  48.9 21.8 %all-to-all-start.3 = ((s16[16,80,128]{2,1,0:T(8,128)(2,1)}), s16[16,80,128]{2,1,0:T(8,128)(2,1)S(1)}, u32[]{:S(2)}, u32[]{:S(2)}) async-start(s16[16,80,128]{2,1,0:T(8,128)(2,1)} %join.2), calls=%async_computation.3 | async-start | bytes 655360 | tf_op jit(solution)/shard_map/all_to_all | solution.py:280
  56.5 26.9 %copy-start.9 = (s32[1,64]{1,0:T(1,128)S(1)}, s32[1,64]{1,0:T(1,128)}, u32[]{:S(2)}) copy-start(s32[1,64]{1,0:T(1,128)} %param.9) | copy-start | bytes 772
  56.5 34.7 %copy-start.3 = (f32[1,64,128]{2,1,0:T(8,128)S(1)}, f32[1,64,128]{2,1,0:T(8,128)}, u32[]{:S(2)}) copy-start(f32[1,64,128]{2,1,0:T(8,128)} %param.7) | copy-start | bytes 98308
  56.5 3.5 %collective-permute-start.1 = (s16[16,80,128]{2,1,0:T(8,128)(2,1)S(1)}, s16[16,80,128]{2,1,0:T(8,128)(2,1)S(1)}, u32[]{:S(2)}, u32[]{:S(2)}) collective-permute-start(s16[16,80,128]{2,1,0:T(8,128)(2,1)S(1)} %all-to-all-done.1.own_ref), channel_id=1, source_target_pairs={{0,1},{1,0},{2,3},{3,2},{4,5},{5,4},{6,7},{7,6},{8,9},{9,8},{10,11... | collective-permute-start | bytes 983048 | tf_op jit(solution)/shard_map/ppermute | solution.py:306
  70.8 20.2 %all-to-all-start.2 = ((s16[16,80,128]{2,1,0:T(8,128)(2,1)}), s16[16,80,128]{2,1,0:T(8,128)(2,1)S(1)}, u32[]{:S(2)}, u32[]{:S(2)}) async-start(s16[16,80,128]{2,1,0:T(8,128)(2,1)} %mirror.2), calls=%async_computation.2 | async-start | bytes 655360 | tf_op jit(solution)/shard_map/all_to_all | solution.py:277
  78.9 12.1 %collective-permute-start.3 = (f32[64,128]{1,0:T(8,128)S(1)}, f32[64,128]{1,0:T(8,128)S(1)}, u32[]{:S(2)}, u32[]{:S(2)}) collective-permute-start(f32[64,128]{1,0:T(8,128)S(1)} %sum.2), channel_id=1, source_target_pairs={{28,0},{12,32},{31,64},{4,96},{7,128},{26,160},{25,192},{3,224},{0... | collective-permute-start | bytes 98312 | tf_op jit(solution)/shard_map/ppermute | solution.py:274
  92.4 18.6 %all-to-all-start.4 = ((s16[16,80,128]{2,1,0:T(8,128)(2,1)}), s16[16,80,128]{2,1,0:T(8,128)(2,1)S(1)}, u32[]{:S(2)}, u32[]{:S(2)}) async-start(s16[16,80,128]{2,1,0:T(8,128)(2,1)} %get-tuple-element.17), calls=%async_computation.4 | async-start | bytes 655360 | tf_op jit(solution)/shard_map/all_to_all | solution.py:277
  99.0 12.0 %collective-permute-start.4 = (s16[80,128]{1,0:T(8,128)(2,1)S(1)}, s16[80,128]{1,0:T(8,128)(2,1)S(1)}, u32[]{:S(2)}, u32[]{:S(2)}) collective-permute-start(s16[80,128]{1,0:T(8,128)(2,1)S(1)} %get-tuple-element.18), channel_id=1, source_target_pairs={{0,28},{32,12},{64,31},{96,4},{128,7},{160,26},{192,25},{224,3},{2... | collective-permute-start | bytes 61448 | tf_op jit(solution)/shard_map/ppermute | solution.py:274
  111.7 15.9 %all-to-all-start.5 = ((s16[16,80,128]{2,1,0:T(8,128)(2,1)}), s16[16,80,128]{2,1,0:T(8,128)(2,1)S(1)}, u32[]{:S(2)}, u32[]{:S(2)}) async-start(s16[16,80,128]{2,1,0:T(8,128)(2,1)} %copies.3), calls=%async_computation.5 | async-start | bytes 655360 | tf_op jit(solution)/shard_map/all_to_all | solution.py:280
  118.8 3.8 %collective-permute-start.6 = (f32[16,64,128]{2,1,0:T(8,128)S(1)}, f32[16,64,128]{2,1,0:T(8,128)S(1)}, u32[]{:S(2)}, u32[]{:S(2)}) collective-permute-start(f32[16,64,128]{2,1,0:T(8,128)S(1)} %get-tuple-element.20), channel_id=1, source_target_pairs={{0,1},{1,0},{2,3},{3,2},{4,5},{5,4},{6,7},{7,6},{8,9},{9,8},{10,11... | collective-permute-start | bytes 1572872 | tf_op jit(solution)/shard_map/ppermute | solution.py:303
  127.6 19.8 %all-to-all-start.7 = ((s16[16,80,128]{2,1,0:T(8,128)(2,1)}), s16[16,80,128]{2,1,0:T(8,128)(2,1)S(1)}, u32[]{:S(2)}, u32[]{:S(2)}) async-start(s16[16,80,128]{2,1,0:T(8,128)(2,1)} %join.3), calls=%async_computation.7 | async-start | bytes 655360 | tf_op jit(solution)/shard_map/all_to_all | solution.py:280
  133.2 3.5 %collective-permute-start.5 = (s16[16,80,128]{2,1,0:T(8,128)(2,1)S(1)}, s16[16,80,128]{2,1,0:T(8,128)(2,1)S(1)}, u32[]{:S(2)}, u32[]{:S(2)}) collective-permute-start(s16[16,80,128]{2,1,0:T(8,128)(2,1)S(1)} %all-to-all-done.5.own_ref), channel_id=1, source_target_pairs={{0,1},{1,0},{2,3},{3,2},{4,5},{5,4},{6,7},{7,6},{8,9},{9,8},{10,11... | collective-permute-start | bytes 983048 | tf_op jit(solution)/shard_map/ppermute | solution.py:306
  147.5 20.3 %all-to-all-start.6 = ((s16[16,80,128]{2,1,0:T(8,128)(2,1)}), s16[16,80,128]{2,1,0:T(8,128)(2,1)S(1)}, u32[]{:S(2)}, u32[]{:S(2)}) async-start(s16[16,80,128]{2,1,0:T(8,128)(2,1)} %mirror.3), calls=%async_computation.6 | async-start | bytes 655360 | tf_op jit(solution)/shard_map/all_to_all | solution.py:277
  155.7 12.1 %collective-permute-start.7 = (f32[64,128]{1,0:T(8,128)S(1)}, f32[64,128]{1,0:T(8,128)S(1)}, u32[]{:S(2)}, u32[]{:S(2)}) collective-permute-start(f32[64,128]{1,0:T(8,128)S(1)} %sum.3), channel_id=1, source_target_pairs={{28,0},{12,32},{31,64},{4,96},{7,128},{26,160},{25,192},{3,224},{0... | collective-permute-start | bytes 98312 | tf_op jit(solution)/shard_map/ppermute | solution.py:274

commit v3 on v2

--- a/solution.py
+++ b/solution.py
@@ -101,7 +101,7 @@
         acc[where, :] += part[:, :classes] + part[:, classes:]
         return carry
 
-    lax.fori_loop(0, tiles_ref.shape[0], body, 0, unroll=8)
+    lax.fori_loop(0, tiles_ref.shape[0], body, 0, unroll=16)
     core = lax.rem(lax.axis_index("bcol"), 2)
     for j in range(keep_ref.shape[0]):
         keep_ref[j] = acc[pl.ds(held_at(held_ref, 2 * j + core, rows), rows), :]
@@ -143,7 +143,7 @@
         acc[where, :] += part[:, :classes] + part[:, classes:]
         return carry
 
-    lax.fori_loop(0, tiles_ref.shape[0], body, 0, unroll=8)
+    lax.fori_loop(0, tiles_ref.shape[0], body, 0, unroll=16)
     for i in range(out_ref.shape[0]):
         code, head = encode(acc[i * rows : (i + 1) * rows, :])
         out_ref[i, :rows] = code
@@ -290,9 +290,9 @@
     copies, one = call(first_kernel, "first", (brow_pieces, piece), (initial,))
     for sweep in range(SWEEPS):
         col_got = over_brow(copies)
-        copies = call(
-            copies_kernel, "copies", bcol_pieces, (col_got, swap(one, pairs)), [ANYWHERE, WHOLE]
-        )
+        other = swap(one, pairs)
+        before = col_got if sweep == 0 else other
+        copies = call(copies_kernel, "copies", bcol_pieces, (before, other), [ANYWHERE, WHOLE])
         row_own = over_bcol(copies)
         keep, send = call(
             forward_kernel, "forward", (sums, sums), (slots, tile_count, held, col_got, stored),

time: 170 us -> 169 us (level)
  waiting for transfers between devices: 58.6 us -> 61.7 us
  Pallas kernels: 24 us -> 21 us
    all_to_all x4, waiting for transfers between devices: 0.01 us -> 5.17 us  [over_brow(): lax.all_to_all(value, 'brow', split_axis=0, concat_axis=0, tiled=True)]
    ppermute x4, waiting for transfers between devices: 33.9 us -> 28.8 us  [swap(): return lax.ppermute(value, ('brow', 'bcol'), way)]
    pallas_call x13, Pallas kernels: 24 us -> 21 us  [call(): pl.pallas_call(kernel, out_shape=outs, in_specs=specs or [WHOLE] * len(ar...]
    all_to_all x4, waiting for transfers between devices: 17.8 us -> 20.7 us  [over_bcol(): lax.all_to_all(value, 'bcol', split_axis=0, concat_axis=0, tiled=True, ax...]
  transfers between devices with their start and end apart: 16 -> 16, of which waited for: 12 -> 13; matrix products, arithmetic and copies ran while one was open for 0% -> 0% of each run, Pallas kernels for 11% -> 10%
where the time goes in v3:
time: 169 us; the launch traced here: 167 us
  starting transfers between devices  79.7 us (47%)
  waiting for transfers between devices  61.7 us (37%)
  Pallas kernels  21 us (12%)
  local copies, waits for them, and re-layouts  3.89 us (2%)
    all_to_all x4, starting transfers between devices, over_brow(): lax.all_to_all(value, 'brow', split_axis=0, concat_axis=0, tiled=True)  31.1 us
    ppermute x4, waiting for transfers between devices, swap(): return lax.ppermute(value, ('brow', 'bcol'), way)  28.8 us
    ppermute x4, starting transfers between devices, swap(): return lax.ppermute(value, ('brow', 'bcol'), way)  22.1 us
    pallas_call x13, Pallas kernels, call(): pl.pallas_call(kernel, out_shape=outs, in_specs=specs or [WHOLE] * len(ar...  21 us
    all_to_all x4, waiting for transfers between devices, over_bcol(): lax.all_to_all(value, 'bcol', split_axis=0, concat_axis=0, tiled=True, ax...  20.7 us
    all_to_all x4, starting transfers between devices, over_bcol(): lax.all_to_all(value, 'bcol', split_axis=0, concat_axis=0, tiled=True, ax...  18.8 us
    all_to_all x4, waiting for transfers between devices, over_brow(): lax.all_to_all(value, 'brow', split_axis=0, concat_axis=0, tiled=True)  5.17 us
    ppermute x2, starting transfers between devices, on_device(): got = lax.ppermute(send, 'bcol', exchange)  3.84 us
  transfers between devices with their start and end apart: 16, of which 13 were waited for; matrix products, arithmetic and copies ran while one was open for 0% of the time, Pallas kernels for 10%

profile of v3, /device:TPU:56, one launch (start us, length us, event | category | flops | bytes accessed | tf_op | source)
XLA Modules:
  0.0 167.1 jit_solution(16169977355472333100)
XLA Ops:
  1.8 8.7 %all-to-all-start = ((s16[16,80,128]{2,1,0:T(8,128)(2,1)}), s16[16,80,128]{2,1,0:T(8,128)(2,1)S(1)}, u32[]{:S(2)}, u32[]{:S(2)}) async-start(s16[16,80,128]{2,1,0:T(8,128)(2,1)} %get-tuple-element.13), calls=%async_computation | async-start | bytes 655360 | tf_op jit(solution)/shard_map/all_to_all | solution.py:277
  10.5 11.8 %collective-permute-start = (s16[80,128]{1,0:T(8,128)(2,1)S(1)}, s16[80,128]{1,0:T(8,128)(2,1)S(1)}, u32[]{:S(2)}, u32[]{:S(2)}) collective-permute-start(s16[80,128]{1,0:T(8,128)(2,1)S(1)} %get-tuple-element.14), channel_id=1, source_target_pairs={{0,28},{32,12},{64,31},{96,4},{128,7},{160,26},{192,25},{224,3},{2... | collective-permute-start | bytes 61448 | tf_op jit(solution)/shard_map/ppermute | solution.py:274
  22.3 8.1 %collective-permute-done.one_ref = s16[80,128]{1,0:T(8,128)(2,1)S(1)} collective-permute-done((s16[80,128]{1,0:T(8,128)(2,1)S(1)}, s16[80,128]{1,0:T(8,128)(2,1)S(1)}, u32[]{:S(2)}, u32[]{:S(2)}) %collective-permute-start) | collective-permute-done | bytes 20512 | tf_op jit(solution)/shard_map/ppermute | solution.py:274
  31.2 3.5 %all-to-all-start.1 = ((s16[16,80,128]{2,1,0:T(8,128)(2,1)}), s16[16,80,128]{2,1,0:T(8,128)(2,1)S(1)}, u32[]{:S(2)}, u32[]{:S(2)}) async-start(s16[16,80,128]{2,1,0:T(8,128)(2,1)} %copies.2), calls=%async_computation.1 | async-start | bytes 655360 | tf_op jit(solution)/shard_map/all_to_all | solution.py:280
  38.3 2.8 %forward.2 = (f32[16,64,128]{2,1,0:T(8,128)S(1)}, f32[16,64,128]{2,1,0:T(8,128)S(1)}) custom-call(s32[2,64]{1,0:T(2,128)S(1)} %bitcast.15, s32[1,1]{1,0:T(1,128)S(6)} %copy.8.count_ref, s32[16,32]{1,0:T(8,128)S(1)} %copy-done.4, s16[16,80,128]{2,1,0:T(8,128)(2,1)S(1)} %all-to-all-done.after_ref.got_ref, bf16[64,128,128]{2,1,0:T(8,128)(2,1)S(1)} %bitcast.8), custom_call_target="tpu_custom_call" | custom-call | tf_op jit(solution)/shard_map/forward/pallas_call | solution.py:239
  41.2 1.9 %collective-permute-start.2 = (f32[16,64,128]{2,1,0:T(8,128)S(1)}, f32[16,64,128]{2,1,0:T(8,128)S(1)}, u32[]{:S(2)}, u32[]{:S(2)}) collective-permute-start(f32[16,64,128]{2,1,0:T(8,128)S(1)} %get-tuple-element.16), channel_id=1, source_target_pairs={{0,1},{1,0},{2,3},{3,2},{4,5},{5,4},{6,7},{7,6},{8,9},{9,8},{10,11... | collective-permute-start | bytes 1572872 | tf_op jit(solution)/shard_map/ppermute | solution.py:303
  43.1 1.9 %collective-permute-done.2.got_ref = f32[16,64,128]{2,1,0:T(8,128)S(1)} collective-permute-done((f32[16,64,128]{2,1,0:T(8,128)S(1)}, f32[16,64,128]{2,1,0:T(8,128)S(1)}, u32[]{:S(2)}, u32[]{:S(2)}) %collective-permute-start.2) | collective-permute-done | bytes 524320 | tf_op jit(solution)/shard_map/ppermute | solution.py:303
  46.1 2.9 %all-to-all-done.1.own_ref = s16[16,80,128]{2,1,0:T(8,128)(2,1)S(1)} async-done(((s16[16,80,128]{2,1,0:T(8,128)(2,1)}), s16[16,80,128]{2,1,0:T(8,128)(2,1)S(1)}, u32[]{:S(2)}, u32[]{:S(2)}) %all-to-all-start.1) | async-done | bytes 327712 | tf_op jit(solution)/shard_map/all_to_all | solution.py:280
  48.9 6.8 %all-to-all-start.3 = ((s16[16,80,128]{2,1,0:T(8,128)(2,1)}), s16[16,80,128]{2,1,0:T(8,128)(2,1)S(1)}, u32[]{:S(2)}, u32[]{:S(2)}) async-start(s16[16,80,128]{2,1,0:T(8,128)(2,1)} %join.2), calls=%async_computation.3 | async-start | bytes 655360 | tf_op jit(solution)/shard_map/all_to_all | solution.py:280
  55.8 1.9 %collective-permute-start.1 = (s16[16,80,128]{2,1,0:T(8,128)(2,1)S(1)}, s16[16,80,128]{2,1,0:T(8,128)(2,1)S(1)}, u32[]{:S(2)}, u32[]{:S(2)}) collective-permute-start(s16[16,80,128]{2,1,0:T(8,128)(2,1)S(1)} %all-to-all-done.1.own_ref), channel_id=1, source_target_pairs={{0,1},{1,0},{2,3},{3,2},{4,5},{5,4},{6,7},{7,6},{8,9},{9,8},{10,11... | collective-permute-start | bytes 983048 | tf_op jit(solution)/shard_map/ppermute | solution.py:306
  57.7 1.6 collective-permute-done.1.other_ref
  59.3 4.1 %mirror.2 = s16[16,80,128]{2,1,0:T(8,128)(2,1)} custom-call(s32[2,64]{1,0:T(2,128)S(1)} %bitcast.16, s32[1,1]{1,0:T(1,128)S(6)} %copy.8.count_ref, s32[16,32]{1,0:T(8,128)S(1)} %copy-done.5, s16[16,80,128]{2,1,0:T(8,128)(2,1)S(1)} %all-to-all-done.1.own_ref, s16[16,80,128]{2,1,0:T(8,128)(2,1)S(1)} %collective-permute-done.1.other_ref, ...), custom_call_target="tpu_custom_call" | custom-call | tf_op jit(solution)/shard_map/mirror/pallas_call | solution.py:239
  63.5 6.6 %all-to-all-done.3.got_ref = s16[16,80,128]{2,1,0:T(8,128)(2,1)S(1)} async-done(((s16[16,80,128]{2,1,0:T(8,128)(2,1)}), s16[16,80,128]{2,1,0:T(8,128)(2,1)S(1)}, u32[]{:S(2)}, u32[]{:S(2)}) %all-to-all-start.3) | async-done | bytes 327712 | tf_op jit(solution)/shard_map/all_to_all | solution.py:280
  70.1 7.9 %all-to-all-start.2 = ((s16[16,80,128]{2,1,0:T(8,128)(2,1)}), s16[16,80,128]{2,1,0:T(8,128)(2,1)S(1)}, u32[]{:S(2)}, u32[]{:S(2)}) async-start(s16[16,80,128]{2,1,0:T(8,128)(2,1)} %mirror.2), calls=%async_computation.2 | async-start | bytes 655360 | tf_op jit(solution)/shard_map/all_to_all | solution.py:277
  78.2 4.5 %collective-permute-start.3 = (f32[64,128]{1,0:T(8,128)S(1)}, f32[64,128]{1,0:T(8,128)S(1)}, u32[]{:S(2)}, u32[]{:S(2)}) collective-permute-start(f32[64,128]{1,0:T(8,128)S(1)} %sum.2), channel_id=1, source_target_pairs={{28,0},{12,32},{31,64},{4,96},{7,128},{26,160},{25,192},{3,224},{0... | collective-permute-start | bytes 98312 | tf_op jit(solution)/shard_map/ppermute | solution.py:274
  82.6 7.7 %collective-permute-done.3.row_ref = f32[64,128]{1,0:T(8,128)S(1)} collective-permute-done((f32[64,128]{1,0:T(8,128)S(1)}, f32[64,128]{1,0:T(8,128)S(1)}, u32[]{:S(2)}, u32[]{:S(2)}) %collective-permute-start.3) | collective-permute-done | bytes 32800 | tf_op jit(solution)/shard_map/ppermute | solution.py:274
  91.7 6.6 %all-to-all-start.6 = ((s16[16,80,128]{2,1,0:T(8,128)(2,1)}), s16[16,80,128]{2,1,0:T(8,128)(2,1)S(1)}, u32[]{:S(2)}, u32[]{:S(2)}) async-start(s16[16,80,128]{2,1,0:T(8,128)(2,1)} %get-tuple-element.18), calls=%async_computation.6 | async-start | bytes 655360 | tf_op jit(solution)/shard_map/all_to_all | solution.py:277
  98.3 1.9 %collective-permute-start.4 = (s16[80,128]{1,0:T(8,128)(2,1)S(1)}, s16[80,128]{1,0:T(8,128)(2,1)S(1)}, u32[]{:S(2)}, u32[]{:S(2)}) collective-permute-start(s16[80,128]{1,0:T(8,128)(2,1)S(1)} %get-tuple-element.17), channel_id=1, source_target_pairs={{0,28},{32,12},{64,31},{96,4},{128,7},{160,26},{192,25},{224,3},{2... | collective-permute-start | bytes 61448 | tf_op jit(solution)/shard_map/ppermute | solution.py:274
  100.2 10.1 %collective-permute-done.4.after_ref.one_ref = s16[80,128]{1,0:T(8,128)(2,1)S(1)} collective-permute-done((s16[80,128]{1,0:T(8,128)(2,1)S(1)}, s16[80,128]{1,0:T(8,128)(2,1)S(1)}, u32[]{:S(2)}, u32[]{:S(2)}) %collective-permute-start.4) | collective-permute-done | bytes 20512 | tf_op jit(solution)/shard_map/ppermute | solution.py:274
  111.0 3.5 %all-to-all-start.4 = ((s16[16,80,128]{2,1,0:T(8,128)(2,1)}), s16[16,80,128]{2,1,0:T(8,128)(2,1)S(1)}, u32[]{:S(2)}, u32[]{:S(2)}) async-start(s16[16,80,128]{2,1,0:T(8,128)(2,1)} %copies.3), calls=%async_computation.4 | async-start | bytes 655360 | tf_op jit(solution)/shard_map/all_to_all | solution.py:280
  114.6 2.8 %forward.3 = (f32[16,64,128]{2,1,0:T(8,128)S(1)}, f32[16,64,128]{2,1,0:T(8,128)S(1)}) custom-call(s32[2,64]{1,0:T(2,128)S(1)} %bitcast.17, s32[1,1]{1,0:T(1,128)S(6)} %copy.8.count_ref, s32[16,32]{1,0:T(8,128)S(1)} %copy-done.5, s16[16,80,128]{2,1,0:T(8,128)(2,1)S(1)} %all-to-all-done.6.got_ref, bf16[64,128,128]{2,1,0:T(8,128)(2,1)S(1)} %bitcast.10), custom_call_target="tpu_custom_call" | custom-call | tf_op jit(solution)/shard_map/forward/pallas_call | solution.py:239
  117.4 1.9 %collective-permute-start.6 = (f32[16,64,128]{2,1,0:T(8,128)S(1)}, f32[16,64,128]{2,1,0:T(8,128)S(1)}, u32[]{:S(2)}, u32[]{:S(2)}) collective-permute-start(f32[16,64,128]{2,1,0:T(8,128)S(1)} %get-tuple-element.20), channel_id=1, source_target_pairs={{0,1},{1,0},{2,3},{3,2},{4,5},{5,4},{6,7},{7,6},{8,9},{9,8},{10,11... | collective-permute-start | bytes 1572872 | tf_op jit(solution)/shard_map/ppermute | solution.py:303
  119.3 1.9 %collective-permute-done.6.got_ref = f32[16,64,128]{2,1,0:T(8,128)S(1)} collective-permute-done((f32[16,64,128]{2,1,0:T(8,128)S(1)}, f32[16,64,128]{2,1,0:T(8,128)S(1)}, u32[]{:S(2)}, u32[]{:S(2)}) %collective-permute-start.6) | collective-permute-done | bytes 524320 | tf_op jit(solution)/shard_map/ppermute | solution.py:303
  122.3 4.6 %all-to-all-done.4.own_ref = s16[16,80,128]{2,1,0:T(8,128)(2,1)S(1)} async-done(((s16[16,80,128]{2,1,0:T(8,128)(2,1)}), s16[16,80,128]{2,1,0:T(8,128)(2,1)S(1)}, u32[]{:S(2)}, u32[]{:S(2)}) %all-to-all-start.4) | async-done | bytes 327712 | tf_op jit(solution)/shard_map/all_to_all | solution.py:280
  126.9 4.9 %all-to-all-start.7 = ((s16[16,80,128]{2,1,0:T(8,128)(2,1)}), s16[16,80,128]{2,1,0:T(8,128)(2,1)S(1)}, u32[]{:S(2)}, u32[]{:S(2)}) async-start(s16[16,80,128]{2,1,0:T(8,128)(2,1)} %join.3), calls=%async_computation.7 | async-start | bytes 655360 | tf_op jit(solution)/shard_map/all_to_all | solution.py:280
  131.9 1.9 %collective-permute-start.5 = (s16[16,80,128]{2,1,0:T(8,128)(2,1)S(1)}, s16[16,80,128]{2,1,0:T(8,128)(2,1)S(1)}, u32[]{:S(2)}, u32[]{:S(2)}) collective-permute-start(s16[16,80,128]{2,1,0:T(8,128)(2,1)S(1)} %all-to-all-done.4.own_ref), channel_id=1, source_target_pairs={{0,1},{1,0},{2,3},{3,2},{4,5},{5,4},{6,7},{7,6},{8,9},{9,8},{10,11... | collective-permute-start | bytes 983048 | tf_op jit(solution)/shard_map/ppermute | solution.py:306
  135.4 4.1 %mirror.3 = s16[16,80,128]{2,1,0:T(8,128)(2,1)} custom-call(s32[2,64]{1,0:T(2,128)S(1)} %bitcast.18, s32[1,1]{1,0:T(1,128)S(6)} %copy.8.count_ref, s32[16,32]{1,0:T(8,128)S(1)} %copy-done.5, s16[16,80,128]{2,1,0:T(8,128)(2,1)S(1)} %all-to-all-done.4.own_ref, s16[16,80,128]{2,1,0:T(8,128)(2,1)S(1)} %collective-permute-done.5.other_ref, ...), custom_call_target="tpu_custom_call" | custom-call | tf_op jit(solution)/shard_map/mirror/pallas_call | solution.py:239
  139.5 6.6 %all-to-all-done.7.got_ref = s16[16,80,128]{2,1,0:T(8,128)(2,1)S(1)} async-done(((s16[16,80,128]{2,1,0:T(8,128)(2,1)}), s16[16,80,128]{2,1,0:T(8,128)(2,1)S(1)}, u32[]{:S(2)}, u32[]{:S(2)}) %all-to-all-start.7) | async-done | bytes 327712 | tf_op jit(solution)/shard_map/all_to_all | solution.py:280
  146.1 7.9 %all-to-all-start.5 = ((s16[16,80,128]{2,1,0:T(8,128)(2,1)}), s16[16,80,128]{2,1,0:T(8,128)(2,1)S(1)}, u32[]{:S(2)}, u32[]{:S(2)}) async-start(s16[16,80,128]{2,1,0:T(8,128)(2,1)} %mirror.3), calls=%async_computation.5 | async-start | bytes 655360 | tf_op jit(solution)/shard_map/all_to_all | solution.py:277
  154.2 4.0 %collective-permute-start.7 = (f32[64,128]{1,0:T(8,128)S(1)}, f32[64,128]{1,0:T(8,128)S(1)}, u32[]{:S(2)}, u32[]{:S(2)}) collective-permute-start(f32[64,128]{1,0:T(8,128)S(1)} %sum.3), channel_id=1, source_target_pairs={{28,0},{12,32},{31,64},{4,96},{7,128},{26,160},{25,192},{3,224},{0... | collective-permute-start | bytes 98312 | tf_op jit(solution)/shard_map/ppermute | solution.py:274
  158.2 5.2 %all-to-all-done.5.got_ref = s16[16,80,128]{2,1,0:T(8,128)(2,1)S(1)} async-done(((s16[16,80,128]{2,1,0:T(8,128)(2,1)}), s16[16,80,128]{2,1,0:T(8,128)(2,1)S(1)}, u32[]{:S(2)}, u32[]{:S(2)}) %all-to-all-start.5) | async-done | bytes 327712 | tf_op jit(solution)/shard_map/all_to_all | solution.py:277
  163.3 3.0 %collective-permute-done.7.row_ref = f32[64,128]{1,0:T(8,128)S(1)} collective-permute-done((f32[64,128]{1,0:T(8,128)S(1)}, f32[64,128]{1,0:T(8,128)S(1)}, u32[]{:S(2)}, u32[]{:S(2)}) %collective-permute-start.7) | collective-permute-done | bytes 32800 | tf_op jit(solution)/shard_map/ppermute | solution.py:274
  (37 shorter events, 12.6 us)
Async XLA Ops:
  0.0 0.8 copy-start.2
  1.8 28.6 %all-to-all-start = ((s16[16,80,128]{2,1,0:T(8,128)(2,1)}), s16[16,80,128]{2,1,0:T(8,128)(2,1)S(1)}, u32[]{:S(2)}, u32[]{:S(2)}) async-start(s16[16,80,128]{2,1,0:T(8,128)(2,1)} %get-tuple-element.13), calls=%async_computation | async-start | bytes 655360 | tf_op jit(solution)/shard_map/all_to_all | solution.py:277
  10.5 19.9 %collective-permute-start = (s16[80,128]{1,0:T(8,128)(2,1)S(1)}, s16[80,128]{1,0:T(8,128)(2,1)S(1)}, u32[]{:S(2)}, u32[]{:S(2)}) collective-permute-start(s16[80,128]{1,0:T(8,128)(2,1)S(1)} %get-tuple-element.14), channel_id=1, source_target_pairs={{0,28},{32,12},{64,31},{96,4},{128,7},{160,26},{192,25},{224,3},{2... | collective-permute-start | bytes 61448 | tf_op jit(solution)/shard_map/ppermute | solution.py:274
  31.2 17.8 %all-to-all-start.1 = ((s16[16,80,128]{2,1,0:T(8,128)(2,1)}), s16[16,80,128]{2,1,0:T(8,128)(2,1)S(1)}, u32[]{:S(2)}, u32[]{:S(2)}) async-start(s16[16,80,128]{2,1,0:T(8,128)(2,1)} %copies.2), calls=%async_computation.1 | async-start | bytes 655360 | tf_op jit(solution)/shard_map/all_to_all | solution.py:280
  35.4 1.6 copy-start
  37.0 0.7 copy-start.4
  37.7 0.7 copy-start.6
  38.3 21.0 %copy-start.1 = (bf16[1,1,64,128,128]{4,3,2,1,0:T(8,128)(2,1)S(1)}, bf16[1,1,64,128,128]{4,3,2,1,0:T(8,128)(2,1)}, u32[]{:S(2)}) copy-start(bf16[1,1,64,128,128]{4,3,2,1,0:T(8,128)(2,1)} %param.10) | copy-start | bytes 6291460
  38.3 21.0 %copy-start.5 = (s32[16,32]{1,0:T(8,128)S(1)}, s32[16,32]{1,0:T(8,128)}, u32[]{:S(2)}) copy-start(s32[16,32]{1,0:T(8,128)} %constant.2.clone.held_ref) | copy-start | bytes 6148
  38.3 21.0 %copy-start.7 = (s32[1,1,2,64]{3,2,1,0:T(2,128)S(1)}, s32[1,1,2,64]{3,2,1,0:T(2,128)}, u32[]{:S(2)}) copy-start(s32[1,1,2,64]{3,2,1,0:T(2,128)} %param.11) | copy-start | bytes 1540
  41.2 3.8 %collective-permute-start.2 = (f32[16,64,128]{2,1,0:T(8,128)S(1)}, f32[16,64,128]{2,1,0:T(8,128)S(1)}, u32[]{:S(2)}, u32[]{:S(2)}) collective-permute-start(f32[16,64,128]{2,1,0:T(8,128)S(1)} %get-tuple-element.16), channel_id=1, source_target_pairs={{0,1},{1,0},{2,3},{3,2},{4,5},{5,4},{6,7},{7,6},{8,9},{9,8},{10,11... | collective-permute-start | bytes 1572872 | tf_op jit(solution)/shard_map/ppermute | solution.py:303
  46.1 31.9 %copy-start.8 = (s32[1,64]{1,0:T(1,128)S(1)}, s32[1,64]{1,0:T(1,128)}, u32[]{:S(2)}) copy-start(s32[1,64]{1,0:T(1,128)} %param.8) | copy-start | bytes 772
  48.9 21.1 %all-to-all-start.3 = ((s16[16,80,128]{2,1,0:T(8,128)(2,1)}), s16[16,80,128]{2,1,0:T(8,128)(2,1)S(1)}, u32[]{:S(2)}, u32[]{:S(2)}) async-start(s16[16,80,128]{2,1,0:T(8,128)(2,1)} %join.2), calls=%async_computation.3 | async-start | bytes 655360 | tf_op jit(solution)/shard_map/all_to_all | solution.py:280
  55.8 26.8 %copy-start.9 = (s32[1,64]{1,0:T(1,128)S(1)}, s32[1,64]{1,0:T(1,128)}, u32[]{:S(2)}) copy-start(s32[1,64]{1,0:T(1,128)} %param.9) | copy-start | bytes 772
  55.8 34.7 %copy-start.3 = (f32[1,64,128]{2,1,0:T(8,128)S(1)}, f32[1,64,128]{2,1,0:T(8,128)}, u32[]{:S(2)}) copy-start(f32[1,64,128]{2,1,0:T(8,128)} %param.7) | copy-start | bytes 98308
  55.8 3.5 %collective-permute-start.1 = (s16[16,80,128]{2,1,0:T(8,128)(2,1)S(1)}, s16[16,80,128]{2,1,0:T(8,128)(2,1)S(1)}, u32[]{:S(2)}, u32[]{:S(2)}) collective-permute-start(s16[16,80,128]{2,1,0:T(8,128)(2,1)S(1)} %all-to-all-done.1.own_ref), channel_id=1, source_target_pairs={{0,1},{1,0},{2,3},{3,2},{4,5},{5,4},{6,7},{7,6},{8,9},{9,8},{10,11... | collective-permute-start | bytes 983048 | tf_op jit(solution)/shard_map/ppermute | solution.py:306
  70.1 20.2 %all-to-all-start.2 = ((s16[16,80,128]{2,1,0:T(8,128)(2,1)}), s16[16,80,128]{2,1,0:T(8,128)(2,1)S(1)}, u32[]{:S(2)}, u32[]{:S(2)}) async-start(s16[16,80,128]{2,1,0:T(8,128)(2,1)} %mirror.2), calls=%async_computation.2 | async-start | bytes 655360 | tf_op jit(solution)/shard_map/all_to_all | solution.py:277
  78.2 12.1 %collective-permute-start.3 = (f32[64,128]{1,0:T(8,128)S(1)}, f32[64,128]{1,0:T(8,128)S(1)}, u32[]{:S(2)}, u32[]{:S(2)}) collective-permute-start(f32[64,128]{1,0:T(8,128)S(1)} %sum.2), channel_id=1, source_target_pairs={{28,0},{12,32},{31,64},{4,96},{7,128},{26,160},{25,192},{3,224},{0... | collective-permute-start | bytes 98312 | tf_op jit(solution)/shard_map/ppermute | solution.py:274
  91.7 19.4 %all-to-all-start.6 = ((s16[16,80,128]{2,1,0:T(8,128)(2,1)}), s16[16,80,128]{2,1,0:T(8,128)(2,1)S(1)}, u32[]{:S(2)}, u32[]{:S(2)}) async-start(s16[16,80,128]{2,1,0:T(8,128)(2,1)} %get-tuple-element.18), calls=%async_computation.6 | async-start | bytes 655360 | tf_op jit(solution)/shard_map/all_to_all | solution.py:277
  98.3 12.0 %collective-permute-start.4 = (s16[80,128]{1,0:T(8,128)(2,1)S(1)}, s16[80,128]{1,0:T(8,128)(2,1)S(1)}, u32[]{:S(2)}, u32[]{:S(2)}) collective-permute-start(s16[80,128]{1,0:T(8,128)(2,1)S(1)} %get-tuple-element.17), channel_id=1, source_target_pairs={{0,28},{32,12},{64,31},{96,4},{128,7},{160,26},{192,25},{224,3},{2... | collective-permute-start | bytes 61448 | tf_op jit(solution)/shard_map/ppermute | solution.py:274
  111.0 15.9 %all-to-all-start.4 = ((s16[16,80,128]{2,1,0:T(8,128)(2,1)}), s16[16,80,128]{2,1,0:T(8,128)(2,1)S(1)}, u32[]{:S(2)}, u32[]{:S(2)}) async-start(s16[16,80,128]{2,1,0:T(8,128)(2,1)} %copies.3), calls=%async_computation.4 | async-start | bytes 655360 | tf_op jit(solution)/shard_map/all_to_all | solution.py:280
  117.4 3.8 %collective-permute-start.6 = (f32[16,64,128]{2,1,0:T(8,128)S(1)}, f32[16,64,128]{2,1,0:T(8,128)S(1)}, u32[]{:S(2)}, u32[]{:S(2)}) collective-permute-start(f32[16,64,128]{2,1,0:T(8,128)S(1)} %get-tuple-element.20), channel_id=1, source_target_pairs={{0,1},{1,0},{2,3},{3,2},{4,5},{5,4},{6,7},{7,6},{8,9},{9,8},{10,11... | collective-permute-start | bytes 1572872 | tf_op jit(solution)/shard_map/ppermute | solution.py:303
  126.9 19.2 %all-to-all-start.7 = ((s16[16,80,128]{2,1,0:T(8,128)(2,1)}), s16[16,80,128]{2,1,0:T(8,128)(2,1)S(1)}, u32[]{:S(2)}, u32[]{:S(2)}) async-start(s16[16,80,128]{2,1,0:T(8,128)(2,1)} %join.3), calls=%async_computation.7 | async-start | bytes 655360 | tf_op jit(solution)/shard_map/all_to_all | solution.py:280
  131.9 3.5 %collective-permute-start.5 = (s16[16,80,128]{2,1,0:T(8,128)(2,1)S(1)}, s16[16,80,128]{2,1,0:T(8,128)(2,1)S(1)}, u32[]{:S(2)}, u32[]{:S(2)}) collective-permute-start(s16[16,80,128]{2,1,0:T(8,128)(2,1)S(1)} %all-to-all-done.4.own_ref), channel_id=1, source_target_pairs={{0,1},{1,0},{2,3},{3,2},{4,5},{5,4},{6,7},{7,6},{8,9},{9,8},{10,11... | collective-permute-start | bytes 983048 | tf_op jit(solution)/shard_map/ppermute | solution.py:306
  146.1 17.2 %all-to-all-start.5 = ((s16[16,80,128]{2,1,0:T(8,128)(2,1)}), s16[16,80,128]{2,1,0:T(8,128)(2,1)S(1)}, u32[]{:S(2)}, u32[]{:S(2)}) async-start(s16[16,80,128]{2,1,0:T(8,128)(2,1)} %mirror.3), calls=%async_computation.5 | async-start | bytes 655360 | tf_op jit(solution)/shard_map/all_to_all | solution.py:277
  154.2 12.1 %collective-permute-start.7 = (f32[64,128]{1,0:T(8,128)S(1)}, f32[64,128]{1,0:T(8,128)S(1)}, u32[]{:S(2)}, u32[]{:S(2)}) collective-permute-start(f32[64,128]{1,0:T(8,128)S(1)} %sum.3), channel_id=1, source_target_pairs={{28,0},{12,32},{31,64},{4,96},{7,128},{26,160},{25,192},{3,224},{0... | collective-permute-start | bytes 98312 | tf_op jit(solution)/shard_map/ppermute | solution.py:274

commit v4 on v3

--- a/solution.py
+++ b/solution.py
@@ -101,7 +101,7 @@
         acc[where, :] += part[:, :classes] + part[:, classes:]
         return carry
 
-    lax.fori_loop(0, tiles_ref.shape[0], body, 0, unroll=16)
+    lax.fori_loop(0, tiles_ref.shape[0], body, 0, unroll=64)
     core = lax.rem(lax.axis_index("bcol"), 2)
     for j in range(keep_ref.shape[0]):
         keep_ref[j] = acc[pl.ds(held_at(held_ref, 2 * j + core, rows), rows), :]
@@ -143,7 +143,7 @@
         acc[where, :] += part[:, :classes] + part[:, classes:]
         return carry
 
-    lax.fori_loop(0, tiles_ref.shape[0], body, 0, unroll=16)
+    lax.fori_loop(0, tiles_ref.shape[0], body, 0, unroll=64)
     for i in range(out_ref.shape[0]):
         code, head = encode(acc[i * rows : (i + 1) * rows, :])
         out_ref[i, :rows] = code

time: 169 us -> 168 us (level)
  Pallas kernels: 21 us -> 18.5 us
  waiting for transfers between devices: 61.7 us -> 64 us
    all_to_all x4, waiting for transfers between devices: 20.7 us -> 23.3 us  [over_bcol(): lax.all_to_all(value, 'bcol', split_axis=0, concat_axis=0, tiled=True, ax...]
    pallas_call x13, Pallas kernels: 21 us -> 18.5 us  [call(): pl.pallas_call(kernel, out_shape=outs, in_specs=specs or [WHOLE] * len(ar...]
  transfers between devices with their start and end apart: 16 -> 16, of which waited for: 13 -> 13; matrix products, arithmetic and copies ran while one was open for 0% -> 0% of each run, Pallas kernels for 10% -> 9%
where the time goes in v4:
time: 168 us; the launch traced here: 166 us
  starting transfers between devices  79.2 us (47%)
  waiting for transfers between devices  64 us (38%)
  Pallas kernels  18.5 us (11%)
  local copies, waits for them, and re-layouts  3.89 us (2%)
    all_to_all x4, starting transfers between devices, over_brow(): lax.all_to_all(value, 'brow', split_axis=0, concat_axis=0, tiled=True)  31.4 us
    ppermute x4, waiting for transfers between devices, swap(): return lax.ppermute(value, ('brow', 'bcol'), way)  28.8 us
    all_to_all x4, waiting for transfers between devices, over_bcol(): lax.all_to_all(value, 'bcol', split_axis=0, concat_axis=0, tiled=True, ax...  23.3 us
    ppermute x4, starting transfers between devices, swap(): return lax.ppermute(value, ('brow', 'bcol'), way)  22.3 us
    pallas_call x13, Pallas kernels, call(): pl.pallas_call(kernel, out_shape=outs, in_specs=specs or [WHOLE] * len(ar...  18.5 us
    all_to_all x4, starting transfers between devices, over_bcol(): lax.all_to_all(value, 'bcol', split_axis=0, concat_axis=0, tiled=True, ax...  17.7 us
    all_to_all x4, waiting for transfers between devices, over_brow(): lax.all_to_all(value, 'brow', split_axis=0, concat_axis=0, tiled=True)  5 us
    ppermute x2, starting transfers between devices, on_device(): got = lax.ppermute(send, 'bcol', exchange)  3.84 us
  transfers between devices with their start and end apart: 16, of which 13 were waited for; matrix products, arithmetic and copies ran while one was open for 0% of the time, Pallas kernels for 9%

profile of v4, /device:TPU:56, one launch (start us, length us, event | category | flops | bytes accessed | tf_op | source)
XLA Modules:
  0.0 166.4 jit_solution(5526596296858587746)
XLA Ops:
  1.8 8.7 %all-to-all-start = ((s16[16,80,128]{2,1,0:T(8,128)(2,1)}), s16[16,80,128]{2,1,0:T(8,128)(2,1)S(1)}, u32[]{:S(2)}, u32[]{:S(2)}) async-start(s16[16,80,128]{2,1,0:T(8,128)(2,1)} %get-tuple-element.13), calls=%async_computation | async-start | bytes 655360 | tf_op jit(solution)/shard_map/all_to_all | solution.py:277
  10.5 11.8 %collective-permute-start = (s16[80,128]{1,0:T(8,128)(2,1)S(1)}, s16[80,128]{1,0:T(8,128)(2,1)S(1)}, u32[]{:S(2)}, u32[]{:S(2)}) collective-permute-start(s16[80,128]{1,0:T(8,128)(2,1)S(1)} %get-tuple-element.14), channel_id=1, source_target_pairs={{0,28},{32,12},{64,31},{96,4},{128,7},{160,26},{192,25},{224,3},{2... | collective-permute-start | bytes 61448 | tf_op jit(solution)/shard_map/ppermute | solution.py:274
  22.3 8.1 %collective-permute-done.one_ref = s16[80,128]{1,0:T(8,128)(2,1)S(1)} collective-permute-done((s16[80,128]{1,0:T(8,128)(2,1)S(1)}, s16[80,128]{1,0:T(8,128)(2,1)S(1)}, u32[]{:S(2)}, u32[]{:S(2)}) %collective-permute-start) | collective-permute-done | bytes 20512 | tf_op jit(solution)/shard_map/ppermute | solution.py:274
  31.2 3.5 %all-to-all-start.1 = ((s16[16,80,128]{2,1,0:T(8,128)(2,1)}), s16[16,80,128]{2,1,0:T(8,128)(2,1)S(1)}, u32[]{:S(2)}, u32[]{:S(2)}) async-start(s16[16,80,128]{2,1,0:T(8,128)(2,1)} %copies.2), calls=%async_computation.1 | async-start | bytes 655360 | tf_op jit(solution)/shard_map/all_to_all | solution.py:280
  38.3 2.3 %forward.2 = (f32[16,64,128]{2,1,0:T(8,128)S(1)}, f32[16,64,128]{2,1,0:T(8,128)S(1)}) custom-call(s32[2,64]{1,0:T(2,128)S(1)} %bitcast.15, s32[1,1]{1,0:T(1,128)S(6)} %copy.8.count_ref, s32[16,32]{1,0:T(8,128)S(1)} %copy-done.4, s16[16,80,128]{2,1,0:T(8,128)(2,1)S(1)} %all-to-all-done.after_ref.got_ref, bf16[64,128,128]{2,1,0:T(8,128)(2,1)S(1)} %bitcast.8), custom_call_target="tpu_custom_call" | custom-call | tf_op jit(solution)/shard_map/forward/pallas_call | solution.py:239
  40.6 1.9 %collective-permute-start.2 = (f32[16,64,128]{2,1,0:T(8,128)S(1)}, f32[16,64,128]{2,1,0:T(8,128)S(1)}, u32[]{:S(2)}, u32[]{:S(2)}) collective-permute-start(f32[16,64,128]{2,1,0:T(8,128)S(1)} %get-tuple-element.16), channel_id=1, source_target_pairs={{0,1},{1,0},{2,3},{3,2},{4,5},{5,4},{6,7},{7,6},{8,9},{9,8},{10,11... | collective-permute-start | bytes 1572872 | tf_op jit(solution)/shard_map/ppermute | solution.py:303
  42.5 1.9 %collective-permute-done.2.got_ref = f32[16,64,128]{2,1,0:T(8,128)S(1)} collective-permute-done((f32[16,64,128]{2,1,0:T(8,128)S(1)}, f32[16,64,128]{2,1,0:T(8,128)S(1)}, u32[]{:S(2)}, u32[]{:S(2)}) %collective-permute-start.2) | collective-permute-done | bytes 524320 | tf_op jit(solution)/shard_map/ppermute | solution.py:303
  45.5 3.4 %all-to-all-done.1.own_ref = s16[16,80,128]{2,1,0:T(8,128)(2,1)S(1)} async-done(((s16[16,80,128]{2,1,0:T(8,128)(2,1)}), s16[16,80,128]{2,1,0:T(8,128)(2,1)S(1)}, u32[]{:S(2)}, u32[]{:S(2)}) %all-to-all-start.1) | async-done | bytes 327712 | tf_op jit(solution)/shard_map/all_to_all | solution.py:280
  48.9 6.3 %all-to-all-start.3 = ((s16[16,80,128]{2,1,0:T(8,128)(2,1)}), s16[16,80,128]{2,1,0:T(8,128)(2,1)S(1)}, u32[]{:S(2)}, u32[]{:S(2)}) async-start(s16[16,80,128]{2,1,0:T(8,128)(2,1)} %join.2), calls=%async_computation.3 | async-start | bytes 655360 | tf_op jit(solution)/shard_map/all_to_all | solution.py:280
  55.2 1.9 %collective-permute-start.1 = (s16[16,80,128]{2,1,0:T(8,128)(2,1)S(1)}, s16[16,80,128]{2,1,0:T(8,128)(2,1)S(1)}, u32[]{:S(2)}, u32[]{:S(2)}) collective-permute-start(s16[16,80,128]{2,1,0:T(8,128)(2,1)S(1)} %all-to-all-done.1.own_ref), channel_id=1, source_target_pairs={{0,1},{1,0},{2,3},{3,2},{4,5},{5,4},{6,7},{7,6},{8,9},{9,8},{10,11... | collective-permute-start | bytes 983048 | tf_op jit(solution)/shard_map/ppermute | solution.py:306
  57.2 1.6 collective-permute-done.1.other_ref
  58.8 3.5 %mirror.2 = s16[16,80,128]{2,1,0:T(8,128)(2,1)} custom-call(s32[2,64]{1,0:T(2,128)S(1)} %bitcast.16, s32[1,1]{1,0:T(1,128)S(6)} %copy.8.count_ref, s32[16,32]{1,0:T(8,128)S(1)} %copy-done.5, s16[16,80,128]{2,1,0:T(8,128)(2,1)S(1)} %all-to-all-done.1.own_ref, s16[16,80,128]{2,1,0:T(8,128)(2,1)S(1)} %collective-permute-done.1.other_ref, ...), custom_call_target="tpu_custom_call" | custom-call | tf_op jit(solution)/shard_map/mirror/pallas_call | solution.py:239
  62.2 7.3 %all-to-all-done.3.got_ref = s16[16,80,128]{2,1,0:T(8,128)(2,1)S(1)} async-done(((s16[16,80,128]{2,1,0:T(8,128)(2,1)}), s16[16,80,128]{2,1,0:T(8,128)(2,1)S(1)}, u32[]{:S(2)}, u32[]{:S(2)}) %all-to-all-start.3) | async-done | bytes 327712 | tf_op jit(solution)/shard_map/all_to_all | solution.py:280
  69.5 7.9 %all-to-all-start.2 = ((s16[16,80,128]{2,1,0:T(8,128)(2,1)}), s16[16,80,128]{2,1,0:T(8,128)(2,1)S(1)}, u32[]{:S(2)}, u32[]{:S(2)}) async-start(s16[16,80,128]{2,1,0:T(8,128)(2,1)} %mirror.2), calls=%async_computation.2 | async-start | bytes 655360 | tf_op jit(solution)/shard_map/all_to_all | solution.py:277
  77.6 4.5 %collective-permute-start.3 = (f32[64,128]{1,0:T(8,128)S(1)}, f32[64,128]{1,0:T(8,128)S(1)}, u32[]{:S(2)}, u32[]{:S(2)}) collective-permute-start(f32[64,128]{1,0:T(8,128)S(1)} %sum.2), channel_id=1, source_target_pairs={{28,0},{12,32},{31,64},{4,96},{7,128},{26,160},{25,192},{3,224},{0... | collective-permute-start | bytes 98312 | tf_op jit(solution)/shard_map/ppermute | solution.py:274
  82.1 7.7 %collective-permute-done.3.row_ref = f32[64,128]{1,0:T(8,128)S(1)} collective-permute-done((f32[64,128]{1,0:T(8,128)S(1)}, f32[64,128]{1,0:T(8,128)S(1)}, u32[]{:S(2)}, u32[]{:S(2)}) %collective-permute-start.3) | collective-permute-done | bytes 32800 | tf_op jit(solution)/shard_map/ppermute | solution.py:274
  91.1 6.6 %all-to-all-start.6 = ((s16[16,80,128]{2,1,0:T(8,128)(2,1)}), s16[16,80,128]{2,1,0:T(8,128)(2,1)S(1)}, u32[]{:S(2)}, u32[]{:S(2)}) async-start(s16[16,80,128]{2,1,0:T(8,128)(2,1)} %get-tuple-element.18), calls=%async_computation.6 | async-start | bytes 655360 | tf_op jit(solution)/shard_map/all_to_all | solution.py:277
  97.7 1.9 %collective-permute-start.4 = (s16[80,128]{1,0:T(8,128)(2,1)S(1)}, s16[80,128]{1,0:T(8,128)(2,1)S(1)}, u32[]{:S(2)}, u32[]{:S(2)}) collective-permute-start(s16[80,128]{1,0:T(8,128)(2,1)S(1)} %get-tuple-element.17), channel_id=1, source_target_pairs={{0,28},{32,12},{64,31},{96,4},{128,7},{160,26},{192,25},{224,3},{2... | collective-permute-start | bytes 61448 | tf_op jit(solution)/shard_map/ppermute | solution.py:274
  99.6 10.1 %collective-permute-done.4.after_ref.one_ref = s16[80,128]{1,0:T(8,128)(2,1)S(1)} collective-permute-done((s16[80,128]{1,0:T(8,128)(2,1)S(1)}, s16[80,128]{1,0:T(8,128)(2,1)S(1)}, u32[]{:S(2)}, u32[]{:S(2)}) %collective-permute-start.4) | collective-permute-done | bytes 20512 | tf_op jit(solution)/shard_map/ppermute | solution.py:274
  110.5 3.5 %all-to-all-start.4 = ((s16[16,80,128]{2,1,0:T(8,128)(2,1)}), s16[16,80,128]{2,1,0:T(8,128)(2,1)S(1)}, u32[]{:S(2)}, u32[]{:S(2)}) async-start(s16[16,80,128]{2,1,0:T(8,128)(2,1)} %copies.3), calls=%async_computation.4 | async-start | bytes 655360 | tf_op jit(solution)/shard_map/all_to_all | solution.py:280
  114.0 2.2 %forward.3 = (f32[16,64,128]{2,1,0:T(8,128)S(1)}, f32[16,64,128]{2,1,0:T(8,128)S(1)}) custom-call(s32[2,64]{1,0:T(2,128)S(1)} %bitcast.17, s32[1,1]{1,0:T(1,128)S(6)} %copy.8.count_ref, s32[16,32]{1,0:T(8,128)S(1)} %copy-done.5, s16[16,80,128]{2,1,0:T(8,128)(2,1)S(1)} %all-to-all-done.6.got_ref, bf16[64,128,128]{2,1,0:T(8,128)(2,1)S(1)} %bitcast.10), custom_call_target="tpu_custom_call" | custom-call | tf_op jit(solution)/shard_map/forward/pallas_call | solution.py:239
  116.3 1.9 %collective-permute-start.6 = (f32[16,64,128]{2,1,0:T(8,128)S(1)}, f32[16,64,128]{2,1,0:T(8,128)S(1)}, u32[]{:S(2)}, u32[]{:S(2)}) collective-permute-start(f32[16,64,128]{2,1,0:T(8,128)S(1)} %get-tuple-element.20), channel_id=1, source_target_pairs={{0,1},{1,0},{2,3},{3,2},{4,5},{5,4},{6,7},{7,6},{8,9},{9,8},{10,11... | collective-permute-start | bytes 1572872 | tf_op jit(solution)/shard_map/ppermute | solution.py:303
  118.2 1.9 %collective-permute-done.6.got_ref = f32[16,64,128]{2,1,0:T(8,128)S(1)} collective-permute-done((f32[16,64,128]{2,1,0:T(8,128)S(1)}, f32[16,64,128]{2,1,0:T(8,128)S(1)}, u32[]{:S(2)}, u32[]{:S(2)}) %collective-permute-start.6) | collective-permute-done | bytes 524320 | tf_op jit(solution)/shard_map/ppermute | solution.py:303
  121.2 5.2 %all-to-all-done.4.own_ref = s16[16,80,128]{2,1,0:T(8,128)(2,1)S(1)} async-done(((s16[16,80,128]{2,1,0:T(8,128)(2,1)}), s16[16,80,128]{2,1,0:T(8,128)(2,1)S(1)}, u32[]{:S(2)}, u32[]{:S(2)}) %all-to-all-start.4) | async-done | bytes 327712 | tf_op jit(solution)/shard_map/all_to_all | solution.py:280
  126.4 4.4 %all-to-all-start.7 = ((s16[16,80,128]{2,1,0:T(8,128)(2,1)}), s16[16,80,128]{2,1,0:T(8,128)(2,1)S(1)}, u32[]{:S(2)}, u32[]{:S(2)}) async-start(s16[16,80,128]{2,1,0:T(8,128)(2,1)} %join.3), calls=%async_computation.7 | async-start | bytes 655360 | tf_op jit(solution)/shard_map/all_to_all | solution.py:280
  130.7 1.9 %collective-permute-start.5 = (s16[16,80,128]{2,1,0:T(8,128)(2,1)S(1)}, s16[16,80,128]{2,1,0:T(8,128)(2,1)S(1)}, u32[]{:S(2)}, u32[]{:S(2)}) collective-permute-start(s16[16,80,128]{2,1,0:T(8,128)(2,1)S(1)} %all-to-all-done.4.own_ref), channel_id=1, source_target_pairs={{0,1},{1,0},{2,3},{3,2},{4,5},{5,4},{6,7},{7,6},{8,9},{9,8},{10,11... | collective-permute-start | bytes 983048 | tf_op jit(solution)/shard_map/ppermute | solution.py:306
  134.3 3.5 %mirror.3 = s16[16,80,128]{2,1,0:T(8,128)(2,1)} custom-call(s32[2,64]{1,0:T(2,128)S(1)} %bitcast.18, s32[1,1]{1,0:T(1,128)S(6)} %copy.8.count_ref, s32[16,32]{1,0:T(8,128)S(1)} %copy-done.5, s16[16,80,128]{2,1,0:T(8,128)(2,1)S(1)} %all-to-all-done.4.own_ref, s16[16,80,128]{2,1,0:T(8,128)(2,1)S(1)} %collective-permute-done.5.other_ref, ...), custom_call_target="tpu_custom_call" | custom-call | tf_op jit(solution)/shard_map/mirror/pallas_call | solution.py:239
  137.7 7.4 %all-to-all-done.7.got_ref = s16[16,80,128]{2,1,0:T(8,128)(2,1)S(1)} async-done(((s16[16,80,128]{2,1,0:T(8,128)(2,1)}), s16[16,80,128]{2,1,0:T(8,128)(2,1)S(1)}, u32[]{:S(2)}, u32[]{:S(2)}) %all-to-all-start.7) | async-done | bytes 327712 | tf_op jit(solution)/shard_map/all_to_all | solution.py:280
  145.1 8.2 %all-to-all-start.5 = ((s16[16,80,128]{2,1,0:T(8,128)(2,1)}), s16[16,80,128]{2,1,0:T(8,128)(2,1)S(1)}, u32[]{:S(2)}, u32[]{:S(2)}) async-start(s16[16,80,128]{2,1,0:T(8,128)(2,1)} %mirror.3), calls=%async_computation.5 | async-start | bytes 655360 | tf_op jit(solution)/shard_map/all_to_all | solution.py:277
  153.5 4.2 %collective-permute-start.7 = (f32[64,128]{1,0:T(8,128)S(1)}, f32[64,128]{1,0:T(8,128)S(1)}, u32[]{:S(2)}, u32[]{:S(2)}) collective-permute-start(f32[64,128]{1,0:T(8,128)S(1)} %sum.3), channel_id=1, source_target_pairs={{28,0},{12,32},{31,64},{4,96},{7,128},{26,160},{25,192},{3,224},{0... | collective-permute-start | bytes 98312 | tf_op jit(solution)/shard_map/ppermute | solution.py:274
  157.7 5.0 %all-to-all-done.5.got_ref = s16[16,80,128]{2,1,0:T(8,128)(2,1)S(1)} async-done(((s16[16,80,128]{2,1,0:T(8,128)(2,1)}), s16[16,80,128]{2,1,0:T(8,128)(2,1)S(1)}, u32[]{:S(2)}, u32[]{:S(2)}) %all-to-all-start.5) | async-done | bytes 327712 | tf_op jit(solution)/shard_map/all_to_all | solution.py:277
  162.7 2.9 %collective-permute-done.7.row_ref = f32[64,128]{1,0:T(8,128)S(1)} collective-permute-done((f32[64,128]{1,0:T(8,128)S(1)}, f32[64,128]{1,0:T(8,128)S(1)}, u32[]{:S(2)}, u32[]{:S(2)}) %collective-permute-start.7) | collective-permute-done | bytes 32800 | tf_op jit(solution)/shard_map/ppermute | solution.py:274
  (37 shorter events, 12.6 us)
Async XLA Ops:
  0.0 0.8 copy-start.2
  1.8 28.6 %all-to-all-start = ((s16[16,80,128]{2,1,0:T(8,128)(2,1)}), s16[16,80,128]{2,1,0:T(8,128)(2,1)S(1)}, u32[]{:S(2)}, u32[]{:S(2)}) async-start(s16[16,80,128]{2,1,0:T(8,128)(2,1)} %get-tuple-element.13), calls=%async_computation | async-start | bytes 655360 | tf_op jit(solution)/shard_map/all_to_all | solution.py:277
  10.5 19.9 %collective-permute-start = (s16[80,128]{1,0:T(8,128)(2,1)S(1)}, s16[80,128]{1,0:T(8,128)(2,1)S(1)}, u32[]{:S(2)}, u32[]{:S(2)}) collective-permute-start(s16[80,128]{1,0:T(8,128)(2,1)S(1)} %get-tuple-element.14), channel_id=1, source_target_pairs={{0,28},{32,12},{64,31},{96,4},{128,7},{160,26},{192,25},{224,3},{2... | collective-permute-start | bytes 61448 | tf_op jit(solution)/shard_map/ppermute | solution.py:274
  31.2 17.8 %all-to-all-start.1 = ((s16[16,80,128]{2,1,0:T(8,128)(2,1)}), s16[16,80,128]{2,1,0:T(8,128)(2,1)S(1)}, u32[]{:S(2)}, u32[]{:S(2)}) async-start(s16[16,80,128]{2,1,0:T(8,128)(2,1)} %copies.2), calls=%async_computation.1 | async-start | bytes 655360 | tf_op jit(solution)/shard_map/all_to_all | solution.py:280
  35.4 1.6 copy-start
  37.0 0.7 copy-start.4
  37.7 0.7 copy-start.6
  38.3 20.4 %copy-start.1 = (bf16[1,1,64,128,128]{4,3,2,1,0:T(8,128)(2,1)S(1)}, bf16[1,1,64,128,128]{4,3,2,1,0:T(8,128)(2,1)}, u32[]{:S(2)}) copy-start(bf16[1,1,64,128,128]{4,3,2,1,0:T(8,128)(2,1)} %param.10) | copy-start | bytes 6291460
  38.3 20.4 %copy-start.5 = (s32[16,32]{1,0:T(8,128)S(1)}, s32[16,32]{1,0:T(8,128)}, u32[]{:S(2)}) copy-start(s32[16,32]{1,0:T(8,128)} %constant.2.clone.held_ref) | copy-start | bytes 6148
  38.3 20.4 %copy-start.7 = (s32[1,1,2,64]{3,2,1,0:T(2,128)S(1)}, s32[1,1,2,64]{3,2,1,0:T(2,128)}, u32[]{:S(2)}) copy-start(s32[1,1,2,64]{3,2,1,0:T(2,128)} %param.11) | copy-start | bytes 1540
  40.6 3.8 %collective-permute-start.2 = (f32[16,64,128]{2,1,0:T(8,128)S(1)}, f32[16,64,128]{2,1,0:T(8,128)S(1)}, u32[]{:S(2)}, u32[]{:S(2)}) collective-permute-start(f32[16,64,128]{2,1,0:T(8,128)S(1)} %get-tuple-element.16), channel_id=1, source_target_pairs={{0,1},{1,0},{2,3},{3,2},{4,5},{5,4},{6,7},{7,6},{8,9},{9,8},{10,11... | collective-permute-start | bytes 1572872 | tf_op jit(solution)/shard_map/ppermute | solution.py:303
  45.5 31.9 %copy-start.8 = (s32[1,64]{1,0:T(1,128)S(1)}, s32[1,64]{1,0:T(1,128)}, u32[]{:S(2)}) copy-start(s32[1,64]{1,0:T(1,128)} %param.8) | copy-start | bytes 772
  48.9 20.6 %all-to-all-start.3 = ((s16[16,80,128]{2,1,0:T(8,128)(2,1)}), s16[16,80,128]{2,1,0:T(8,128)(2,1)S(1)}, u32[]{:S(2)}, u32[]{:S(2)}) async-start(s16[16,80,128]{2,1,0:T(8,128)(2,1)} %join.2), calls=%async_computation.3 | async-start | bytes 655360 | tf_op jit(solution)/shard_map/all_to_all | solution.py:280
  55.2 26.8 %copy-start.9 = (s32[1,64]{1,0:T(1,128)S(1)}, s32[1,64]{1,0:T(1,128)}, u32[]{:S(2)}) copy-start(s32[1,64]{1,0:T(1,128)} %param.9) | copy-start | bytes 772
  55.2 34.7 %copy-start.3 = (f32[1,64,128]{2,1,0:T(8,128)S(1)}, f32[1,64,128]{2,1,0:T(8,128)}, u32[]{:S(2)}) copy-start(f32[1,64,128]{2,1,0:T(8,128)} %param.7) | copy-start | bytes 98308
  55.2 3.5 %collective-permute-start.1 = (s16[16,80,128]{2,1,0:T(8,128)(2,1)S(1)}, s16[16,80,128]{2,1,0:T(8,128)(2,1)S(1)}, u32[]{:S(2)}, u32[]{:S(2)}) collective-permute-start(s16[16,80,128]{2,1,0:T(8,128)(2,1)S(1)} %all-to-all-done.1.own_ref), channel_id=1, source_target_pairs={{0,1},{1,0},{2,3},{3,2},{4,5},{5,4},{6,7},{7,6},{8,9},{9,8},{10,11... | collective-permute-start | bytes 983048 | tf_op jit(solution)/shard_map/ppermute | solution.py:306
  69.5 20.2 %all-to-all-start.2 = ((s16[16,80,128]{2,1,0:T(8,128)(2,1)}), s16[16,80,128]{2,1,0:T(8,128)(2,1)S(1)}, u32[]{:S(2)}, u32[]{:S(2)}) async-start(s16[16,80,128]{2,1,0:T(8,128)(2,1)} %mirror.2), calls=%async_computation.2 | async-start | bytes 655360 | tf_op jit(solution)/shard_map/all_to_all | solution.py:277
  77.6 12.1 %collective-permute-start.3 = (f32[64,128]{1,0:T(8,128)S(1)}, f32[64,128]{1,0:T(8,128)S(1)}, u32[]{:S(2)}, u32[]{:S(2)}) collective-permute-start(f32[64,128]{1,0:T(8,128)S(1)} %sum.2), channel_id=1, source_target_pairs={{28,0},{12,32},{31,64},{4,96},{7,128},{26,160},{25,192},{3,224},{0... | collective-permute-start | bytes 98312 | tf_op jit(solution)/shard_map/ppermute | solution.py:274
  91.1 19.4 %all-to-all-start.6 = ((s16[16,80,128]{2,1,0:T(8,128)(2,1)}), s16[16,80,128]{2,1,0:T(8,128)(2,1)S(1)}, u32[]{:S(2)}, u32[]{:S(2)}) async-start(s16[16,80,128]{2,1,0:T(8,128)(2,1)} %get-tuple-element.18), calls=%async_computation.6 | async-start | bytes 655360 | tf_op jit(solution)/shard_map/all_to_all | solution.py:277
  97.7 12.0 %collective-permute-start.4 = (s16[80,128]{1,0:T(8,128)(2,1)S(1)}, s16[80,128]{1,0:T(8,128)(2,1)S(1)}, u32[]{:S(2)}, u32[]{:S(2)}) collective-permute-start(s16[80,128]{1,0:T(8,128)(2,1)S(1)} %get-tuple-element.17), channel_id=1, source_target_pairs={{0,28},{32,12},{64,31},{96,4},{128,7},{160,26},{192,25},{224,3},{2... | collective-permute-start | bytes 61448 | tf_op jit(solution)/shard_map/ppermute | solution.py:274
  110.5 15.9 %all-to-all-start.4 = ((s16[16,80,128]{2,1,0:T(8,128)(2,1)}), s16[16,80,128]{2,1,0:T(8,128)(2,1)S(1)}, u32[]{:S(2)}, u32[]{:S(2)}) async-start(s16[16,80,128]{2,1,0:T(8,128)(2,1)} %copies.3), calls=%async_computation.4 | async-start | bytes 655360 | tf_op jit(solution)/shard_map/all_to_all | solution.py:280
  116.3 3.8 %collective-permute-start.6 = (f32[16,64,128]{2,1,0:T(8,128)S(1)}, f32[16,64,128]{2,1,0:T(8,128)S(1)}, u32[]{:S(2)}, u32[]{:S(2)}) collective-permute-start(f32[16,64,128]{2,1,0:T(8,128)S(1)} %get-tuple-element.20), channel_id=1, source_target_pairs={{0,1},{1,0},{2,3},{3,2},{4,5},{5,4},{6,7},{7,6},{8,9},{9,8},{10,11... | collective-permute-start | bytes 1572872 | tf_op jit(solution)/shard_map/ppermute | solution.py:303
  126.4 18.7 %all-to-all-start.7 = ((s16[16,80,128]{2,1,0:T(8,128)(2,1)}), s16[16,80,128]{2,1,0:T(8,128)(2,1)S(1)}, u32[]{:S(2)}, u32[]{:S(2)}) async-start(s16[16,80,128]{2,1,0:T(8,128)(2,1)} %join.3), calls=%async_computation.7 | async-start | bytes 655360 | tf_op jit(solution)/shard_map/all_to_all | solution.py:280
  130.7 3.5 %collective-permute-start.5 = (s16[16,80,128]{2,1,0:T(8,128)(2,1)S(1)}, s16[16,80,128]{2,1,0:T(8,128)(2,1)S(1)}, u32[]{:S(2)}, u32[]{:S(2)}) collective-permute-start(s16[16,80,128]{2,1,0:T(8,128)(2,1)S(1)} %all-to-all-done.4.own_ref), channel_id=1, source_target_pairs={{0,1},{1,0},{2,3},{3,2},{4,5},{5,4},{6,7},{7,6},{8,9},{9,8},{10,11... | collective-permute-start | bytes 983048 | tf_op jit(solution)/shard_map/ppermute | solution.py:306
  145.1 17.6 %all-to-all-start.5 = ((s16[16,80,128]{2,1,0:T(8,128)(2,1)}), s16[16,80,128]{2,1,0:T(8,128)(2,1)S(1)}, u32[]{:S(2)}, u32[]{:S(2)}) async-start(s16[16,80,128]{2,1,0:T(8,128)(2,1)} %mirror.3), calls=%async_computation.5 | async-start | bytes 655360 | tf_op jit(solution)/shard_map/all_to_all | solution.py:277
  153.5 12.1 %collective-permute-start.7 = (f32[64,128]{1,0:T(8,128)S(1)}, f32[64,128]{1,0:T(8,128)S(1)}, u32[]{:S(2)}, u32[]{:S(2)}) collective-permute-start(f32[64,128]{1,0:T(8,128)S(1)} %sum.3), channel_id=1, source_target_pairs={{28,0},{12,32},{31,64},{4,96},{7,128},{26,160},{25,192},{3,224},{0... | collective-permute-start | bytes 98312 | tf_op jit(solution)/shard_map/ppermute | solution.py:274

commit v5 on v4

--- a/solution.py
+++ b/solution.py
@@ -55,7 +55,7 @@
     return high, (value - high.astype(jnp.float32)).astype(jnp.bfloat16)
 
 
-def first_kernel(scores_ref, copies_ref, one_ref):
+def first_kernel(tiles_ref, slots_ref, scores_ref, copies_ref, one_ref):
     put_message(scores_ref[...], copies_ref, one_ref)
 
 
@@ -287,7 +287,8 @@
     sums = jax.ShapeDtypeStruct((half, rows, classes), jnp.float32)
     share = jax.ShapeDtypeStruct((rows, classes), jnp.float32)
 
-    copies, one = call(first_kernel, "first", (brow_pieces, piece), (initial,))
+    copies, one = call(first_kernel, "first", (brow_pieces, piece), (stored, slots, initial),
+                       [ANYWHERE, ANYWHERE, WHOLE])
     for sweep in range(SWEEPS):
         col_got = over_brow(copies)
         other = swap(one, pairs)

time: 168 us -> 167 us (level)
  starting transfers between devices: 79.2 us -> 76.3 us
  waiting for transfers between devices: 64 us -> 66.9 us
    all_to_all x4, waiting for transfers between devices: 23.3 us -> 26.1 us  [over_bcol(): lax.all_to_all(value, 'bcol', split_axis=0, concat_axis=0, tiled=True, ax...]
    all_to_all x4, starting transfers between devices: 17.7 us -> 15 us  [over_bcol(): lax.all_to_all(value, 'bcol', split_axis=0, concat_axis=0, tiled=True, ax...]
    unnamed x20 -> x18, local copies, waits for them, and re-layouts: 3.75 us -> 3.07 us
where the time goes in v5:
time: 167 us; the launch traced here: 166 us
  starting transfers between devices  76.3 us (46%)
  waiting for transfers between devices  66.9 us (40%)
  Pallas kernels  18.6 us (11%)
  local copies, waits for them, and re-layouts  3.21 us (2%)
    all_to_all x4, starting transfers between devices, over_brow(): lax.all_to_all(value, 'brow', split_axis=0, concat_axis=0, tiled=True)  31.3 us
    ppermute x4, waiting for transfers between devices, swap(): return lax.ppermute(value, ('brow', 'bcol'), way)  28.8 us
    all_to_all x4, waiting for transfers between devices, over_bcol(): lax.all_to_all(value, 'bcol', split_axis=0, concat_axis=0, tiled=True, ax...  26.1 us
    ppermute x4, starting transfers between devices, swap(): return lax.ppermute(value, ('brow', 'bcol'), way)  22.3 us
    pallas_call x13, Pallas kernels, call(): pl.pallas_call(kernel, out_shape=outs, in_specs=specs or [WHOLE] * len(ar...  18.6 us
    all_to_all x4, starting transfers between devices, over_bcol(): lax.all_to_all(value, 'bcol', split_axis=0, concat_axis=0, tiled=True, ax...  15 us
    all_to_all x4, waiting for transfers between devices, over_brow(): lax.all_to_all(value, 'brow', split_axis=0, concat_axis=0, tiled=True)  5.03 us
    ppermute x2, starting transfers between devices, on_device(): got = lax.ppermute(send, 'bcol', exchange)  3.84 us
  transfers between devices with their start and end apart: 16, of which 13 were waited for; matrix products, arithmetic and copies ran while one was open for 0% of the time, Pallas kernels for 9%

profile of v5, /device:TPU:56, one launch (start us, length us, event | category | flops | bytes accessed | tf_op | source)
XLA Modules:
  0.0 165.8 jit_solution(3223041038458810844)
XLA Ops:
  0.0 1.6 copy-done
  4.1 8.7 %all-to-all-start = ((s16[16,80,128]{2,1,0:T(8,128)(2,1)}), s16[16,80,128]{2,1,0:T(8,128)(2,1)S(1)}, u32[]{:S(2)}, u32[]{:S(2)}) async-start(s16[16,80,128]{2,1,0:T(8,128)(2,1)} %get-tuple-element.13), calls=%async_computation | async-start | bytes 655360 | tf_op jit(solution)/shard_map/all_to_all | solution.py:277
  12.8 11.8 %collective-permute-start = (s16[80,128]{1,0:T(8,128)(2,1)S(1)}, s16[80,128]{1,0:T(8,128)(2,1)S(1)}, u32[]{:S(2)}, u32[]{:S(2)}) collective-permute-start(s16[80,128]{1,0:T(8,128)(2,1)S(1)} %get-tuple-element.14), channel_id=1, source_target_pairs={{0,28},{32,12},{64,31},{96,4},{128,7},{160,26},{192,25},{224,3},{2... | collective-permute-start | bytes 61448 | tf_op jit(solution)/shard_map/ppermute | solution.py:274
  24.6 8.1 %collective-permute-done.one_ref = s16[80,128]{1,0:T(8,128)(2,1)S(1)} collective-permute-done((s16[80,128]{1,0:T(8,128)(2,1)S(1)}, s16[80,128]{1,0:T(8,128)(2,1)S(1)}, u32[]{:S(2)}, u32[]{:S(2)}) %collective-permute-start) | collective-permute-done | bytes 20512 | tf_op jit(solution)/shard_map/ppermute | solution.py:274
  33.5 3.5 %all-to-all-start.1 = ((s16[16,80,128]{2,1,0:T(8,128)(2,1)}), s16[16,80,128]{2,1,0:T(8,128)(2,1)S(1)}, u32[]{:S(2)}, u32[]{:S(2)}) async-start(s16[16,80,128]{2,1,0:T(8,128)(2,1)} %copies.2), calls=%async_computation.1 | async-start | bytes 655360 | tf_op jit(solution)/shard_map/all_to_all | solution.py:280
  37.7 2.2 %forward.2 = (f32[16,64,128]{2,1,0:T(8,128)S(1)}, f32[16,64,128]{2,1,0:T(8,128)S(1)}) custom-call(s32[2,64]{1,0:T(2,128)S(1)} %bitcast.17, s32[1,1]{1,0:T(1,128)S(6)} %copy.8.count_ref, s32[16,32]{1,0:T(8,128)S(1)} %copy-done.4, s16[16,80,128]{2,1,0:T(8,128)(2,1)S(1)} %all-to-all-done.after_ref.got_ref, bf16[64,128,128]{2,1,0:T(8,128)(2,1)S(1)} %bitcast.9), custom_call_target="tpu_custom_call" | custom-call | tf_op jit(solution)/shard_map/forward/pallas_call | solution.py:239
  39.9 1.9 %collective-permute-start.2 = (f32[16,64,128]{2,1,0:T(8,128)S(1)}, f32[16,64,128]{2,1,0:T(8,128)S(1)}, u32[]{:S(2)}, u32[]{:S(2)}) collective-permute-start(f32[16,64,128]{2,1,0:T(8,128)S(1)} %get-tuple-element.16), channel_id=1, source_target_pairs={{0,1},{1,0},{2,3},{3,2},{4,5},{5,4},{6,7},{7,6},{8,9},{9,8},{10,11... | collective-permute-start | bytes 1572872 | tf_op jit(solution)/shard_map/ppermute | solution.py:304
  41.9 1.9 %collective-permute-done.2.got_ref = f32[16,64,128]{2,1,0:T(8,128)S(1)} collective-permute-done((f32[16,64,128]{2,1,0:T(8,128)S(1)}, f32[16,64,128]{2,1,0:T(8,128)S(1)}, u32[]{:S(2)}, u32[]{:S(2)}) %collective-permute-start.2) | collective-permute-done | bytes 524320 | tf_op jit(solution)/shard_map/ppermute | solution.py:304
  44.8 6.4 %all-to-all-done.1.own_ref = s16[16,80,128]{2,1,0:T(8,128)(2,1)S(1)} async-done(((s16[16,80,128]{2,1,0:T(8,128)(2,1)}), s16[16,80,128]{2,1,0:T(8,128)(2,1)S(1)}, u32[]{:S(2)}, u32[]{:S(2)}) %all-to-all-start.1) | async-done | bytes 327712 | tf_op jit(solution)/shard_map/all_to_all | solution.py:280
  51.2 3.5 %all-to-all-start.3 = ((s16[16,80,128]{2,1,0:T(8,128)(2,1)}), s16[16,80,128]{2,1,0:T(8,128)(2,1)S(1)}, u32[]{:S(2)}, u32[]{:S(2)}) async-start(s16[16,80,128]{2,1,0:T(8,128)(2,1)} %join.2), calls=%async_computation.3 | async-start | bytes 655360 | tf_op jit(solution)/shard_map/all_to_all | solution.py:280
  54.8 1.9 %collective-permute-start.1 = (s16[16,80,128]{2,1,0:T(8,128)(2,1)S(1)}, s16[16,80,128]{2,1,0:T(8,128)(2,1)S(1)}, u32[]{:S(2)}, u32[]{:S(2)}) collective-permute-start(s16[16,80,128]{2,1,0:T(8,128)(2,1)S(1)} %all-to-all-done.1.own_ref), channel_id=1, source_target_pairs={{0,1},{1,0},{2,3},{3,2},{4,5},{5,4},{6,7},{7,6},{8,9},{9,8},{10,11... | collective-permute-start | bytes 983048 | tf_op jit(solution)/shard_map/ppermute | solution.py:307
  58.3 3.5 %mirror.2 = s16[16,80,128]{2,1,0:T(8,128)(2,1)} custom-call(s32[2,64]{1,0:T(2,128)S(1)} %bitcast.18, s32[1,1]{1,0:T(1,128)S(6)} %copy.8.count_ref, s32[16,32]{1,0:T(8,128)S(1)} %copy-done.4, s16[16,80,128]{2,1,0:T(8,128)(2,1)S(1)} %all-to-all-done.1.own_ref, s16[16,80,128]{2,1,0:T(8,128)(2,1)S(1)} %collective-permute-done.1.other_ref, ...), custom_call_target="tpu_custom_call" | custom-call | tf_op jit(solution)/shard_map/mirror/pallas_call | solution.py:239
  61.8 7.2 %all-to-all-done.3.got_ref = s16[16,80,128]{2,1,0:T(8,128)(2,1)S(1)} async-done(((s16[16,80,128]{2,1,0:T(8,128)(2,1)}), s16[16,80,128]{2,1,0:T(8,128)(2,1)S(1)}, u32[]{:S(2)}, u32[]{:S(2)}) %all-to-all-start.3) | async-done | bytes 327712 | tf_op jit(solution)/shard_map/all_to_all | solution.py:280
  69.0 7.8 %all-to-all-start.2 = ((s16[16,80,128]{2,1,0:T(8,128)(2,1)}), s16[16,80,128]{2,1,0:T(8,128)(2,1)S(1)}, u32[]{:S(2)}, u32[]{:S(2)}) async-start(s16[16,80,128]{2,1,0:T(8,128)(2,1)} %mirror.2), calls=%async_computation.2 | async-start | bytes 655360 | tf_op jit(solution)/shard_map/all_to_all | solution.py:277
  76.9 4.5 %collective-permute-start.3 = (f32[64,128]{1,0:T(8,128)S(1)}, f32[64,128]{1,0:T(8,128)S(1)}, u32[]{:S(2)}, u32[]{:S(2)}) collective-permute-start(f32[64,128]{1,0:T(8,128)S(1)} %sum.2), channel_id=1, source_target_pairs={{28,0},{12,32},{31,64},{4,96},{7,128},{26,160},{25,192},{3,224},{0... | collective-permute-start | bytes 98312 | tf_op jit(solution)/shard_map/ppermute | solution.py:274
  81.4 7.7 %collective-permute-done.3.row_ref = f32[64,128]{1,0:T(8,128)S(1)} collective-permute-done((f32[64,128]{1,0:T(8,128)S(1)}, f32[64,128]{1,0:T(8,128)S(1)}, u32[]{:S(2)}, u32[]{:S(2)}) %collective-permute-start.3) | collective-permute-done | bytes 32800 | tf_op jit(solution)/shard_map/ppermute | solution.py:274
  90.5 6.6 %all-to-all-start.6 = ((s16[16,80,128]{2,1,0:T(8,128)(2,1)}), s16[16,80,128]{2,1,0:T(8,128)(2,1)S(1)}, u32[]{:S(2)}, u32[]{:S(2)}) async-start(s16[16,80,128]{2,1,0:T(8,128)(2,1)} %get-tuple-element.18), calls=%async_computation.6 | async-start | bytes 655360 | tf_op jit(solution)/shard_map/all_to_all | solution.py:277
  97.1 1.9 %collective-permute-start.4 = (s16[80,128]{1,0:T(8,128)(2,1)S(1)}, s16[80,128]{1,0:T(8,128)(2,1)S(1)}, u32[]{:S(2)}, u32[]{:S(2)}) collective-permute-start(s16[80,128]{1,0:T(8,128)(2,1)S(1)} %get-tuple-element.17), channel_id=1, source_target_pairs={{0,28},{32,12},{64,31},{96,4},{128,7},{160,26},{192,25},{224,3},{2... | collective-permute-start | bytes 61448 | tf_op jit(solution)/shard_map/ppermute | solution.py:274
  99.0 10.1 %collective-permute-done.4.after_ref.one_ref = s16[80,128]{1,0:T(8,128)(2,1)S(1)} collective-permute-done((s16[80,128]{1,0:T(8,128)(2,1)S(1)}, s16[80,128]{1,0:T(8,128)(2,1)S(1)}, u32[]{:S(2)}, u32[]{:S(2)}) %collective-permute-start.4) | collective-permute-done | bytes 20512 | tf_op jit(solution)/shard_map/ppermute | solution.py:274
  109.8 3.5 %all-to-all-start.4 = ((s16[16,80,128]{2,1,0:T(8,128)(2,1)}), s16[16,80,128]{2,1,0:T(8,128)(2,1)S(1)}, u32[]{:S(2)}, u32[]{:S(2)}) async-start(s16[16,80,128]{2,1,0:T(8,128)(2,1)} %copies.3), calls=%async_computation.4 | async-start | bytes 655360 | tf_op jit(solution)/shard_map/all_to_all | solution.py:280
  113.4 2.2 %forward.3 = (f32[16,64,128]{2,1,0:T(8,128)S(1)}, f32[16,64,128]{2,1,0:T(8,128)S(1)}) custom-call(s32[2,64]{1,0:T(2,128)S(1)} %bitcast.19, s32[1,1]{1,0:T(1,128)S(6)} %copy.8.count_ref, s32[16,32]{1,0:T(8,128)S(1)} %copy-done.4, s16[16,80,128]{2,1,0:T(8,128)(2,1)S(1)} %all-to-all-done.6.got_ref, bf16[64,128,128]{2,1,0:T(8,128)(2,1)S(1)} %bitcast.11), custom_call_target="tpu_custom_call" | custom-call | tf_op jit(solution)/shard_map/forward/pallas_call | solution.py:239
  115.6 1.9 %collective-permute-start.6 = (f32[16,64,128]{2,1,0:T(8,128)S(1)}, f32[16,64,128]{2,1,0:T(8,128)S(1)}, u32[]{:S(2)}, u32[]{:S(2)}) collective-permute-start(f32[16,64,128]{2,1,0:T(8,128)S(1)} %get-tuple-element.20), channel_id=1, source_target_pairs={{0,1},{1,0},{2,3},{3,2},{4,5},{5,4},{6,7},{7,6},{8,9},{9,8},{10,11... | collective-permute-start | bytes 1572872 | tf_op jit(solution)/shard_map/ppermute | solution.py:304
  117.5 1.9 %collective-permute-done.6.got_ref = f32[16,64,128]{2,1,0:T(8,128)S(1)} collective-permute-done((f32[16,64,128]{2,1,0:T(8,128)S(1)}, f32[16,64,128]{2,1,0:T(8,128)S(1)}, u32[]{:S(2)}, u32[]{:S(2)}) %collective-permute-start.6) | collective-permute-done | bytes 524320 | tf_op jit(solution)/shard_map/ppermute | solution.py:304
  120.5 5.2 %all-to-all-done.4.own_ref = s16[16,80,128]{2,1,0:T(8,128)(2,1)S(1)} async-done(((s16[16,80,128]{2,1,0:T(8,128)(2,1)}), s16[16,80,128]{2,1,0:T(8,128)(2,1)S(1)}, u32[]{:S(2)}, u32[]{:S(2)}) %all-to-all-start.4) | async-done | bytes 327712 | tf_op jit(solution)/shard_map/all_to_all | solution.py:280
  125.7 4.4 %all-to-all-start.7 = ((s16[16,80,128]{2,1,0:T(8,128)(2,1)}), s16[16,80,128]{2,1,0:T(8,128)(2,1)S(1)}, u32[]{:S(2)}, u32[]{:S(2)}) async-start(s16[16,80,128]{2,1,0:T(8,128)(2,1)} %join.3), calls=%async_computation.7 | async-start | bytes 655360 | tf_op jit(solution)/shard_map/all_to_all | solution.py:280
  130.1 1.9 %collective-permute-start.5 = (s16[16,80,128]{2,1,0:T(8,128)(2,1)S(1)}, s16[16,80,128]{2,1,0:T(8,128)(2,1)S(1)}, u32[]{:S(2)}, u32[]{:S(2)}) collective-permute-start(s16[16,80,128]{2,1,0:T(8,128)(2,1)S(1)} %all-to-all-done.4.own_ref), channel_id=1, source_target_pairs={{0,1},{1,0},{2,3},{3,2},{4,5},{5,4},{6,7},{7,6},{8,9},{9,8},{10,11... | collective-permute-start | bytes 983048 | tf_op jit(solution)/shard_map/ppermute | solution.py:307
  133.6 3.5 %mirror.3 = s16[16,80,128]{2,1,0:T(8,128)(2,1)} custom-call(s32[2,64]{1,0:T(2,128)S(1)} %bitcast.20, s32[1,1]{1,0:T(1,128)S(6)} %copy.8.count_ref, s32[16,32]{1,0:T(8,128)S(1)} %copy-done.4, s16[16,80,128]{2,1,0:T(8,128)(2,1)S(1)} %all-to-all-done.4.own_ref, s16[16,80,128]{2,1,0:T(8,128)(2,1)S(1)} %collective-permute-done.5.other_ref, ...), custom_call_target="tpu_custom_call" | custom-call | tf_op jit(solution)/shard_map/mirror/pallas_call | solution.py:239
  137.1 7.4 %all-to-all-done.7.got_ref = s16[16,80,128]{2,1,0:T(8,128)(2,1)S(1)} async-done(((s16[16,80,128]{2,1,0:T(8,128)(2,1)}), s16[16,80,128]{2,1,0:T(8,128)(2,1)S(1)}, u32[]{:S(2)}, u32[]{:S(2)}) %all-to-all-start.7) | async-done | bytes 327712 | tf_op jit(solution)/shard_map/all_to_all | solution.py:280
  144.4 8.3 %all-to-all-start.5 = ((s16[16,80,128]{2,1,0:T(8,128)(2,1)}), s16[16,80,128]{2,1,0:T(8,128)(2,1)S(1)}, u32[]{:S(2)}, u32[]{:S(2)}) async-start(s16[16,80,128]{2,1,0:T(8,128)(2,1)} %mirror.3), calls=%async_computation.5 | async-start | bytes 655360 | tf_op jit(solution)/shard_map/all_to_all | solution.py:277
  152.9 4.2 %collective-permute-start.7 = (f32[64,128]{1,0:T(8,128)S(1)}, f32[64,128]{1,0:T(8,128)S(1)}, u32[]{:S(2)}, u32[]{:S(2)}) collective-permute-start(f32[64,128]{1,0:T(8,128)S(1)} %sum.3), channel_id=1, source_target_pairs={{28,0},{12,32},{31,64},{4,96},{7,128},{26,160},{25,192},{3,224},{0... | collective-permute-start | bytes 98312 | tf_op jit(solution)/shard_map/ppermute | solution.py:274
  157.1 5.0 %all-to-all-done.5.got_ref = s16[16,80,128]{2,1,0:T(8,128)(2,1)S(1)} async-done(((s16[16,80,128]{2,1,0:T(8,128)(2,1)}), s16[16,80,128]{2,1,0:T(8,128)(2,1)S(1)}, u32[]{:S(2)}, u32[]{:S(2)}) %all-to-all-start.5) | async-done | bytes 327712 | tf_op jit(solution)/shard_map/all_to_all | solution.py:277
  162.1 2.9 %collective-permute-done.7.row_ref = f32[64,128]{1,0:T(8,128)S(1)} collective-permute-done((f32[64,128]{1,0:T(8,128)S(1)}, f32[64,128]{1,0:T(8,128)S(1)}, u32[]{:S(2)}, u32[]{:S(2)}) %collective-permute-start.7) | collective-permute-done | bytes 32800 | tf_op jit(solution)/shard_map/ppermute | solution.py:274
  (35 shorter events, 12.0 us)
Async XLA Ops:
  0.0 37.7 %copy-start.6 = (s32[1,1,2,64]{3,2,1,0:T(2,128)S(1)}, s32[1,1,2,64]{3,2,1,0:T(2,128)}, u32[]{:S(2)}) copy-start(s32[1,1,2,64]{3,2,1,0:T(2,128)} %param.11) | copy-start | bytes 1540
  0.0 1.6 copy-start
  1.6 0.8 copy-start.2
  2.4 0.7 copy-start.5
  3.0 34.6 %copy-start.1 = (bf16[1,1,64,128,128]{4,3,2,1,0:T(8,128)(2,1)S(1)}, bf16[1,1,64,128,128]{4,3,2,1,0:T(8,128)(2,1)}, u32[]{:S(2)}) copy-start(bf16[1,1,64,128,128]{4,3,2,1,0:T(8,128)(2,1)} %param.10) | copy-start | bytes 6291460
  3.0 34.6 %copy-start.4 = (s32[16,32]{1,0:T(8,128)S(1)}, s32[16,32]{1,0:T(8,128)}, u32[]{:S(2)}) copy-start(s32[16,32]{1,0:T(8,128)} %constant.2.clone.held_ref) | copy-start | bytes 6148
  4.1 28.6 %all-to-all-start = ((s16[16,80,128]{2,1,0:T(8,128)(2,1)}), s16[16,80,128]{2,1,0:T(8,128)(2,1)S(1)}, u32[]{:S(2)}, u32[]{:S(2)}) async-start(s16[16,80,128]{2,1,0:T(8,128)(2,1)} %get-tuple-element.13), calls=%async_computation | async-start | bytes 655360 | tf_op jit(solution)/shard_map/all_to_all | solution.py:277
  12.8 19.9 %collective-permute-start = (s16[80,128]{1,0:T(8,128)(2,1)S(1)}, s16[80,128]{1,0:T(8,128)(2,1)S(1)}, u32[]{:S(2)}, u32[]{:S(2)}) collective-permute-start(s16[80,128]{1,0:T(8,128)(2,1)S(1)} %get-tuple-element.14), channel_id=1, source_target_pairs={{0,28},{32,12},{64,31},{96,4},{128,7},{160,26},{192,25},{224,3},{2... | collective-permute-start | bytes 61448 | tf_op jit(solution)/shard_map/ppermute | solution.py:274
  33.5 17.8 %all-to-all-start.1 = ((s16[16,80,128]{2,1,0:T(8,128)(2,1)}), s16[16,80,128]{2,1,0:T(8,128)(2,1)S(1)}, u32[]{:S(2)}, u32[]{:S(2)}) async-start(s16[16,80,128]{2,1,0:T(8,128)(2,1)} %copies.2), calls=%async_computation.1 | async-start | bytes 655360 | tf_op jit(solution)/shard_map/all_to_all | solution.py:280
  39.9 3.8 %collective-permute-start.2 = (f32[16,64,128]{2,1,0:T(8,128)S(1)}, f32[16,64,128]{2,1,0:T(8,128)S(1)}, u32[]{:S(2)}, u32[]{:S(2)}) collective-permute-start(f32[16,64,128]{2,1,0:T(8,128)S(1)} %get-tuple-element.16), channel_id=1, source_target_pairs={{0,1},{1,0},{2,3},{3,2},{4,5},{5,4},{6,7},{7,6},{8,9},{9,8},{10,11... | collective-permute-start | bytes 1572872 | tf_op jit(solution)/shard_map/ppermute | solution.py:304
  44.8 31.9 %copy-start.7 = (s32[1,64]{1,0:T(1,128)S(1)}, s32[1,64]{1,0:T(1,128)}, u32[]{:S(2)}) copy-start(s32[1,64]{1,0:T(1,128)} %param.8) | copy-start | bytes 772
  51.2 17.7 %all-to-all-start.3 = ((s16[16,80,128]{2,1,0:T(8,128)(2,1)}), s16[16,80,128]{2,1,0:T(8,128)(2,1)S(1)}, u32[]{:S(2)}, u32[]{:S(2)}) async-start(s16[16,80,128]{2,1,0:T(8,128)(2,1)} %join.2), calls=%async_computation.3 | async-start | bytes 655360 | tf_op jit(solution)/shard_map/all_to_all | solution.py:280
  54.8 26.6 %copy-start.8 = (s32[1,64]{1,0:T(1,128)S(1)}, s32[1,64]{1,0:T(1,128)}, u32[]{:S(2)}) copy-start(s32[1,64]{1,0:T(1,128)} %param.9) | copy-start | bytes 772
  54.8 34.4 %copy-start.3 = (f32[1,64,128]{2,1,0:T(8,128)S(1)}, f32[1,64,128]{2,1,0:T(8,128)}, u32[]{:S(2)}) copy-start(f32[1,64,128]{2,1,0:T(8,128)} %param.7) | copy-start | bytes 98308
  54.8 3.5 %collective-permute-start.1 = (s16[16,80,128]{2,1,0:T(8,128)(2,1)S(1)}, s16[16,80,128]{2,1,0:T(8,128)(2,1)S(1)}, u32[]{:S(2)}, u32[]{:S(2)}) collective-permute-start(s16[16,80,128]{2,1,0:T(8,128)(2,1)S(1)} %all-to-all-done.1.own_ref), channel_id=1, source_target_pairs={{0,1},{1,0},{2,3},{3,2},{4,5},{5,4},{6,7},{7,6},{8,9},{9,8},{10,11... | collective-permute-start | bytes 983048 | tf_op jit(solution)/shard_map/ppermute | solution.py:307
  69.0 20.1 %all-to-all-start.2 = ((s16[16,80,128]{2,1,0:T(8,128)(2,1)}), s16[16,80,128]{2,1,0:T(8,128)(2,1)S(1)}, u32[]{:S(2)}, u32[]{:S(2)}) async-start(s16[16,80,128]{2,1,0:T(8,128)(2,1)} %mirror.2), calls=%async_computation.2 | async-start | bytes 655360 | tf_op jit(solution)/shard_map/all_to_all | solution.py:277
  76.9 12.1 %collective-permute-start.3 = (f32[64,128]{1,0:T(8,128)S(1)}, f32[64,128]{1,0:T(8,128)S(1)}, u32[]{:S(2)}, u32[]{:S(2)}) collective-permute-start(f32[64,128]{1,0:T(8,128)S(1)} %sum.2), channel_id=1, source_target_pairs={{28,0},{12,32},{31,64},{4,96},{7,128},{26,160},{25,192},{3,224},{0... | collective-permute-start | bytes 98312 | tf_op jit(solution)/shard_map/ppermute | solution.py:274
  90.5 19.4 %all-to-all-start.6 = ((s16[16,80,128]{2,1,0:T(8,128)(2,1)}), s16[16,80,128]{2,1,0:T(8,128)(2,1)S(1)}, u32[]{:S(2)}, u32[]{:S(2)}) async-start(s16[16,80,128]{2,1,0:T(8,128)(2,1)} %get-tuple-element.18), calls=%async_computation.6 | async-start | bytes 655360 | tf_op jit(solution)/shard_map/all_to_all | solution.py:277
  97.1 12.0 %collective-permute-start.4 = (s16[80,128]{1,0:T(8,128)(2,1)S(1)}, s16[80,128]{1,0:T(8,128)(2,1)S(1)}, u32[]{:S(2)}, u32[]{:S(2)}) collective-permute-start(s16[80,128]{1,0:T(8,128)(2,1)S(1)} %get-tuple-element.17), channel_id=1, source_target_pairs={{0,28},{32,12},{64,31},{96,4},{128,7},{160,26},{192,25},{224,3},{2... | collective-permute-start | bytes 61448 | tf_op jit(solution)/shard_map/ppermute | solution.py:274
  109.8 15.9 %all-to-all-start.4 = ((s16[16,80,128]{2,1,0:T(8,128)(2,1)}), s16[16,80,128]{2,1,0:T(8,128)(2,1)S(1)}, u32[]{:S(2)}, u32[]{:S(2)}) async-start(s16[16,80,128]{2,1,0:T(8,128)(2,1)} %copies.3), calls=%async_computation.4 | async-start | bytes 655360 | tf_op jit(solution)/shard_map/all_to_all | solution.py:280
  115.6 3.8 %collective-permute-start.6 = (f32[16,64,128]{2,1,0:T(8,128)S(1)}, f32[16,64,128]{2,1,0:T(8,128)S(1)}, u32[]{:S(2)}, u32[]{:S(2)}) collective-permute-start(f32[16,64,128]{2,1,0:T(8,128)S(1)} %get-tuple-element.20), channel_id=1, source_target_pairs={{0,1},{1,0},{2,3},{3,2},{4,5},{5,4},{6,7},{7,6},{8,9},{9,8},{10,11... | collective-permute-start | bytes 1572872 | tf_op jit(solution)/shard_map/ppermute | solution.py:304
  125.7 18.7 %all-to-all-start.7 = ((s16[16,80,128]{2,1,0:T(8,128)(2,1)}), s16[16,80,128]{2,1,0:T(8,128)(2,1)S(1)}, u32[]{:S(2)}, u32[]{:S(2)}) async-start(s16[16,80,128]{2,1,0:T(8,128)(2,1)} %join.3), calls=%async_computation.7 | async-start | bytes 655360 | tf_op jit(solution)/shard_map/all_to_all | solution.py:280
  130.1 3.5 %collective-permute-start.5 = (s16[16,80,128]{2,1,0:T(8,128)(2,1)S(1)}, s16[16,80,128]{2,1,0:T(8,128)(2,1)S(1)}, u32[]{:S(2)}, u32[]{:S(2)}) collective-permute-start(s16[16,80,128]{2,1,0:T(8,128)(2,1)S(1)} %all-to-all-done.4.own_ref), channel_id=1, source_target_pairs={{0,1},{1,0},{2,3},{3,2},{4,5},{5,4},{6,7},{7,6},{8,9},{9,8},{10,11... | collective-permute-start | bytes 983048 | tf_op jit(solution)/shard_map/ppermute | solution.py:307
  144.4 17.6 %all-to-all-start.5 = ((s16[16,80,128]{2,1,0:T(8,128)(2,1)}), s16[16,80,128]{2,1,0:T(8,128)(2,1)S(1)}, u32[]{:S(2)}, u32[]{:S(2)}) async-start(s16[16,80,128]{2,1,0:T(8,128)(2,1)} %mirror.3), calls=%async_computation.5 | async-start | bytes 655360 | tf_op jit(solution)/shard_map/all_to_all | solution.py:277
  152.9 12.1 %collective-permute-start.7 = (f32[64,128]{1,0:T(8,128)S(1)}, f32[64,128]{1,0:T(8,128)S(1)}, u32[]{:S(2)}, u32[]{:S(2)}) collective-permute-start(f32[64,128]{1,0:T(8,128)S(1)} %sum.3), channel_id=1, source_target_pairs={{28,0},{12,32},{31,64},{4,96},{7,128},{26,160},{25,192},{3,224},{0... | collective-permute-start | bytes 98312 | tf_op jit(solution)/shard_map/ppermute | solution.py:274

commit v6 on v4

--- a/solution.py
+++ b/solution.py
@@ -55,7 +55,7 @@
     return high, (value - high.astype(jnp.float32)).astype(jnp.bfloat16)
 
 
-def first_kernel(scores_ref, copies_ref, one_ref):
+def first_kernel(tiles_ref, slots_ref, count_ref, scores_ref, copies_ref, one_ref):
     put_message(scores_ref[...], copies_ref, one_ref)
 
 
@@ -287,7 +287,8 @@
     sums = jax.ShapeDtypeStruct((half, rows, classes), jnp.float32)
     share = jax.ShapeDtypeStruct((rows, classes), jnp.float32)
 
-    copies, one = call(first_kernel, "first", (brow_pieces, piece), (initial,))
+    copies, one = call(first_kernel, "first", (brow_pieces, piece), (stored, slots, tile_count, initial),
+                       [ANYWHERE, ANYWHERE, SCALARS, WHOLE])
     for sweep in range(SWEEPS):
         col_got = over_brow(copies)
         other = swap(one, pairs)

time: 168 us -> 167 us (level)
  starting transfers between devices: 79.2 us -> 75.8 us
  waiting for transfers between devices: 64 us -> 67.3 us
    all_to_all x4, waiting for transfers between devices: 23.3 us -> 26.3 us  [over_bcol(): lax.all_to_all(value, 'bcol', split_axis=0, concat_axis=0, tiled=True, ax...]
    all_to_all x4, starting transfers between devices: 17.7 us -> 14.8 us  [over_bcol(): lax.all_to_all(value, 'bcol', split_axis=0, concat_axis=0, tiled=True, ax...]
    unnamed x20 -> x18, local copies, waits for them, and re-layouts: 3.75 us -> 3.05 us
where the time goes in v6:
time: 167 us; the launch traced here: 166 us
  starting transfers between devices  75.8 us (45%)
  waiting for transfers between devices  67.3 us (40%)
  Pallas kernels  18.6 us (11%)
  local copies, waits for them, and re-layouts  3.19 us (2%)
    all_to_all x4, starting transfers between devices, over_brow(): lax.all_to_all(value, 'brow', split_axis=0, concat_axis=0, tiled=True)  31.4 us
    ppermute x4, waiting for transfers between devices, swap(): return lax.ppermute(value, ('brow', 'bcol'), way)  29 us
    all_to_all x4, waiting for transfers between devices, over_bcol(): lax.all_to_all(value, 'bcol', split_axis=0, concat_axis=0, tiled=True, ax...  26.3 us
    ppermute x4, starting transfers between devices, swap(): return lax.ppermute(value, ('brow', 'bcol'), way)  22 us
    pallas_call x13, Pallas kernels, call(): pl.pallas_call(kernel, out_shape=outs, in_specs=specs or [WHOLE] * len(ar...  18.6 us
    all_to_all x4, starting transfers between devices, over_bcol(): lax.all_to_all(value, 'bcol', split_axis=0, concat_axis=0, tiled=True, ax...  14.8 us
    all_to_all x4, waiting for transfers between devices, over_brow(): lax.all_to_all(value, 'brow', split_axis=0, concat_axis=0, tiled=True)  5.09 us
    ppermute x2, starting transfers between devices, on_device(): got = lax.ppermute(send, 'bcol', exchange)  3.84 us
  transfers between devices with their start and end apart: 16, of which 13 were waited for; matrix products, arithmetic and copies ran while one was open for 0% of the time, Pallas kernels for 9%

profile of v6, /device:TPU:56, one launch (start us, length us, event | category | flops | bytes accessed | tf_op | source)
XLA Modules:
  0.0 165.8 jit_solution(2517653573056046803)
XLA Ops:
  4.8 8.7 %all-to-all-start = ((s16[16,80,128]{2,1,0:T(8,128)(2,1)}), s16[16,80,128]{2,1,0:T(8,128)(2,1)S(1)}, u32[]{:S(2)}, u32[]{:S(2)}) async-start(s16[16,80,128]{2,1,0:T(8,128)(2,1)} %get-tuple-element.13), calls=%async_computation | async-start | bytes 655360 | tf_op jit(solution)/shard_map/all_to_all | solution.py:277
  13.5 11.8 %collective-permute-start = (s16[80,128]{1,0:T(8,128)(2,1)S(1)}, s16[80,128]{1,0:T(8,128)(2,1)S(1)}, u32[]{:S(2)}, u32[]{:S(2)}) collective-permute-start(s16[80,128]{1,0:T(8,128)(2,1)S(1)} %get-tuple-element.14), channel_id=1, source_target_pairs={{0,28},{32,12},{64,31},{96,4},{128,7},{160,26},{192,25},{224,3},{2... | collective-permute-start | bytes 61448 | tf_op jit(solution)/shard_map/ppermute | solution.py:274
  25.2 8.1 %collective-permute-done.one_ref = s16[80,128]{1,0:T(8,128)(2,1)S(1)} collective-permute-done((s16[80,128]{1,0:T(8,128)(2,1)S(1)}, s16[80,128]{1,0:T(8,128)(2,1)S(1)}, u32[]{:S(2)}, u32[]{:S(2)}) %collective-permute-start) | collective-permute-done | bytes 20512 | tf_op jit(solution)/shard_map/ppermute | solution.py:274
  34.1 3.5 %all-to-all-start.1 = ((s16[16,80,128]{2,1,0:T(8,128)(2,1)}), s16[16,80,128]{2,1,0:T(8,128)(2,1)S(1)}, u32[]{:S(2)}, u32[]{:S(2)}) async-start(s16[16,80,128]{2,1,0:T(8,128)(2,1)} %copies.2), calls=%async_computation.1 | async-start | bytes 655360 | tf_op jit(solution)/shard_map/all_to_all | solution.py:280
  37.7 2.2 %forward.2 = (f32[16,64,128]{2,1,0:T(8,128)S(1)}, f32[16,64,128]{2,1,0:T(8,128)S(1)}) custom-call(s32[2,64]{1,0:T(2,128)S(1)} %bitcast.17, s32[1,1]{1,0:T(1,128)S(6)} %copy.8.count_ref, s32[16,32]{1,0:T(8,128)S(1)} %copy-done.4, s16[16,80,128]{2,1,0:T(8,128)(2,1)S(1)} %all-to-all-done.after_ref.got_ref, bf16[64,128,128]{2,1,0:T(8,128)(2,1)S(1)} %bitcast.9), custom_call_target="tpu_custom_call" | custom-call | tf_op jit(solution)/shard_map/forward/pallas_call | solution.py:239
  39.9 1.9 %collective-permute-start.2 = (f32[16,64,128]{2,1,0:T(8,128)S(1)}, f32[16,64,128]{2,1,0:T(8,128)S(1)}, u32[]{:S(2)}, u32[]{:S(2)}) collective-permute-start(f32[16,64,128]{2,1,0:T(8,128)S(1)} %get-tuple-element.16), channel_id=1, source_target_pairs={{0,1},{1,0},{2,3},{3,2},{4,5},{5,4},{6,7},{7,6},{8,9},{9,8},{10,11... | collective-permute-start | bytes 1572872 | tf_op jit(solution)/shard_map/ppermute | solution.py:304
  41.9 1.9 %collective-permute-done.2.got_ref = f32[16,64,128]{2,1,0:T(8,128)S(1)} collective-permute-done((f32[16,64,128]{2,1,0:T(8,128)S(1)}, f32[16,64,128]{2,1,0:T(8,128)S(1)}, u32[]{:S(2)}, u32[]{:S(2)}) %collective-permute-start.2) | collective-permute-done | bytes 524320 | tf_op jit(solution)/shard_map/ppermute | solution.py:304
  44.8 7.0 %all-to-all-done.1.own_ref = s16[16,80,128]{2,1,0:T(8,128)(2,1)S(1)} async-done(((s16[16,80,128]{2,1,0:T(8,128)(2,1)}), s16[16,80,128]{2,1,0:T(8,128)(2,1)S(1)}, u32[]{:S(2)}, u32[]{:S(2)}) %all-to-all-start.1) | async-done | bytes 327712 | tf_op jit(solution)/shard_map/all_to_all | solution.py:280
  51.9 3.5 %all-to-all-start.3 = ((s16[16,80,128]{2,1,0:T(8,128)(2,1)}), s16[16,80,128]{2,1,0:T(8,128)(2,1)S(1)}, u32[]{:S(2)}, u32[]{:S(2)}) async-start(s16[16,80,128]{2,1,0:T(8,128)(2,1)} %join.2), calls=%async_computation.3 | async-start | bytes 655360 | tf_op jit(solution)/shard_map/all_to_all | solution.py:280
  55.5 1.9 %collective-permute-start.1 = (s16[16,80,128]{2,1,0:T(8,128)(2,1)S(1)}, s16[16,80,128]{2,1,0:T(8,128)(2,1)S(1)}, u32[]{:S(2)}, u32[]{:S(2)}) collective-permute-start(s16[16,80,128]{2,1,0:T(8,128)(2,1)S(1)} %all-to-all-done.1.own_ref), channel_id=1, source_target_pairs={{0,1},{1,0},{2,3},{3,2},{4,5},{5,4},{6,7},{7,6},{8,9},{9,8},{10,11... | collective-permute-start | bytes 983048 | tf_op jit(solution)/shard_map/ppermute | solution.py:307
  57.4 1.6 collective-permute-done.1.other_ref
  59.0 3.5 %mirror.2 = s16[16,80,128]{2,1,0:T(8,128)(2,1)} custom-call(s32[2,64]{1,0:T(2,128)S(1)} %bitcast.18, s32[1,1]{1,0:T(1,128)S(6)} %copy.8.count_ref, s32[16,32]{1,0:T(8,128)S(1)} %copy-done.4, s16[16,80,128]{2,1,0:T(8,128)(2,1)S(1)} %all-to-all-done.1.own_ref, s16[16,80,128]{2,1,0:T(8,128)(2,1)S(1)} %collective-permute-done.1.other_ref, ...), custom_call_target="tpu_custom_call" | custom-call | tf_op jit(solution)/shard_map/mirror/pallas_call | solution.py:239
  62.5 6.7 %all-to-all-done.3.got_ref = s16[16,80,128]{2,1,0:T(8,128)(2,1)S(1)} async-done(((s16[16,80,128]{2,1,0:T(8,128)(2,1)}), s16[16,80,128]{2,1,0:T(8,128)(2,1)S(1)}, u32[]{:S(2)}, u32[]{:S(2)}) %all-to-all-start.3) | async-done | bytes 327712 | tf_op jit(solution)/shard_map/all_to_all | solution.py:280
  69.2 7.6 %all-to-all-start.2 = ((s16[16,80,128]{2,1,0:T(8,128)(2,1)}), s16[16,80,128]{2,1,0:T(8,128)(2,1)S(1)}, u32[]{:S(2)}, u32[]{:S(2)}) async-start(s16[16,80,128]{2,1,0:T(8,128)(2,1)} %mirror.2), calls=%async_computation.2 | async-start | bytes 655360 | tf_op jit(solution)/shard_map/all_to_all | solution.py:277
  77.0 4.3 %collective-permute-start.3 = (f32[64,128]{1,0:T(8,128)S(1)}, f32[64,128]{1,0:T(8,128)S(1)}, u32[]{:S(2)}, u32[]{:S(2)}) collective-permute-start(f32[64,128]{1,0:T(8,128)S(1)} %sum.2), channel_id=1, source_target_pairs={{28,0},{12,32},{31,64},{4,96},{7,128},{26,160},{25,192},{3,224},{0... | collective-permute-start | bytes 98312 | tf_op jit(solution)/shard_map/ppermute | solution.py:274
  81.4 7.8 %collective-permute-done.3.row_ref = f32[64,128]{1,0:T(8,128)S(1)} collective-permute-done((f32[64,128]{1,0:T(8,128)S(1)}, f32[64,128]{1,0:T(8,128)S(1)}, u32[]{:S(2)}, u32[]{:S(2)}) %collective-permute-start.3) | collective-permute-done | bytes 32800 | tf_op jit(solution)/shard_map/ppermute | solution.py:274
  90.6 6.6 %all-to-all-start.6 = ((s16[16,80,128]{2,1,0:T(8,128)(2,1)}), s16[16,80,128]{2,1,0:T(8,128)(2,1)S(1)}, u32[]{:S(2)}, u32[]{:S(2)}) async-start(s16[16,80,128]{2,1,0:T(8,128)(2,1)} %get-tuple-element.18), calls=%async_computation.6 | async-start | bytes 655360 | tf_op jit(solution)/shard_map/all_to_all | solution.py:277
  97.2 1.9 %collective-permute-start.4 = (s16[80,128]{1,0:T(8,128)(2,1)S(1)}, s16[80,128]{1,0:T(8,128)(2,1)S(1)}, u32[]{:S(2)}, u32[]{:S(2)}) collective-permute-start(s16[80,128]{1,0:T(8,128)(2,1)S(1)} %get-tuple-element.17), channel_id=1, source_target_pairs={{0,28},{32,12},{64,31},{96,4},{128,7},{160,26},{192,25},{224,3},{2... | collective-permute-start | bytes 61448 | tf_op jit(solution)/shard_map/ppermute | solution.py:274
  99.1 10.1 %collective-permute-done.4.after_ref.one_ref = s16[80,128]{1,0:T(8,128)(2,1)S(1)} collective-permute-done((s16[80,128]{1,0:T(8,128)(2,1)S(1)}, s16[80,128]{1,0:T(8,128)(2,1)S(1)}, u32[]{:S(2)}, u32[]{:S(2)}) %collective-permute-start.4) | collective-permute-done | bytes 20512 | tf_op jit(solution)/shard_map/ppermute | solution.py:274
  109.9 3.5 %all-to-all-start.4 = ((s16[16,80,128]{2,1,0:T(8,128)(2,1)}), s16[16,80,128]{2,1,0:T(8,128)(2,1)S(1)}, u32[]{:S(2)}, u32[]{:S(2)}) async-start(s16[16,80,128]{2,1,0:T(8,128)(2,1)} %copies.3), calls=%async_computation.4 | async-start | bytes 655360 | tf_op jit(solution)/shard_map/all_to_all | solution.py:280
  113.5 2.2 %forward.3 = (f32[16,64,128]{2,1,0:T(8,128)S(1)}, f32[16,64,128]{2,1,0:T(8,128)S(1)}) custom-call(s32[2,64]{1,0:T(2,128)S(1)} %bitcast.19, s32[1,1]{1,0:T(1,128)S(6)} %copy.8.count_ref, s32[16,32]{1,0:T(8,128)S(1)} %copy-done.4, s16[16,80,128]{2,1,0:T(8,128)(2,1)S(1)} %all-to-all-done.6.got_ref, bf16[64,128,128]{2,1,0:T(8,128)(2,1)S(1)} %bitcast.11), custom_call_target="tpu_custom_call" | custom-call | tf_op jit(solution)/shard_map/forward/pallas_call | solution.py:239
  115.7 1.9 %collective-permute-start.6 = (f32[16,64,128]{2,1,0:T(8,128)S(1)}, f32[16,64,128]{2,1,0:T(8,128)S(1)}, u32[]{:S(2)}, u32[]{:S(2)}) collective-permute-start(f32[16,64,128]{2,1,0:T(8,128)S(1)} %get-tuple-element.20), channel_id=1, source_target_pairs={{0,1},{1,0},{2,3},{3,2},{4,5},{5,4},{6,7},{7,6},{8,9},{9,8},{10,11... | collective-permute-start | bytes 1572872 | tf_op jit(solution)/shard_map/ppermute | solution.py:304
  117.6 1.9 %collective-permute-done.6.got_ref = f32[16,64,128]{2,1,0:T(8,128)S(1)} collective-permute-done((f32[16,64,128]{2,1,0:T(8,128)S(1)}, f32[16,64,128]{2,1,0:T(8,128)S(1)}, u32[]{:S(2)}, u32[]{:S(2)}) %collective-permute-start.6) | collective-permute-done | bytes 524320 | tf_op jit(solution)/shard_map/ppermute | solution.py:304
  120.6 5.4 %all-to-all-done.4.own_ref = s16[16,80,128]{2,1,0:T(8,128)(2,1)S(1)} async-done(((s16[16,80,128]{2,1,0:T(8,128)(2,1)}), s16[16,80,128]{2,1,0:T(8,128)(2,1)S(1)}, u32[]{:S(2)}, u32[]{:S(2)}) %all-to-all-start.4) | async-done | bytes 327712 | tf_op jit(solution)/shard_map/all_to_all | solution.py:280
  126.0 4.2 %all-to-all-start.7 = ((s16[16,80,128]{2,1,0:T(8,128)(2,1)}), s16[16,80,128]{2,1,0:T(8,128)(2,1)S(1)}, u32[]{:S(2)}, u32[]{:S(2)}) async-start(s16[16,80,128]{2,1,0:T(8,128)(2,1)} %join.3), calls=%async_computation.7 | async-start | bytes 655360 | tf_op jit(solution)/shard_map/all_to_all | solution.py:280
  130.2 1.9 %collective-permute-start.5 = (s16[16,80,128]{2,1,0:T(8,128)(2,1)S(1)}, s16[16,80,128]{2,1,0:T(8,128)(2,1)S(1)}, u32[]{:S(2)}, u32[]{:S(2)}) collective-permute-start(s16[16,80,128]{2,1,0:T(8,128)(2,1)S(1)} %all-to-all-done.4.own_ref), channel_id=1, source_target_pairs={{0,1},{1,0},{2,3},{3,2},{4,5},{5,4},{6,7},{7,6},{8,9},{9,8},{10,11... | collective-permute-start | bytes 983048 | tf_op jit(solution)/shard_map/ppermute | solution.py:307
  133.7 3.5 %mirror.3 = s16[16,80,128]{2,1,0:T(8,128)(2,1)} custom-call(s32[2,64]{1,0:T(2,128)S(1)} %bitcast.20, s32[1,1]{1,0:T(1,128)S(6)} %copy.8.count_ref, s32[16,32]{1,0:T(8,128)S(1)} %copy-done.4, s16[16,80,128]{2,1,0:T(8,128)(2,1)S(1)} %all-to-all-done.4.own_ref, s16[16,80,128]{2,1,0:T(8,128)(2,1)S(1)} %collective-permute-done.5.other_ref, ...), custom_call_target="tpu_custom_call" | custom-call | tf_op jit(solution)/shard_map/mirror/pallas_call | solution.py:239
  137.2 7.1 %all-to-all-done.7.got_ref = s16[16,80,128]{2,1,0:T(8,128)(2,1)S(1)} async-done(((s16[16,80,128]{2,1,0:T(8,128)(2,1)}), s16[16,80,128]{2,1,0:T(8,128)(2,1)S(1)}, u32[]{:S(2)}, u32[]{:S(2)}) %all-to-all-start.7) | async-done | bytes 327712 | tf_op jit(solution)/shard_map/all_to_all | solution.py:280
  144.3 8.4 %all-to-all-start.5 = ((s16[16,80,128]{2,1,0:T(8,128)(2,1)}), s16[16,80,128]{2,1,0:T(8,128)(2,1)S(1)}, u32[]{:S(2)}, u32[]{:S(2)}) async-start(s16[16,80,128]{2,1,0:T(8,128)(2,1)} %mirror.3), calls=%async_computation.5 | async-start | bytes 655360 | tf_op jit(solution)/shard_map/all_to_all | solution.py:277
  152.9 4.0 %collective-permute-start.7 = (f32[64,128]{1,0:T(8,128)S(1)}, f32[64,128]{1,0:T(8,128)S(1)}, u32[]{:S(2)}, u32[]{:S(2)}) collective-permute-start(f32[64,128]{1,0:T(8,128)S(1)} %sum.3), channel_id=1, source_target_pairs={{28,0},{12,32},{31,64},{4,96},{7,128},{26,160},{25,192},{3,224},{0... | collective-permute-start | bytes 98312 | tf_op jit(solution)/shard_map/ppermute | solution.py:274
  156.8 5.1 %all-to-all-done.5.got_ref = s16[16,80,128]{2,1,0:T(8,128)(2,1)S(1)} async-done(((s16[16,80,128]{2,1,0:T(8,128)(2,1)}), s16[16,80,128]{2,1,0:T(8,128)(2,1)S(1)}, u32[]{:S(2)}, u32[]{:S(2)}) %all-to-all-start.5) | async-done | bytes 327712 | tf_op jit(solution)/shard_map/all_to_all | solution.py:277
  161.9 3.1 %collective-permute-done.7.row_ref = f32[64,128]{1,0:T(8,128)S(1)} collective-permute-done((f32[64,128]{1,0:T(8,128)S(1)}, f32[64,128]{1,0:T(8,128)S(1)}, u32[]{:S(2)}, u32[]{:S(2)}) %collective-permute-start.7) | collective-permute-done | bytes 32800 | tf_op jit(solution)/shard_map/ppermute | solution.py:274
  (35 shorter events, 12.0 us)
Async XLA Ops:
  0.0 37.7 %copy-start.6 = (s32[1,1,2,64]{3,2,1,0:T(2,128)S(1)}, s32[1,1,2,64]{3,2,1,0:T(2,128)}, u32[]{:S(2)}) copy-start(s32[1,1,2,64]{3,2,1,0:T(2,128)} %param.11) | copy-start | bytes 1540
  0.7 1.6 copy-start
  2.3 0.8 copy-start.2
  3.0 0.7 copy-start.5
  3.7 34.0 %copy-start.1 = (bf16[1,1,64,128,128]{4,3,2,1,0:T(8,128)(2,1)S(1)}, bf16[1,1,64,128,128]{4,3,2,1,0:T(8,128)(2,1)}, u32[]{:S(2)}) copy-start(bf16[1,1,64,128,128]{4,3,2,1,0:T(8,128)(2,1)} %param.10) | copy-start | bytes 6291460
  3.7 34.0 %copy-start.4 = (s32[16,32]{1,0:T(8,128)S(1)}, s32[16,32]{1,0:T(8,128)}, u32[]{:S(2)}) copy-start(s32[16,32]{1,0:T(8,128)} %constant.2.clone.held_ref) | copy-start | bytes 6148
  4.8 28.6 %all-to-all-start = ((s16[16,80,128]{2,1,0:T(8,128)(2,1)}), s16[16,80,128]{2,1,0:T(8,128)(2,1)S(1)}, u32[]{:S(2)}, u32[]{:S(2)}) async-start(s16[16,80,128]{2,1,0:T(8,128)(2,1)} %get-tuple-element.13), calls=%async_computation | async-start | bytes 655360 | tf_op jit(solution)/shard_map/all_to_all | solution.py:277
  13.5 19.9 %collective-permute-start = (s16[80,128]{1,0:T(8,128)(2,1)S(1)}, s16[80,128]{1,0:T(8,128)(2,1)S(1)}, u32[]{:S(2)}, u32[]{:S(2)}) collective-permute-start(s16[80,128]{1,0:T(8,128)(2,1)S(1)} %get-tuple-element.14), channel_id=1, source_target_pairs={{0,28},{32,12},{64,31},{96,4},{128,7},{160,26},{192,25},{224,3},{2... | collective-permute-start | bytes 61448 | tf_op jit(solution)/shard_map/ppermute | solution.py:274
  34.1 17.8 %all-to-all-start.1 = ((s16[16,80,128]{2,1,0:T(8,128)(2,1)}), s16[16,80,128]{2,1,0:T(8,128)(2,1)S(1)}, u32[]{:S(2)}, u32[]{:S(2)}) async-start(s16[16,80,128]{2,1,0:T(8,128)(2,1)} %copies.2), calls=%async_computation.1 | async-start | bytes 655360 | tf_op jit(solution)/shard_map/all_to_all | solution.py:280
  39.9 3.8 %collective-permute-start.2 = (f32[16,64,128]{2,1,0:T(8,128)S(1)}, f32[16,64,128]{2,1,0:T(8,128)S(1)}, u32[]{:S(2)}, u32[]{:S(2)}) collective-permute-start(f32[16,64,128]{2,1,0:T(8,128)S(1)} %get-tuple-element.16), channel_id=1, source_target_pairs={{0,1},{1,0},{2,3},{3,2},{4,5},{5,4},{6,7},{7,6},{8,9},{9,8},{10,11... | collective-permute-start | bytes 1572872 | tf_op jit(solution)/shard_map/ppermute | solution.py:304
  44.8 32.0 %copy-start.7 = (s32[1,64]{1,0:T(1,128)S(1)}, s32[1,64]{1,0:T(1,128)}, u32[]{:S(2)}) copy-start(s32[1,64]{1,0:T(1,128)} %param.8) | copy-start | bytes 772
  51.9 17.3 %all-to-all-start.3 = ((s16[16,80,128]{2,1,0:T(8,128)(2,1)}), s16[16,80,128]{2,1,0:T(8,128)(2,1)S(1)}, u32[]{:S(2)}, u32[]{:S(2)}) async-start(s16[16,80,128]{2,1,0:T(8,128)(2,1)} %join.2), calls=%async_computation.3 | async-start | bytes 655360 | tf_op jit(solution)/shard_map/all_to_all | solution.py:280
  55.4 25.9 %copy-start.8 = (s32[1,64]{1,0:T(1,128)S(1)}, s32[1,64]{1,0:T(1,128)}, u32[]{:S(2)}) copy-start(s32[1,64]{1,0:T(1,128)} %param.9) | copy-start | bytes 772
  55.5 33.9 %copy-start.3 = (f32[1,64,128]{2,1,0:T(8,128)S(1)}, f32[1,64,128]{2,1,0:T(8,128)}, u32[]{:S(2)}) copy-start(f32[1,64,128]{2,1,0:T(8,128)} %param.7) | copy-start | bytes 98308
  55.5 3.5 %collective-permute-start.1 = (s16[16,80,128]{2,1,0:T(8,128)(2,1)S(1)}, s16[16,80,128]{2,1,0:T(8,128)(2,1)S(1)}, u32[]{:S(2)}, u32[]{:S(2)}) collective-permute-start(s16[16,80,128]{2,1,0:T(8,128)(2,1)S(1)} %all-to-all-done.1.own_ref), channel_id=1, source_target_pairs={{0,1},{1,0},{2,3},{3,2},{4,5},{5,4},{6,7},{7,6},{8,9},{9,8},{10,11... | collective-permute-start | bytes 983048 | tf_op jit(solution)/shard_map/ppermute | solution.py:307
  69.2 20.0 %all-to-all-start.2 = ((s16[16,80,128]{2,1,0:T(8,128)(2,1)}), s16[16,80,128]{2,1,0:T(8,128)(2,1)S(1)}, u32[]{:S(2)}, u32[]{:S(2)}) async-start(s16[16,80,128]{2,1,0:T(8,128)(2,1)} %mirror.2), calls=%async_computation.2 | async-start | bytes 655360 | tf_op jit(solution)/shard_map/all_to_all | solution.py:277
  77.0 12.1 %collective-permute-start.3 = (f32[64,128]{1,0:T(8,128)S(1)}, f32[64,128]{1,0:T(8,128)S(1)}, u32[]{:S(2)}, u32[]{:S(2)}) collective-permute-start(f32[64,128]{1,0:T(8,128)S(1)} %sum.2), channel_id=1, source_target_pairs={{28,0},{12,32},{31,64},{4,96},{7,128},{26,160},{25,192},{3,224},{0... | collective-permute-start | bytes 98312 | tf_op jit(solution)/shard_map/ppermute | solution.py:274
  90.6 19.4 %all-to-all-start.6 = ((s16[16,80,128]{2,1,0:T(8,128)(2,1)}), s16[16,80,128]{2,1,0:T(8,128)(2,1)S(1)}, u32[]{:S(2)}, u32[]{:S(2)}) async-start(s16[16,80,128]{2,1,0:T(8,128)(2,1)} %get-tuple-element.18), calls=%async_computation.6 | async-start | bytes 655360 | tf_op jit(solution)/shard_map/all_to_all | solution.py:277
  97.2 12.0 %collective-permute-start.4 = (s16[80,128]{1,0:T(8,128)(2,1)S(1)}, s16[80,128]{1,0:T(8,128)(2,1)S(1)}, u32[]{:S(2)}, u32[]{:S(2)}) collective-permute-start(s16[80,128]{1,0:T(8,128)(2,1)S(1)} %get-tuple-element.17), channel_id=1, source_target_pairs={{0,28},{32,12},{64,31},{96,4},{128,7},{160,26},{192,25},{224,3},{2... | collective-permute-start | bytes 61448 | tf_op jit(solution)/shard_map/ppermute | solution.py:274
  109.9 16.1 %all-to-all-start.4 = ((s16[16,80,128]{2,1,0:T(8,128)(2,1)}), s16[16,80,128]{2,1,0:T(8,128)(2,1)S(1)}, u32[]{:S(2)}, u32[]{:S(2)}) async-start(s16[16,80,128]{2,1,0:T(8,128)(2,1)} %copies.3), calls=%async_computation.4 | async-start | bytes 655360 | tf_op jit(solution)/shard_map/all_to_all | solution.py:280
  115.7 3.8 %collective-permute-start.6 = (f32[16,64,128]{2,1,0:T(8,128)S(1)}, f32[16,64,128]{2,1,0:T(8,128)S(1)}, u32[]{:S(2)}, u32[]{:S(2)}) collective-permute-start(f32[16,64,128]{2,1,0:T(8,128)S(1)} %get-tuple-element.20), channel_id=1, source_target_pairs={{0,1},{1,0},{2,3},{3,2},{4,5},{5,4},{6,7},{7,6},{8,9},{9,8},{10,11... | collective-permute-start | bytes 1572872 | tf_op jit(solution)/shard_map/ppermute | solution.py:304
  126.0 18.3 %all-to-all-start.7 = ((s16[16,80,128]{2,1,0:T(8,128)(2,1)}), s16[16,80,128]{2,1,0:T(8,128)(2,1)S(1)}, u32[]{:S(2)}, u32[]{:S(2)}) async-start(s16[16,80,128]{2,1,0:T(8,128)(2,1)} %join.3), calls=%async_computation.7 | async-start | bytes 655360 | tf_op jit(solution)/shard_map/all_to_all | solution.py:280
  130.2 3.5 %collective-permute-start.5 = (s16[16,80,128]{2,1,0:T(8,128)(2,1)S(1)}, s16[16,80,128]{2,1,0:T(8,128)(2,1)S(1)}, u32[]{:S(2)}, u32[]{:S(2)}) collective-permute-start(s16[16,80,128]{2,1,0:T(8,128)(2,1)S(1)} %all-to-all-done.4.own_ref), channel_id=1, source_target_pairs={{0,1},{1,0},{2,3},{3,2},{4,5},{5,4},{6,7},{7,6},{8,9},{9,8},{10,11... | collective-permute-start | bytes 983048 | tf_op jit(solution)/shard_map/ppermute | solution.py:307
  144.3 17.6 %all-to-all-start.5 = ((s16[16,80,128]{2,1,0:T(8,128)(2,1)}), s16[16,80,128]{2,1,0:T(8,128)(2,1)S(1)}, u32[]{:S(2)}, u32[]{:S(2)}) async-start(s16[16,80,128]{2,1,0:T(8,128)(2,1)} %mirror.3), calls=%async_computation.5 | async-start | bytes 655360 | tf_op jit(solution)/shard_map/all_to_all | solution.py:277
  152.9 12.1 %collective-permute-start.7 = (f32[64,128]{1,0:T(8,128)S(1)}, f32[64,128]{1,0:T(8,128)S(1)}, u32[]{:S(2)}, u32[]{:S(2)}) collective-permute-start(f32[64,128]{1,0:T(8,128)S(1)} %sum.3), channel_id=1, source_target_pairs={{28,0},{12,32},{31,64},{4,96},{7,128},{26,160},{25,192},{3,224},{0... | collective-permute-start | bytes 98312 | tf_op jit(solution)/shard_map/ppermute | solution.py:274
